TPU v7x, 512 devices: a whole 4x8x8 slice. The times are simulated.
512 devices in a mesh: seq: 64 (over y, z_lo, core), head: 8 (over z_hi, x).
Axes of the slice: x: 4, y: 8, z: 8 (z_hi: 2, z_lo: 4; z = z_hi * 4 + z_lo), core: 2. Of those that a mesh axis runs over, the one named last changes fastest.
Arguments:
- frames: bfloat16 [8192, 1024], P('seq', 'head'), may hold values from -11 to 11
- weights: bfloat16 [3, 512, 1024], P(None, 'head')
- offset_table: bfloat16 [4096, 512], P('seq', 'head'), may hold values from -6 to 6
- clip_range: int32 [8], P('head'), may hold values from 1024 to 2047, as said below
- valid_frames: int32 [64], replicated, may hold values from 32 to 128, as said below
- context_grad: bfloat16 [8192, 512], P('seq', 'head'), may hold values from -192 to 192
Outputs:
- input_grad: bfloat16 [8192, 1024], P('seq', 'head')
- table_grad: float32 [4096, 512], P('seq', 'head')
Inputs may be any that keep to these rules, and one draw needn't show every extreme that they name: `clip_range`: each head's clip lies inside the table's offsets; some head has the largest clip. `valid_frames`: frames of a block at or past its entry are padding and are never attended to; some block is full and some holds the fewest.
All inputs are finite; a program needn't handle non-finite values.
Results may differ from a plain program's by a relative error of at most 0.03.
Values may be sent and summed in bfloat16 or wider, within the bound.
No kernel may reach another device: no remote copies, remote signals or barrier semaphores. Data moves between devices by JAX's collectives and lax.ppermute only.
A program may use at most 64 MiB of HBM per device.

v0:
```python
import jax
import jax.numpy as jnp
from jax import lax
from jax.sharding import PartitionSpec as P

HEAD_DIM = 64
TOK_DEV = 128


def shifted(shard, axis, by):
    peers = lax.axis_size(axis)
    return lax.ppermute(shard, axis, [(i, (i + by) % peers) for i in range(peers)])


def skewed(bands, key_count):
    query_count, band_width = bands.shape
    flat = jnp.pad(bands, ((0, 0), (0, 1))).reshape(-1)
    start_at = query_count - 1
    return flat[start_at : start_at + query_count * band_width].reshape(query_count, band_width)[
        :, :key_count
    ]


def unskewed(grid_values, band_width):
    query_count, key_count = grid_values.shape
    flat = jnp.pad(grid_values, ((0, 0), (0, band_width - key_count))).reshape(-1)
    flat = jnp.pad(flat, (query_count - 1, 1))
    return flat.reshape(query_count, band_width + 1)[:, :band_width]


def attention_tile(paired, key_value, full_table, query_start, key_start, clip_reach, valid_frames):
    head_size = paired.shape[1] // 2
    query_count = paired.shape[0]
    key_count = key_value.shape[0]
    band_width = key_count + query_count - 1
    score_scale = HEAD_DIM ** (-0.5)
    middle = full_table.shape[0] // 2
    offsets = key_start - query_start - (query_count - 1) + jnp.arange(band_width, dtype=jnp.int32)
    band_rows = jnp.take(full_table, jnp.clip(offsets, -clip_reach, clip_reach) + middle, axis=0)
    queries = paired[:, :head_size]
    content = jnp.einsum(
        "ie,je->ij", queries, key_value[:, :head_size], preferred_element_type=jnp.float32
    )
    bands = jnp.einsum("ie,we->iw", queries, band_rows, preferred_element_type=jnp.float32)
    key_places = key_start + jnp.arange(key_count, dtype=jnp.int32)
    live_keys = key_places % TOK_DEV < jnp.take(valid_frames, key_places // TOK_DEV)
    scores = jnp.where(
        live_keys[None, :], score_scale * (content + skewed(bands, key_count)), -jnp.inf
    )
    slope_term = jnp.einsum(
        "ie,je->ij",
        paired[:, head_size:],
        key_value[:, head_size:],
        preferred_element_type=jnp.float32,
    )
    return (scores, slope_term, offsets, band_rows)


def tile_grads(
    paired, stats, key_value, full_table, query_start, key_start, clip_reach, valid_frames
):
    scores, slope_term, offsets, band_rows = attention_tile(
        paired, key_value, full_table, query_start, key_start, clip_reach, valid_frames
    )
    head_size = paired.shape[1] // 2
    score_scale = HEAD_DIM ** (-0.5)
    attention = jnp.exp(scores - stats[0][:, None])
    score_grads = (attention * (slope_term - stats[1][:, None])).astype(jnp.bfloat16)
    attention_low = attention.astype(jnp.bfloat16)
    queries = paired[:, :head_size]
    band_grads = unskewed(score_grads, band_rows.shape[0])
    query_grad = score_scale * (
        jnp.einsum(
            "ij,je->ie", score_grads, key_value[:, :head_size], preferred_element_type=jnp.float32
        )
        + jnp.einsum("iw,we->ie", band_grads, band_rows, preferred_element_type=jnp.float32)
    )
    key_grad = score_scale * jnp.einsum(
        "ij,ie->je", score_grads, queries, preferred_element_type=jnp.float32
    )
    value_grad = jnp.einsum(
        "ij,ie->je", attention_low, paired[:, head_size:], preferred_element_type=jnp.float32
    )
    table_part = score_scale * jnp.einsum(
        "iw,ie->we", band_grads, queries, preferred_element_type=jnp.float32
    )
    return (query_grad, jnp.concatenate([key_grad, value_grad], axis=1), table_part, offsets)


def add_band(store, tails, table_part, offsets, clip_reach, margin):
    middle = (store.shape[0] - 2 * margin) // 2
    inner = (jnp.abs(offsets) < clip_reach)[:, None]
    upper_side = (offsets >= clip_reach)[:, None]
    lower_side = (offsets <= -clip_reach)[:, None]
    tails = tails + jnp.stack(
        [
            jnp.sum(jnp.where(upper_side, table_part, 0.0), axis=0),
            jnp.sum(jnp.where(lower_side, table_part, 0.0), axis=0),
        ]
    )
    band_width = table_part.shape[0]
    start_row = jnp.clip(offsets[0] + middle + margin, 0, store.shape[0] - band_width)
    window = lax.dynamic_slice_in_dim(store, start_row, band_width, 0)
    store = lax.dynamic_update_slice_in_dim(
        store, window + jnp.where(inner, table_part, 0.0), start_row, 0
    )
    return (store, tails)


def circulate(
    fixed_part, moving_part, state, process, pass_fixed, pass_moving, cycle_size, cycle_place
):
    state, moving_part = process(state, fixed_part, moving_part, cycle_place)

    def advance(step_index, running):
        state_now, fixed_now, moving_now = running
        fixed_now = pass_fixed(fixed_now)
        moving_now = pass_moving(moving_now)
        state_now, moving_now = process(
            state_now, fixed_now, moving_now, (cycle_place - step_index) % cycle_size
        )
        return (state_now, fixed_now, moving_now)

    state, fixed_part, moving_part = lax.fori_loop(
        1, cycle_size, advance, (state, fixed_part, moving_part)
    )
    return (state, pass_moving(moving_part))


def shards(frames, weights, offset_table, clip_range, valid_frames, context_grad):
    frame_count = frames.shape[0]
    head_size = context_grad.shape[1]
    cycle_size = lax.axis_size("seq")
    cycle_place = lax.axis_index("seq")
    weight_rows = weights.reshape(3 * head_size, weights.shape[2])
    projected = jnp.einsum(
        "id,cd->ic",
        lax.all_gather(frames, "head", axis=1, tiled=True),
        weight_rows,
        preferred_element_type=jnp.float32,
    ).astype(jnp.bfloat16)
    paired = jnp.concatenate([projected[:, :head_size], context_grad], axis=1)
    key_value = projected[:, head_size:]
    full_table = lax.all_gather(offset_table, "seq", axis=0, tiled=True)
    clip_reach = clip_range[0]
    query_start = cycle_place * frame_count
    row_max = jnp.full((frame_count,), -1e30, jnp.float32)
    scores, slope_term, offsets, band_rows = attention_tile(
        paired,
        lax.all_gather(key_value, "seq", axis=0, tiled=True),
        full_table,
        query_start,
        jnp.int32(0),
        clip_reach,
        valid_frames,
    )
    new_max = jnp.maximum(row_max, jnp.max(scores, axis=1))
    exponent = jnp.exp(scores - new_max[:, None])
    denominator = jnp.sum(exponent, axis=1)
    weighted = jnp.sum(exponent * slope_term, axis=1)
    stats = jnp.stack([new_max + jnp.log(denominator), weighted / denominator])
    table_rows = full_table.shape[0]
    margin = 2 * frame_count
    store = jnp.zeros((table_rows + 2 * margin, head_size), jnp.float32)
    tails = jnp.zeros((2, head_size), jnp.float32)

    def key_step(state, moving_kv, moving_grads, block_index):
        query_sum, store_now, tails_now = state
        step_query, pair_grad, table_part, offsets = tile_grads(
            paired,
            stats,
            moving_kv,
            full_table,
            query_start,
            block_index * frame_count,
            clip_reach,
            valid_frames,
        )
        store_now, tails_now = add_band(
            store_now, tails_now, table_part, offsets, clip_reach, margin
        )
        return ((query_sum + step_query, store_now, tails_now), moving_grads + pair_grad)

    def pass_keys(moving_kv):
        return shifted(moving_kv, "seq", 1)

    def pass_key_grads(moving_grads):
        return shifted(moving_grads.astype(jnp.bfloat16), "seq", 1).astype(moving_grads.dtype)

    start_state = (jnp.zeros((frame_count, head_size), jnp.float32), store, tails)
    start_moving = jnp.zeros((frame_count, 2 * head_size), jnp.float32)
    (query_grad, store, tails), kv_grad = circulate(
        key_value,
        start_moving,
        start_state,
        key_step,
        pass_keys,
        pass_key_grads,
        cycle_size,
        cycle_place,
    )
    position = jnp.arange(table_rows, dtype=jnp.int32) - table_rows // 2
    folded = store[margin : margin + table_rows]
    folded = folded + jnp.where((position == clip_reach)[:, None], tails[0][None, :], 0.0)
    folded = folded + jnp.where((position == -clip_reach)[:, None], tails[1][None, :], 0.0)
    table_grad = lax.psum_scatter(folded, "seq", scatter_dimension=0, tiled=True)
    all_grads = jnp.concatenate([query_grad, kv_grad], axis=1).astype(jnp.bfloat16)
    input_terms = jnp.einsum(
        "ic,cd->id", all_grads, weight_rows, preferred_element_type=jnp.float32
    )
    input_grad = lax.psum_scatter(
        input_terms.astype(jnp.bfloat16), "head", scatter_dimension=1, tiled=True
    )
    return (input_grad, table_grad)


def solution(mesh):
    placed = (
        P("seq", "head"),
        P(None, "head", None),
        P("seq", "head"),
        P("head"),
        P(),
        P("seq", "head"),
    )
    return jax.shard_map(
        shards,
        mesh=mesh,
        in_specs=placed,
        out_specs=(P("seq", "head"), P("seq", "head")),
        check_vma=False,
    )
```

profile of v0, /device:TPU:2, one launch (start us, length us, event | category | flops | bytes accessed | tf_op | source)
XLA Modules:
  0.0 1484.9 jit_solution(12665207510627220042)
XLA Ops:
  7.2 43.6 %all_gather.9 = bf16[128,1024]{1,0:T(8,128)(2,1)S(1)} all-gather(bf16[128,128]{1,0:T(8,128)(2,1)} %param.12), channel_id=1, replica_groups=mesh['seq'=64,'head'=8] {'head'}, dimensions={1}, use_global_device_ids=true | all-gather | bytes 294912 | tf_op jit(solution)/shard_map/all_gather | solution.py:138
  52.7 83.7 %all_gather.10 = bf16[4096,64]{1,0:T(8,128)(2,1)S(1)} all-gather(bf16[64,64]{1,0:T(8,128)(2,1)} %param.14), channel_id=1, replica_groups=mesh['seq'=64,'head'=8] {'seq'}, dimensions={0}, use_global_device_ids=true | all-gather | bytes 532480 | tf_op jit(solution)/shard_map/all_gather | solution.py:144
  136.4 17.7 %gather_fusion.2 = bf16[8319,64]{1,0:T(8,128)(2,1)} fusion(bf16[4096,64]{1,0:T(8,128)(2,1)S(1)} %all_gather.10, s32[9216]{0:T(1024)S(1)} %pad_clamp_fusion.2), kind=kCustom, calls=%fused_computation.4 | custom fusion | bytes 2162940 | tf_op jit(solution)/shard_map/jit(_take)/gather | solution.py:39
  155.0 7.0 fusion.25
  162.3 4.5 pad.50
  166.8 4.8 reshape.252
  171.7 4.2 slice.216
  175.9 7.2 reshape.253
  192.3 4.3 compare_select_fusion.7
  196.6 36.3 %fusion.50 = pred[8192]{0:T(1024)(128)(4,1)S(1)} fusion(pred[8192]{0:T(1024)(128)(4,1)S(1)} %compare_reduce_fusion, pred[8192]{0:T(1024)(128)(4,1)S(1)} %compare_reduce_fusion.1, pred[8192]{0:T(1024)(128)(4,1)S(1)} %compare_reduce_fusion.2, pred[8192]{0:T(1024)(128)(4,1)S(1)} %compare_reduce_fusion.3, pred[8192]{0:T(1024)(128)(4,1)S(1)} %compare_reduce_fusion.4, ...), kind=kLoop, calls=%fused_computation.174 | loop fusion | flops 630784 | bytes 508132 | tf_op jit(solution)/shard_map/lt | solution.py:46
  232.9 3.4 fusion.86
  241.9 859.0 %while.24 = (s32[]{:T(128)}, f32[128,64]{0,1:T(8,128)S(1)}, f32[4608,64]{0,1:T(8,128)S(1)}, f32[2,64]{1,0:T(2,128)S(1)}, bf16[128,128]{1,0:T(8,128)(2,1)S(1)}, /...) while((s32[]{:T(128)}, f32[128,64]{0,1:T(8,128)S(1)}, ...), condition=%wide.region_8.11_spmd, body=%wide.region_5.10_spmd.sunk | while | flops 23408068 | bytes 3684885 | solution.py:124
  241.9 2.2 collective-permute-start
  365.2 2.4 collective-permute-start
  367.5 5.1 collective-permute-start.1
  382.9 7.5 collective-permute-start.1
  400.9 2.2 collective-permute-start.1
  411.4 2.3 collective-permute-start
  413.7 4.8 collective-permute-start.1
  428.8 5.3 collective-permute-start.1
  444.4 8.5 collective-permute-start.1
  461.1 2.5 collective-permute-start
  549.2 3.8 collective-permute-start.1
  587.9 4.9 collective-permute-start.1
  603.0 7.3 collective-permute-start.1
  618.5 2.3 collective-permute-start
  620.8 2.4 collective-permute-start.1
  633.6 4.7 collective-permute-start.1
  648.7 5.0 collective-permute-start.1
  664.1 8.5 collective-permute-start.1
  804.5 4.8 collective-permute-start.1
  819.7 7.3 collective-permute-start.1
  847.8 2.3 collective-permute-start
  850.0 4.5 collective-permute-start.1
  865.0 5.0 collective-permute-start.1
  880.3 8.3 collective-permute-start.1
  897.0 2.5 collective-permute-start
  986.6 3.6 collective-permute-start.1
  1025.9 4.7 collective-permute-start.1
  1041.1 7.3 collective-permute-start.1
  1056.9 2.3 collective-permute-start
  1059.2 2.4 collective-permute-start.1
  1072.2 4.6 collective-permute-start.1
  1087.5 5.0 collective-permute-start.1
  1105.0 5.1 collective-permute-done.2
  1111.2 6.0 fusion.28
  1117.2 77.5 %reduce-scatter.7.cloned.1.call-done = bf16[128,128]{1,0:T(8,128)(2,1)} async-done(((bf16[1024,128]{1,0:T(8,128)(2,1)}), bf16[128,128]{1,0:T(8,128)(2,1)}) %reduce-scatter.7.cloned.1.call-update) | async-done | bytes 32784
  1196.2 282.1 %reduce-scatter.5.cloned.1.call-done = f32[64,64]{1,0:T(8,128)} async-done(((f32[4096,64]{1,0:T(8,128)}), f32[64,64]{1,0:T(8,128)}) %reduce-scatter.5.cloned.1.call-update) | async-done | bytes 16400 | tf_op jit(solution)/shard_map/reduce_scatter | solution.py:206
  (2309 shorter events, 679.7 us)
Async XLA Ops:
  7.2 225.7 %all-gather.2.cloned.1.call-start = ((), (), s32[]{:S(2)}) async-start(), calls=%async_computation.2 | async-start | bytes 2129920 | tf_op jit(solution)/shard_map/all_gather | solution.py:150
  51.8 1143.0 %reduce-scatter.7.cloned.1.call-start = ((), (), s32[]{:S(2)}) async-start(), calls=%async_computation.4 | async-start | bytes 294912
  365.2 13.0 collective-permute-start
  367.5 13.3 collective-permute-start.1
  380.9 15.1 %collective-permute-start = (bf16[128,128]{1,0:T(8,128)(2,1)S(1)}, bf16[128,128]{1,0:T(8,128)(2,1)S(1)}, u32[]{:S(2)}, u32[]{:S(2)}) collective-permute-start(bf16[128,128]{1,0:T(8,128)(2,1)S(1)} %get-tuple-element.737), channel_id=1, source_target_pairs={{0,8},{8,16},{16,24},{24,32},{32,40},{40,48},{48,56},{56,64},{64,7... | collective-permute-start | bytes 98312 | tf_op jit(solution)/shard_map/while/body/eval_jaxpr/ppermute | solution.py:12
  382.9 15.7 %collective-permute-start.1 = (bf16[128,128]{0,1:T(8,128)(2,1)S(1)}, bf16[128,128]{0,1:T(8,128)(2,1)S(1)}, u32[]{:S(2)}, u32[]{:S(2)}) collective-permute-start(bf16[128,128]{0,1:T(8,128)(2,1)S(1)} %get-tuple-element.738), channel_id=1, source_target_pairs={{0,8},{8,16},{16,24},{24,32},{32,40},{40,48},{48,56},{56,64},{64,7... | collective-permute-start | bytes 98312 | tf_op jit(solution)/shard_map/while/body/eval_jaxpr/ppermute | solution.py:12
  411.4 12.6 collective-permute-start
  413.7 13.0 collective-permute-start.1
  426.7 12.9 collective-permute-start
  428.8 13.5 collective-permute-start.1
  442.3 16.1 %collective-permute-start = (bf16[128,128]{1,0:T(8,128)(2,1)S(1)}, bf16[128,128]{1,0:T(8,128)(2,1)S(1)}, u32[]{:S(2)}, u32[]{:S(2)}) collective-permute-start(bf16[128,128]{1,0:T(8,128)(2,1)S(1)} %get-tuple-element.737), channel_id=1, source_target_pairs={{0,8},{8,16},{16,24},{24,32},{32,40},{40,48},{48,56},{56,64},{64,7... | collective-permute-start | bytes 98312 | tf_op jit(solution)/shard_map/while/body/eval_jaxpr/ppermute | solution.py:12
  444.4 16.7 %collective-permute-start.1 = (bf16[128,128]{0,1:T(8,128)(2,1)S(1)}, bf16[128,128]{0,1:T(8,128)(2,1)S(1)}, u32[]{:S(2)}, u32[]{:S(2)}) collective-permute-start(bf16[128,128]{0,1:T(8,128)(2,1)S(1)} %get-tuple-element.738), channel_id=1, source_target_pairs={{0,8},{8,16},{16,24},{24,32},{32,40},{40,48},{48,56},{56,64},{64,7... | collective-permute-start | bytes 98312 | tf_op jit(solution)/shard_map/while/body/eval_jaxpr/ppermute | solution.py:12
  547.3 11.2 collective-permute-start
  549.2 12.0 collective-permute-start.1
  585.9 12.3 collective-permute-start
  587.9 13.1 collective-permute-start.1
  601.0 14.9 %collective-permute-start = (bf16[128,128]{1,0:T(8,128)(2,1)S(1)}, bf16[128,128]{1,0:T(8,128)(2,1)S(1)}, u32[]{:S(2)}, u32[]{:S(2)}) collective-permute-start(bf16[128,128]{1,0:T(8,128)(2,1)S(1)} %get-tuple-element.737), channel_id=1, source_target_pairs={{0,8},{8,16},{16,24},{24,32},{32,40},{40,48},{48,56},{56,64},{64,7... | collective-permute-start | bytes 98312 | tf_op jit(solution)/shard_map/while/body/eval_jaxpr/ppermute | solution.py:12
  603.0 15.5 %collective-permute-start.1 = (bf16[128,128]{0,1:T(8,128)(2,1)S(1)}, bf16[128,128]{0,1:T(8,128)(2,1)S(1)}, u32[]{:S(2)}, u32[]{:S(2)}) collective-permute-start(bf16[128,128]{0,1:T(8,128)(2,1)S(1)} %get-tuple-element.738), channel_id=1, source_target_pairs={{0,8},{8,16},{16,24},{24,32},{32,40},{40,48},{48,56},{56,64},{64,7... | collective-permute-start | bytes 98312 | tf_op jit(solution)/shard_map/while/body/eval_jaxpr/ppermute | solution.py:12
  620.8 10.6 collective-permute-start.1
  631.5 12.2 collective-permute-start
  633.6 12.9 collective-permute-start.1
  646.5 12.8 collective-permute-start
  648.7 13.2 collective-permute-start.1
  661.9 16.2 %collective-permute-start = (bf16[128,128]{1,0:T(8,128)(2,1)S(1)}, bf16[128,128]{1,0:T(8,128)(2,1)S(1)}, u32[]{:S(2)}, u32[]{:S(2)}) collective-permute-start(bf16[128,128]{1,0:T(8,128)(2,1)S(1)} %get-tuple-element.737), channel_id=1, source_target_pairs={{0,8},{8,16},{16,24},{24,32},{32,40},{40,48},{48,56},{56,64},{64,7... | collective-permute-start | bytes 98312 | tf_op jit(solution)/shard_map/while/body/eval_jaxpr/ppermute | solution.py:12
  664.1 16.7 %collective-permute-start.1 = (bf16[128,128]{0,1:T(8,128)(2,1)S(1)}, bf16[128,128]{0,1:T(8,128)(2,1)S(1)}, u32[]{:S(2)}, u32[]{:S(2)}) collective-permute-start(bf16[128,128]{0,1:T(8,128)(2,1)S(1)} %get-tuple-element.738), channel_id=1, source_target_pairs={{0,8},{8,16},{16,24},{24,32},{32,40},{40,48},{48,56},{56,64},{64,7... | collective-permute-start | bytes 98312 | tf_op jit(solution)/shard_map/while/body/eval_jaxpr/ppermute | solution.py:12
  802.6 12.3 collective-permute-start
  804.5 13.0 collective-permute-start.1
  817.5 15.0 %collective-permute-start = (bf16[128,128]{1,0:T(8,128)(2,1)S(1)}, bf16[128,128]{1,0:T(8,128)(2,1)S(1)}, u32[]{:S(2)}, u32[]{:S(2)}) collective-permute-start(bf16[128,128]{1,0:T(8,128)(2,1)S(1)} %get-tuple-element.737), channel_id=1, source_target_pairs={{0,8},{8,16},{16,24},{24,32},{32,40},{40,48},{48,56},{56,64},{64,7... | collective-permute-start | bytes 98312 | tf_op jit(solution)/shard_map/while/body/eval_jaxpr/ppermute | solution.py:12
  819.7 15.5 %collective-permute-start.1 = (bf16[128,128]{0,1:T(8,128)(2,1)S(1)}, bf16[128,128]{0,1:T(8,128)(2,1)S(1)}, u32[]{:S(2)}, u32[]{:S(2)}) collective-permute-start(bf16[128,128]{0,1:T(8,128)(2,1)S(1)} %get-tuple-element.738), channel_id=1, source_target_pairs={{0,8},{8,16},{16,24},{24,32},{32,40},{40,48},{48,56},{56,64},{64,7... | collective-permute-start | bytes 98312 | tf_op jit(solution)/shard_map/while/body/eval_jaxpr/ppermute | solution.py:12
  847.8 12.4 collective-permute-start
  850.0 12.7 collective-permute-start.1
  862.8 12.7 collective-permute-start
  865.0 13.2 collective-permute-start.1
  878.2 15.9 %collective-permute-start = (bf16[128,128]{1,0:T(8,128)(2,1)S(1)}, bf16[128,128]{1,0:T(8,128)(2,1)S(1)}, u32[]{:S(2)}, u32[]{:S(2)}) collective-permute-start(bf16[128,128]{1,0:T(8,128)(2,1)S(1)} %get-tuple-element.737), channel_id=1, source_target_pairs={{0,8},{8,16},{16,24},{24,32},{32,40},{40,48},{48,56},{56,64},{64,7... | collective-permute-start | bytes 98312 | tf_op jit(solution)/shard_map/while/body/eval_jaxpr/ppermute | solution.py:12
  880.3 16.6 %collective-permute-start.1 = (bf16[128,128]{0,1:T(8,128)(2,1)S(1)}, bf16[128,128]{0,1:T(8,128)(2,1)S(1)}, u32[]{:S(2)}, u32[]{:S(2)}) collective-permute-start(bf16[128,128]{0,1:T(8,128)(2,1)S(1)} %get-tuple-element.738), channel_id=1, source_target_pairs={{0,8},{8,16},{16,24},{24,32},{32,40},{40,48},{48,56},{56,64},{64,7... | collective-permute-start | bytes 98312 | tf_op jit(solution)/shard_map/while/body/eval_jaxpr/ppermute | solution.py:12
  949.1 10.5 collective-permute-start.1
  984.6 11.2 collective-permute-start
  986.6 12.1 collective-permute-start.1
  1023.9 12.3 collective-permute-start
  1025.9 13.2 collective-permute-start.1
  1039.1 14.9 %collective-permute-start = (bf16[128,128]{1,0:T(8,128)(2,1)S(1)}, bf16[128,128]{1,0:T(8,128)(2,1)S(1)}, u32[]{:S(2)}, u32[]{:S(2)}) collective-permute-start(bf16[128,128]{1,0:T(8,128)(2,1)S(1)} %get-tuple-element.737), channel_id=1, source_target_pairs={{0,8},{8,16},{16,24},{24,32},{32,40},{40,48},{48,56},{56,64},{64,7... | collective-permute-start | bytes 98312 | tf_op jit(solution)/shard_map/while/body/eval_jaxpr/ppermute | solution.py:12
  1041.1 15.7 %collective-permute-start.1 = (bf16[128,128]{0,1:T(8,128)(2,1)S(1)}, bf16[128,128]{0,1:T(8,128)(2,1)S(1)}, u32[]{:S(2)}, u32[]{:S(2)}) collective-permute-start(bf16[128,128]{0,1:T(8,128)(2,1)S(1)} %get-tuple-element.738), channel_id=1, source_target_pairs={{0,8},{8,16},{16,24},{24,32},{32,40},{40,48},{48,56},{56,64},{64,7... | collective-permute-start | bytes 98312 | tf_op jit(solution)/shard_map/while/body/eval_jaxpr/ppermute | solution.py:12
  1059.2 10.8 collective-permute-start.1
  1070.0 12.3 collective-permute-start
  1072.2 13.0 collective-permute-start.1
  1085.2 12.8 collective-permute-start
  1087.5 13.4 collective-permute-start.1
  1111.2 367.2 %reduce-scatter.5.cloned.1.call-start = ((), (), s32[]{:S(2)}) async-start(), calls=%async_computation.3 | async-start | bytes 2129920 | tf_op jit(solution)/shard_map/reduce_scatter | solution.py:206
  (90 other events, 1045.4 us)
Sparse Core Ops, SparseCore 0:
  51.9 117.6 all-gather.1
  1111.3 83.4 reduce-scatter.6
  1198.4 279.9 reduce-scatter.4
where the time goes:
time: 1490 us; the launch traced here: 1480 us
  waiting for transfers between devices  367 us (25%)
  starting transfers between devices  336 us (23%)
  local copies, waits for them, and re-layouts  323 us (22%)
  other arithmetic  138 us (9%)
  blocking collectives  127 us (9%)
  matrix products  122 us (8%)
  loops' own time  56.6 us (4%)
  between operations  15.3 us (1%)
    ppermute x127, starting transfers between devices, shifted(): lax.ppermute(shard, axis, [(i, (i + by) % peers) for i in range(peers)])  336 us
    reduce_scatter x1, waiting for transfers between devices, shards(): lax.psum_scatter(folded, 'seq', scatter_dimension=0, tiled=True)  282 us
    all_gather x1, blocking collectives, shards(): full_table = lax.all_gather(offset_table, 'seq', axis=0, tiled=True)  83.7 us
    gather x68, local copies, waits for them, and re-layouts, attention_tile(): jnp.take(valid_frames, key_places // TOK_DEV)  81.4 us
    unnamed x4, waiting for transfers between devices  77.6 us
    gather x65, local copies, waits for them, and re-layouts, attention_tile(): jnp.take(full_table, jnp.clip(offsets, -clip_reach, clip_reach) + middle,...  72.3 us
    another operation x1, loops' own time, circulate(): lax.fori_loop(1, cycle_size, advance, (state, fixed_part, moving_part))  56.6 us
    all_gather x1, blocking collectives, shards(): lax.all_gather(frames, 'head', axis=1, tiled=True)  43.6 us
  transfers between devices with their start and end apart: 130, of which 9 were waited for; matrix products, arithmetic and copies ran while one was open for 38% of the time, Pallas kernels for 0%

commit v1 on v0

v1 whole, which is shorter than its diff:
```python
import jax
import jax.numpy as jnp
from jax import lax
from jax.experimental import pallas as pl
from jax.experimental.pallas import tpu as pltpu
from jax.sharding import Mesh
from jax.sharding import PartitionSpec as P

B = 128
G = 8
E = 64
N = B * G
TABLE = 4096
REACH = 17
PAD = 256
WIDE = TABLE + 2 * PAD
SCALE = E ** (-0.5)
STEP = 2
HIDDEN = -1e30
BF = jnp.bfloat16
F32 = jnp.float32
LIMIT = 48 * 1024 * 1024


def nt(a, b):
    return lax.dot_general(a, b, (((1,), (1,)), ((), ())), preferred_element_type=F32)


def nn(a, b):
    return lax.dot_general(a, b, (((1,), (0,)), ((), ())), preferred_element_type=F32)


def whole(shape):
    return pl.BlockSpec(shape, lambda *_: (0,) * len(shape))


def project_kernel(frames_ref, weights_ref, grad_ref, table_ref, near_ref, kv_ref):
    total = jnp.zeros((B, 3 * E), F32)
    for h in range(G):
        total = total + nt(frames_ref[h], weights_ref[:, h * B : (h + 1) * B])
    low = total.astype(BF)
    scaled = (low[:, :E].astype(F32) * SCALE).astype(BF)
    paired = jnp.concatenate([scaled, grad_ref[...]], axis=1)
    for g in range(G):
        near_ref[g, :B] = paired
        near_ref[g, B:] = table_ref[...]
    kv_ref[...] = low[:, E:]


def project(frames, weights, grad, table):
    return pl.pallas_call(
        project_kernel,
        out_shape=(
            jax.ShapeDtypeStruct((G, B + 32, B), BF),
            jax.ShapeDtypeStruct((B, B), BF),
        ),
        compiler_params=pltpu.CompilerParams(vmem_limit_bytes=LIMIT),
        name="project",
    )(frames, weights, grad, table)


def tile_start(place, u, v):
    apart = G * (v - place[0]) + place[1] - u
    return pl.multiple_of((jnp.clip(apart, -REACH, REACH) + REACH) * B, B)


def stats_kernel(place, valid, near_ref, far_ref, scores_ref, stats_ref, table_ref):
    step = pl.program_id(0)
    clip = place[2]

    @pl.when(step == 0)
    def _():
        table_ref[:, :PAD] = jnp.zeros((E, PAD), BF)
        table_ref[:, WIDE - PAD :] = jnp.zeros((E, PAD), BF)
        for y in range(G):
            for k in range(4):
                at = PAD + (4 * y + k) * B
                table_ref[:, at : at + B] = far_ref[y, B + k * E : B + (k + 1) * E, :]
        offsets = lax.broadcasted_iota(jnp.int32, (E, WIDE), 1) - (TABLE // 2 + PAD)
        rows = table_ref[...].astype(F32)
        upper = jnp.sum(jnp.where(offsets == clip, rows, 0.0), axis=1, keepdims=True)
        lower = jnp.sum(jnp.where(offsets == -clip, rows, 0.0), axis=1, keepdims=True)
        rows = jnp.where(offsets >= clip, upper, jnp.where(offsets <= -clip, lower, rows))
        table_ref[...] = rows.astype(BF)

    keys = far_ref[:, :B, :E].reshape(N, E)
    values = far_ref[:, :B, E:].reshape(N, E)
    lane = lax.broadcasted_iota(jnp.int32, (B, B), 1)
    for part in range(STEP):
        u = step * STEP + part
        queries = near_ref[u, :B, :E]
        grads = near_ref[u, :B, E:]
        content = nt(queries, keys)
        slope = nt(grads, values)
        pieces = []
        for v in range(G):
            band = nn(queries, table_ref[:, pl.ds(tile_start(place, u, v), 2 * B)])
            moved = pltpu.roll(band, B, 1, stride=1, stride_axis=0)[:, :B]
            live = lane < valid[G * v + place[1]]
            pieces.append(jnp.where(live, content[:, v * B : (v + 1) * B] + moved, HIDDEN))
        scores = jnp.concatenate(pieces, axis=1)
        scores_ref[part * B : (part + 1) * B, :] = scores
        top = jnp.max(scores, axis=1, keepdims=True)
        weight = jnp.exp(scores - top)
        amount = jnp.sum(weight, axis=1, keepdims=True)
        mean = jnp.sum(weight * slope, axis=1, keepdims=True) / amount
        both = jnp.where(lane == 0, top + jnp.log(amount), jnp.where(lane == 1, mean, 0.0))
        turned = both.T
        stats_ref[pl.ds(u, 1), :] = turned[0:1]
        stats_ref[pl.ds(G + u, 1), :] = turned[1:2]


def statistics(place, valid, near, far):
    return pl.pallas_call(
        stats_kernel,
        grid_spec=pltpu.PrefetchScalarGridSpec(
            num_scalar_prefetch=2,
            grid=(G // STEP,),
            in_specs=[whole(near.shape), whole(far.shape)],
            out_specs=[
                pl.BlockSpec((STEP * B, N), lambda i, *_: (i, 0)),
                whole((2 * G, B)),
                whole((E, WIDE)),
            ],
        ),
        out_shape=(
            jax.ShapeDtypeStruct((N, N), F32),
            jax.ShapeDtypeStruct((2 * G, B), F32),
            jax.ShapeDtypeStruct((E, WIDE), BF),
        ),
        compiler_params=pltpu.CompilerParams(vmem_limit_bytes=LIMIT),
        name="statistics",
    )(place, valid, near, far)


def grads_kernel(
    place,
    near_ref,
    far_ref,
    scores_ref,
    parts_ref,
    table_ref,
    far_out,
    near_out,
    columns,
    pair_sum,
    table_sum,
):
    step = pl.program_id(0)
    clip = place[2]

    @pl.when(step == 0)
    def _():
        parts = parts_ref[...]
        each = parts[:, :G]
        top = jnp.max(each, axis=0)
        total = top + jnp.log(jnp.sum(jnp.exp(each - top[None]), axis=0))
        mean = jnp.sum(jnp.exp(each - total[None]) * parts[:, G:], axis=0)
        rest = jnp.zeros((B - 2 * G, B), F32)
        columns[...] = jnp.concatenate([total, mean, rest], axis=0).T
        pair_sum[...] = jnp.zeros_like(pair_sum)
        table_sum[...] = jnp.zeros_like(table_sum)

    keys = far_ref[:, :B, :E].reshape(N, E)
    values = far_ref[:, :B, E:].reshape(N, E)
    row = lax.broadcasted_iota(jnp.int32, (B, B), 0)
    lane = lax.broadcasted_iota(jnp.int32, (B, B), 1)
    turn = (lane + row) % B
    early = lane + row < B
    lows, probs, turned = [], [], []
    for part in range(STEP):
        u = step * STEP + part
        paired = near_ref[u, :B, :]
        flipped = paired.astype(F32).T.astype(BF)
        turned.append(flipped)
        total = jnp.sum(jnp.where(lane == u, columns[...], 0.0), axis=1, keepdims=True)
        mean = jnp.sum(jnp.where(lane == G + u, columns[...], 0.0), axis=1, keepdims=True)
        slope = nt(paired[:, E:], values)
        prob = jnp.exp(scores_ref[part * B : (part + 1) * B, :] - total)
        low = (prob * (slope - mean)).astype(BF)
        query_grad = nn(low, keys)
        wide = low.astype(F32)
        for v in range(G):
            at = tile_start(place, u, v)
            spun = jnp.take_along_axis(wide[:, v * B : (v + 1) * B], turn, axis=1)
            band = jnp.concatenate(
                [jnp.where(early, 0.0, spun), jnp.where(early, spun, 0.0)], axis=1
            ).astype(BF)
            query_grad = query_grad + nt(band, table_ref[:, pl.ds(at, 2 * B)])
            table_sum[:, pl.ds(at, 2 * B)] += nn(flipped[:E], band)
        query_low = (query_grad * SCALE).astype(BF)
        near_out[u] = jnp.concatenate([query_low[:E], query_low[E:]], axis=1)
        lows.append(low)
        probs.append(prob.astype(BF))
    both = jnp.concatenate(turned, axis=1)
    pair_sum[:E] += nn(both[:E], jnp.concatenate(lows, axis=0))
    pair_sum[E:] += nn(both[E:], jnp.concatenate(probs, axis=0))

    @pl.when(step == pl.num_programs(0) - 1)
    def _():
        offsets = lax.broadcasted_iota(jnp.int32, (E, WIDE), 1) - (TABLE // 2 + PAD)
        terms = table_sum[...]
        upper = jnp.sum(jnp.where(offsets >= clip, terms, 0.0), axis=1, keepdims=True)
        lower = jnp.sum(jnp.where(offsets <= -clip, terms, 0.0), axis=1, keepdims=True)
        terms = jnp.where(jnp.abs(offsets) < clip, terms, 0.0)
        terms = jnp.where(offsets == clip, upper, jnp.where(offsets == -clip, lower, terms))
        folded = terms.astype(BF)
        for y in range(G):
            far_out[y, :B] = pair_sum[:, y * B : (y + 1) * B].T.astype(BF)
            for k in range(4):
                at = PAD + (4 * y + k) * B
                far_out[y, B + k * E : B + (k + 1) * E, :] = folded[:, at : at + B]


def gradients(place, near, far, scores, parts, table):
    return pl.pallas_call(
        grads_kernel,
        grid_spec=pltpu.PrefetchScalarGridSpec(
            num_scalar_prefetch=1,
            grid=(G // STEP,),
            in_specs=[
                whole(near.shape),
                whole(far.shape),
                pl.BlockSpec((STEP * B, N), lambda i, *_: (i, 0)),
                whole(parts.shape),
                whole(table.shape),
            ],
            out_specs=[whole((G, B + 4 * E, B)), whole((G, E, B))],
            scratch_shapes=[
                pltpu.VMEM((B, B), F32),
                pltpu.VMEM((B, N), F32),
                pltpu.VMEM((E, WIDE), F32),
            ],
        ),
        out_shape=(
            jax.ShapeDtypeStruct((G, B + 4 * E, B), BF),
            jax.ShapeDtypeStruct((G, E, B), BF),
        ),
        compiler_params=pltpu.CompilerParams(vmem_limit_bytes=LIMIT),
        name="gradients",
    )(place, near, far, scores, parts, table)


def fold_kernel(far_ref, near_ref, kv_ref, out_ref):
    total = jnp.sum(far_ref[...].astype(F32), axis=0)
    kv_ref[...] = total[:B].astype(BF)
    low = total[B:].astype(BF)
    for k in range(4):
        block = low[k * E : (k + 1) * E]
        top, end = block[: E // 2], block[E // 2 :]
        out_ref[2 * k, :E] = near_ref[2 * k]
        out_ref[2 * k, E:] = jnp.concatenate([top[:, :E], end[:, :E]], axis=1)
        out_ref[2 * k + 1, :E] = near_ref[2 * k + 1]
        out_ref[2 * k + 1, E:] = jnp.concatenate([top[:, E:], end[:, E:]], axis=1)


def fold(far, near):
    return pl.pallas_call(
        fold_kernel,
        out_shape=(
            jax.ShapeDtypeStruct((B, B), BF),
            jax.ShapeDtypeStruct((G, E + E // 2, B), BF),
        ),
        compiler_params=pltpu.CompilerParams(vmem_limit_bytes=LIMIT),
        name="fold",
    )(far, near)


def unproject_kernel(near_ref, kv_ref, weights_ref, out_ref, table_ref):
    total = jnp.sum(near_ref[...].astype(F32), axis=0)
    packed = total[:E].astype(BF)
    query = jnp.concatenate([packed[:, :E], packed[:, E:]], axis=0)
    terms = nn(query, weights_ref[:E]) + nn(kv_ref[...], weights_ref[E:])
    for h in range(G):
        out_ref[h] = terms[:, h * B : (h + 1) * B].astype(BF)
    table_ref[...] = total[E:]


def unproject(near, kv, weights):
    return pl.pallas_call(
        unproject_kernel,
        out_shape=(
            jax.ShapeDtypeStruct((G, B, B), BF),
            jax.ShapeDtypeStruct((E // 2, B), F32),
        ),
        compiler_params=pltpu.CompilerParams(vmem_limit_bytes=LIMIT),
        name="unproject",
    )(near, kv, weights)


def exchange(parts, axis):
    return lax.all_to_all(parts, axis, 0, 0, tiled=True)


def to_all(shard):
    return jnp.broadcast_to(shard[None], (G,) + shard.shape)


def shards(frames, weights, offset_table, clip_range, valid_frames, context_grad):
    weight_rows = weights.reshape(3 * E, G * B)
    place = jnp.stack([lax.axis_index("far"), lax.axis_index("near"), clip_range[0]])
    turned = offset_table.T
    packed = jnp.concatenate([turned[: E // 2], turned[E // 2 :]], axis=1)
    gathered = exchange(to_all(frames), "head")
    near, kv = project(gathered, weight_rows, context_grad, packed)
    near = exchange(near, "near")
    rows = near[:, B:].reshape(4, 2, E // 2, 2, E)
    rows = rows.transpose(0, 3, 2, 1, 4).reshape(4 * E, B)
    far = exchange(to_all(jnp.concatenate([kv, rows], axis=0)), "far")
    scores, stats, table = statistics(place, valid_frames, near, far)
    parts = exchange(to_all(stats), "near")
    far_grads, near_grads = gradients(place, near, far, scores, parts, table)
    kv_grad, near_grads = fold(exchange(far_grads, "far"), near_grads)
    terms, table_part = unproject(exchange(near_grads, "near"), kv_grad, weight_rows)
    table_grad = table_part.reshape(E // 2, 2, E).transpose(2, 1, 0).reshape(E, E)
    terms = exchange(terms, "head")
    input_grad = jnp.sum(terms.astype(F32), axis=0).astype(BF)
    return (input_grad, table_grad)


def solution(mesh):
    split = Mesh(mesh.devices.reshape(G, G, G), ("far", "near", "head"))
    seq = ("far", "near")
    placed = (
        P(seq, "head"),
        P(None, "head", None),
        P(seq, "head"),
        P("head"),
        P(),
        P(seq, "head"),
    )
    return jax.shard_map(
        shards,
        mesh=split,
        in_specs=placed,
        out_specs=(P(seq, "head"), P(seq, "head")),
        check_vma=False,
    )
```

time: 1490 us -> 158 us (0.11)
  the two profiles are of different devices: /device:TPU:2 before, /device:TPU:64 now
where the time goes in v1:
time: 158 us; the launch traced here: 157 us
  blocking collectives  58.2 us (37%)
  waiting for transfers between devices  47.5 us (30%)
  starting transfers between devices  22.3 us (14%)
  Pallas kernels  18.8 us (12%)
  local copies, waits for them, and re-layouts  8.23 us (5%)
    all_to_all x4, blocking collectives, exchange(): return lax.all_to_all(parts, axis, 0, 0, tiled=True)  58.2 us
    all_to_all x3, waiting for transfers between devices, exchange(): return lax.all_to_all(parts, axis, 0, 0, tiled=True)  47.5 us
    all_to_all x3, starting transfers between devices, exchange(): return lax.all_to_all(parts, axis, 0, 0, tiled=True)  22.3 us
    pallas_call x1, Pallas kernels, gradients(): pl.pallas_call(grads_kernel, grid_spec=pltpu.PrefetchScalarGridSpec(num_s...  9.1 us
    pallas_call x1, Pallas kernels, statistics(): pl.pallas_call(stats_kernel, grid_spec=pltpu.PrefetchScalarGridSpec(num_s...  8.15 us
    unnamed x11, local copies, waits for them, and re-layouts  5.29 us
  transfers between devices with their start and end apart: 3, of which 3 were waited for; matrix products, arithmetic and copies ran while one was open for 2% of the time, Pallas kernels for 0%

profile of v1, /device:TPU:64, one launch (start us, length us, event | category | flops | bytes accessed | tf_op | source)
XLA Modules:
  0.0 157.3 jit_solution(16216093651153987760)
XLA Ops:
  0.6 0.0 copy-start.3
  0.6 1.5 broadcast_in_dim.6
  2.1 11.8 %all-to-all-start = ((bf16[8,128,128]{2,1,0:T(8,128)(2,1)}), bf16[8,128,128]{2,1,0:T(8,128)(2,1)S(1)}, u32[]{:S(2)}, u32[]{:S(2)}) async-start(bf16[8,128,128]{2,1,0:T(8,128)(2,1)} %broadcast_in_dim.6), calls=%async_computation | async-start | bytes 524288 | tf_op jit(solution)/shard_map/all_to_all | solution.py:292
  14.0 0.8 copy.12
  14.8 0.8 copy.13.grad_ref
  15.6 0.1 pad_maximum_fusion.1.table_ref
  15.7 12.1 %all-to-all-done.frames_ref = bf16[8,128,128]{2,1,0:T(8,128)(2,1)S(1)} async-done(((bf16[8,128,128]{2,1,0:T(8,128)(2,1)}), bf16[8,128,128]{2,1,0:T(8,128)(2,1)S(1)}, u32[]{:S(2)}, u32[]{:S(2)}) %all-to-all-start) | async-done | bytes 262176 | tf_op jit(solution)/shard_map/all_to_all | solution.py:292
  27.8 0.0 copy-start.1
  27.8 1.0 copy-done.1
  28.8 0.5 project.1
  29.3 13.2 %all_to_all.35.near_ref = bf16[8,160,128]{2,1,0:T(8,128)(2,1)S(1)} all-to-all(bf16[8,160,128]{2,1,0:T(8,128)(2,1)S(1)} %get-tuple-element.13), channel_id=1, replica_groups=mesh['far'=8,'near'=8,'head'=8] {'near'}, dimensions={0} | all-to-all | bytes 655360 | tf_op jit(solution)/shard_map/all_to_all | solution.py:292
  42.5 0.1 reshape.23
  42.6 0.1 copy.14
  42.8 0.1 reshape.24
  42.9 1.0 broadcast_in_dim.7
  43.9 7.1 %all-to-all-start.2 = ((bf16[8,384,128]{2,1,0:T(8,128)(2,1)}), bf16[8,384,128]{2,1,0:T(8,128)(2,1)S(1)}, u32[]{:S(2)}, u32[]{:S(2)}) async-start(bf16[8,384,128]{2,1,0:T(8,128)(2,1)} %broadcast_in_dim.7), calls=%async_computation.2 | async-start | bytes 1572864 | tf_op jit(solution)/shard_map/all_to_all | solution.py:292
  51.7 0.1 pad_add_fusion.place
  51.7 22.3 %all-to-all-done.2.far_ref = bf16[8,384,128]{2,1,0:T(8,128)(2,1)S(1)} async-done(((bf16[8,384,128]{2,1,0:T(8,128)(2,1)}), bf16[8,384,128]{2,1,0:T(8,128)(2,1)S(1)}, u32[]{:S(2)}, u32[]{:S(2)}) %all-to-all-start.2) | async-done | bytes 786464 | tf_op jit(solution)/shard_map/all_to_all | solution.py:292
  74.0 0.0 copy-done.3
  74.0 8.2 %statistics.1 = (f32[1024,1024]{1,0:T(8,128)S(1)}, f32[16,128]{1,0:T(8,128)S(1)}, bf16[64,4608]{1,0:T(8,128)(2,1)S(1)}) custom-call(s32[3]{0:T(128)S(1)} %pad_add_fusion.place, s32[64]{0:T(128)S(1)} %copy-done.3, bf16[8,160,128]{2,1,0:T(8,128)(2,1)S(1)} %all_to_all.35.near_ref, bf16[8,384,128]{2,1,0:T(8,128)(2,1)S(1)} %all-to-all-done.2.far_ref), custom_call_target="tpu_custom_call" | custom-call | tf_op jit(solution)/shard_map/statistics/pallas_call | solution.py:114
  82.2 0.0 copy-start
  82.2 1.9 %copy-done = f32[1024,1024]{1,0:T(8,128)} copy-done((f32[1024,1024]{1,0:T(8,128)}, f32[1024,1024]{1,0:T(8,128)S(1)}, u32[]{:S(2)}) %copy-start) | copy-done | bytes 4194328
  84.1 8.9 %all_to_all.36.parts_ref = f32[8,16,128]{2,1,0:T(8,128)S(1)} all-to-all(f32[8,16,128]{2,1,0:T(8,128)S(1)} %broadcast_in_dim.8), channel_id=1, replica_groups=mesh['far'=8,'near'=8,'head'=8] {'near'}, dimensions={0} | all-to-all | bytes 131072 | tf_op jit(solution)/shard_map/all_to_all | solution.py:292
  93.1 0.0 copy-start.2
  93.1 9.1 %gradients.1 = (bf16[8,384,128]{2,1,0:T(8,128)(2,1)S(1)}, bf16[8,64,128]{2,1,0:T(8,128)(2,1)S(1)}) custom-call(s32[3]{0:T(128)S(1)} %pad_add_fusion.place, bf16[8,160,128]{2,1,0:T(8,128)(2,1)S(1)} %all_to_all.35.near_ref, bf16[8,384,128]{2,1,0:T(8,128)(2,1)S(1)} %all-to-all-done.2.far_ref, f32[1024,1024]{1,0:T(8,128)} %copy-done, ...), custom_call_target="tpu_custom_call" | custom-call | tf_op jit(solution)/shard_map/gradients/pallas_call | solution.py:216
  102.2 25.7 %all_to_all.37.far_ref = bf16[8,384,128]{2,1,0:T(8,128)(2,1)S(1)} all-to-all(bf16[8,384,128]{2,1,0:T(8,128)(2,1)S(1)} %get-tuple-element.18), channel_id=1, replica_groups=mesh['far'=8,'near'=8,'head'=8] {'far'}, dimensions={0} | all-to-all | bytes 1572864 | tf_op jit(solution)/shard_map/all_to_all | solution.py:292
  127.9 0.1 fold.1
  128.0 10.3 %all_to_all.38.near_ref = bf16[8,96,128]{2,1,0:T(8,128)(2,1)S(1)} all-to-all(bf16[8,96,128]{2,1,0:T(8,128)(2,1)S(1)} %get-tuple-element.20), channel_id=1, replica_groups=mesh['far'=8,'near'=8,'head'=8] {'near'}, dimensions={0} | all-to-all | bytes 393216 | tf_op jit(solution)/shard_map/all_to_all | solution.py:292
  138.3 0.0 copy-done.2
  138.3 1.0 unproject.1
  139.3 3.4 %all-to-all-start.6 = ((bf16[8,128,128]{2,1,0:T(8,128)(2,1)}), bf16[8,128,128]{2,1,0:T(8,128)(2,1)S(1)}, u32[]{:S(2)}, u32[]{:S(2)}) async-start(bf16[8,128,128]{2,1,0:T(8,128)(2,1)} %get-tuple-element.22), calls=%async_computation.6 | async-start | bytes 524288 | tf_op jit(solution)/shard_map/all_to_all | solution.py:292
  142.8 0.1 reshape.25
  142.9 0.7 copy.16
  143.6 13.1 %all-to-all-done.6 = bf16[8,128,128]{2,1,0:T(8,128)(2,1)S(1)} async-done(((bf16[8,128,128]{2,1,0:T(8,128)(2,1)}), bf16[8,128,128]{2,1,0:T(8,128)(2,1)S(1)}, u32[]{:S(2)}, u32[]{:S(2)}) %all-to-all-start.6) | async-done | bytes 262176 | tf_op jit(solution)/shard_map/all_to_all | solution.py:292
  156.6 0.7 reduce_sum.12
  (5 shorter events, 0.0 us)
Async XLA Ops:
  0.6 73.4 %copy-start.3 = (s32[64]{0:T(128)S(1)}, s32[64]{0:T(128)}, u32[]{:S(2)}) copy-start(s32[64]{0:T(128)} %valid.1) | copy-start | bytes 772
  2.1 25.7 %all-to-all-start = ((bf16[8,128,128]{2,1,0:T(8,128)(2,1)}), bf16[8,128,128]{2,1,0:T(8,128)(2,1)S(1)}, u32[]{:S(2)}, u32[]{:S(2)}) async-start(bf16[8,128,128]{2,1,0:T(8,128)(2,1)} %broadcast_in_dim.6), calls=%async_computation | async-start | bytes 524288 | tf_op jit(solution)/shard_map/all_to_all | solution.py:292
  27.8 1.0 copy-start.1
  43.9 30.1 %all-to-all-start.2 = ((bf16[8,384,128]{2,1,0:T(8,128)(2,1)}), bf16[8,384,128]{2,1,0:T(8,128)(2,1)S(1)}, u32[]{:S(2)}, u32[]{:S(2)}) async-start(bf16[8,384,128]{2,1,0:T(8,128)(2,1)} %broadcast_in_dim.7), calls=%async_computation.2 | async-start | bytes 1572864 | tf_op jit(solution)/shard_map/all_to_all | solution.py:292
  82.2 2.0 %copy-start = (f32[1024,1024]{1,0:T(8,128)}, f32[1024,1024]{1,0:T(8,128)S(1)}, u32[]{:S(2)}) copy-start(f32[1024,1024]{1,0:T(8,128)S(1)} %get-tuple-element.15.scores_ref) | copy-start | bytes 12582916
  93.1 45.3 %copy-start.2 = (bf16[3,64,1024]{2,1,0:T(8,128)(2,1)S(1)}, bf16[3,64,1024]{2,1,0:T(8,128)(2,1)}, u32[]{:S(2)}) copy-start(bf16[3,64,1024]{2,1,0:T(8,128)(2,1)} %param.7) | copy-start | bytes 1179652
  139.3 17.3 %all-to-all-start.6 = ((bf16[8,128,128]{2,1,0:T(8,128)(2,1)}), bf16[8,128,128]{2,1,0:T(8,128)(2,1)S(1)}, u32[]{:S(2)}, u32[]{:S(2)}) async-start(bf16[8,128,128]{2,1,0:T(8,128)(2,1)} %get-tuple-element.22), calls=%async_computation.6 | async-start | bytes 524288 | tf_op jit(solution)/shard_map/all_to_all | solution.py:292

commit v2 on v1

v2 whole, which is shorter than its diff:
```python
import jax
import jax.numpy as jnp
from jax import lax
from jax.experimental import pallas as pl
from jax.experimental.pallas import tpu as pltpu
from jax.sharding import Mesh
from jax.sharding import PartitionSpec as P

B = 128
G = 8
E = 64
N = B * G
TABLE = 4096
REACH = 17
PAD = 256
WIDE = TABLE + 2 * PAD
SCALE = E ** (-0.5)
SPAN = 2
STRIDES = (32, 16, 8, 4, 2)
HIDDEN = -1e30
BF = jnp.bfloat16
F32 = jnp.float32
LIMIT = 32 * 1024 * 1024


def nt(a, b):
    return lax.dot_general(a, b, (((1,), (1,)), ((), ())), preferred_element_type=F32)


def nn(a, b):
    return lax.dot_general(a, b, (((1,), (0,)), ((), ())), preferred_element_type=F32)


def project_kernel(frames_ref, weights_ref, grad_ref, near_ref, far_ref):
    total = jnp.zeros((B, 3 * E), F32)
    for h in range(G):
        total = total + nt(frames_ref[h], weights_ref[:, h * B : (h + 1) * B])
    low = total.astype(BF)
    scaled = (low[:, :E].astype(F32) * SCALE).astype(BF)
    paired = jnp.concatenate([scaled, grad_ref[...]], axis=1)
    for g in range(G):
        near_ref[g] = paired
        far_ref[g] = low[:, E:]


def project(frames, weights, grad):
    return pl.pallas_call(
        project_kernel,
        out_shape=(jax.ShapeDtypeStruct((G, B, B), BF), jax.ShapeDtypeStruct((G, B, B), BF)),
        compiler_params=pltpu.CompilerParams(vmem_limit_bytes=LIMIT),
        name="project",
    )(frames, weights, grad)


def slot_column(place, slot):
    bits = sum(((slot >> k) & 1) * (STRIDES[k] // 2) for k in range(len(STRIDES)))
    own = place[0] * (G // 2) + place[1] // 2
    return pl.multiple_of(PAD + jnp.bitwise_xor(own, bits) * B, B)


def near_tiles(place, u):
    shift = place[1] - u
    first = jnp.where(shift >= 0, -2, -1)
    return [(place[0] + first + w, G * (first + w) + shift) for w in range(4)]


def band_at(apart):
    return pl.ds(pl.multiple_of((apart + REACH) * B, B), 2 * B)


def block_at(v):
    return pl.ds(pl.multiple_of((v + SPAN) * B, B), B)


def stats_kernel(
    place, valid, near_ref, far_ref, mine_ref, theirs_ref, scores_ref, stats_ref, table_ref, shifts
):
    clip = place[2]
    table_ref[:, :PAD] = jnp.zeros((E, PAD), BF)
    table_ref[:, WIDE - PAD :] = jnp.zeros((E, PAD), BF)
    first = place[1] % 2 == 0
    for slot in range(2 ** len(STRIDES)):
        mine = mine_ref[slot].astype(F32)
        theirs = theirs_ref[slot].astype(F32)
        left = jnp.where(first, mine, theirs)
        right = jnp.where(first, theirs, mine)
        top = jnp.concatenate([left[:, :E], right[:, :E]], axis=1)
        end = jnp.concatenate([left[:, E:], right[:, E:]], axis=1)
        block = jnp.concatenate([top, end], axis=0)
        table_ref[:, pl.ds(slot_column(place, slot), B)] = block.astype(BF)
    offsets = lax.broadcasted_iota(jnp.int32, (E, WIDE), 1) - (TABLE // 2 + PAD)
    rows = table_ref[...].astype(F32)
    upper = jnp.sum(jnp.where(offsets == clip, rows, 0.0), axis=1, keepdims=True)
    lower = jnp.sum(jnp.where(offsets == -clip, rows, 0.0), axis=1, keepdims=True)
    rows = jnp.where(offsets >= clip, upper, jnp.where(offsets <= -clip, lower, rows))
    table_ref[...] = rows.astype(BF)

    keys = far_ref[:, :, :E].reshape(N, E)
    values = far_ref[:, :, E:].reshape(N, E)
    ends = jnp.concatenate([table_ref[:, :B], table_ref[:, WIDE - B :]], axis=1)
    lane = lax.broadcasted_iota(jnp.int32, (B, B), 1)
    row = lax.broadcasted_iota(jnp.int32, (B, B), 0)
    late = lane + row < B

    def put_band(u, v, apart):
        band = nn(near_ref[u, :, :E], table_ref[:, band_at(apart)])
        picked = jnp.where(late, band[:, B:], band[:, :B])
        shifts[u, :, block_at(v)] = pltpu.roll(picked, 0, 1, stride=1, stride_axis=0)

    for u in range(G):
        edges = nn(near_ref[u, :, :E], ends)
        for v in range(G):
            at = (v + SPAN) * B
            shifts[u, :, at : at + B] = jnp.where(v > place[0], edges[:, B:], edges[:, :B])
    put_band(place[1], place[0] + 2, 2 * G)
    for u in range(G):
        content = nt(near_ref[u, :, :E], keys)
        slope = nt(near_ref[u, :, E:], values)
        for v, apart in near_tiles(place, u):
            put_band(u, v, apart)
        pieces = []
        for v in range(G):
            at = (v + SPAN) * B
            both = content[:, v * B : (v + 1) * B] + shifts[u, :, at : at + B]
            pieces.append(jnp.where(lane < valid[G * v + place[1]], both, HIDDEN))
        scores = jnp.concatenate(pieces, axis=1)
        scores_ref[u * B : (u + 1) * B, :] = scores
        top = jnp.max(scores, axis=1, keepdims=True)
        weight = jnp.exp(scores - top)
        amount = jnp.sum(weight, axis=1, keepdims=True)
        mean = jnp.sum(weight * slope, axis=1, keepdims=True) / amount
        both = jnp.where(lane == 0, top + jnp.log(amount), jnp.where(lane == 1, mean, 0.0))
        turned = both.T
        stats_ref[u : u + 1, :] = turned[0:1]
        stats_ref[G + u : G + u + 1, :] = turned[1:2]


SCALARS = pl.BlockSpec(memory_space=pltpu.SMEM)
ARRAY = pl.BlockSpec(memory_space=pltpu.VMEM)


def statistics(place, valid, near, far, mine, theirs):
    return pl.pallas_call(
        stats_kernel,
        in_specs=[SCALARS] * 2 + [ARRAY] * 4,
        out_specs=[ARRAY] * 3,
        out_shape=(
            jax.ShapeDtypeStruct((N, N), F32),
            jax.ShapeDtypeStruct((2 * G, B), F32),
            jax.ShapeDtypeStruct((E, WIDE), BF),
        ),
        scratch_shapes=[pltpu.VMEM((G, B, N + 2 * SPAN * B), F32)],
        compiler_params=pltpu.CompilerParams(vmem_limit_bytes=LIMIT),
        name="statistics",
    )(place, valid, near, far, mine, theirs)


def grads_kernel(
    place,
    near_ref,
    far_ref,
    scores_ref,
    parts_ref,
    table_ref,
    far_out,
    near_out,
    keep_out,
    send_out,
    query_sum,
    table_sum,
    held,
):
    clip = place[2]
    parts = parts_ref[...]
    each = parts[:, :G]
    top = jnp.max(each, axis=0)
    total = top + jnp.log(jnp.sum(jnp.exp(each - top[None]), axis=0))
    mean = jnp.sum(jnp.exp(each - total[None]) * parts[:, G:], axis=0)
    rest = jnp.zeros((B - 2 * G, B), F32)
    columns = jnp.concatenate([total, mean, rest], axis=0).T
    table_sum[...] = jnp.zeros_like(table_sum)
    held[:, :, : SPAN * B] = jnp.zeros((G, B, SPAN * B), F32)
    held[:, :, SPAN * B + N :] = jnp.zeros((G, B, SPAN * B), F32)

    keys = far_ref[:, :, :E].reshape(N, E)
    values = far_ref[:, :, E:].reshape(N, E)
    low_end, high_end = table_ref[:, :B], table_ref[:, WIDE - B :]
    ends = jnp.concatenate([low_end, high_end, low_end, high_end], axis=1)
    row = lax.broadcasted_iota(jnp.int32, (B, B), 0)
    lane = lax.broadcasted_iota(jnp.int32, (B, B), 1)
    turn = (lane + row) % B
    early = lane + row < B
    lows, probs, turned = [], [], []
    end_sum = jnp.zeros((E, 4 * B), F32)

    def add_band(u, v, apart, flipped):
        spun = jnp.take_along_axis(held[u, :, block_at(v)], turn, axis=1)
        band = jnp.concatenate(
            [jnp.where(early, 0.0, spun), jnp.where(early, spun, 0.0)], axis=1
        ).astype(BF)
        table_sum[:, band_at(apart)] += nn(flipped[:E], band)
        return nt(band, table_ref[:, band_at(apart)])

    for u in range(G):
        paired = near_ref[u]
        flipped = paired.astype(F32).T.astype(BF)
        turned.append(flipped)
        total = columns[:, u : u + 1]
        mean = columns[:, G + u : G + u + 1]
        slope = nt(paired[:, E:], values)
        prob = jnp.exp(scores_ref[u * B : (u + 1) * B, :] - total)
        low = (prob * (slope - mean)).astype(BF)
        wide = low.astype(F32)
        held[u, :, SPAN * B : SPAN * B + N] = wide
        lower = jnp.zeros((B, B), F32)
        upper = jnp.zeros((B, B), F32)
        for v in range(G):
            apart = G * (v - place[0]) + place[1] - u
            piece = wide[:, v * B : (v + 1) * B]
            lower = lower + jnp.where(apart <= -REACH, piece, 0.0)
            upper = upper + jnp.where(apart >= REACH, piece, 0.0)
        outer = jnp.concatenate([lower, upper], axis=1)
        coarse = outer.astype(BF)
        fine = (outer - coarse.astype(F32)).astype(BF)
        outer = jnp.concatenate([coarse, fine], axis=1)
        end_sum = end_sum + nn(flipped[:E], outer)
        query_grad = nn(low, keys) + nt(outer, ends)
        for v, apart in near_tiles(place, u):
            query_grad = query_grad + add_band(u, v, apart, flipped)
        query_sum[u] = query_grad
        lows.append(low)
        probs.append(prob.astype(BF))
    flipped = near_ref[place[1]].astype(F32).T.astype(BF)
    query_sum[place[1]] += add_band(place[1], place[0] + 2, 2 * G, flipped)
    for u in range(G):
        query_low = (query_sum[u] * SCALE).astype(BF)
        near_out[u] = jnp.concatenate([query_low[:E], query_low[E:]], axis=1)
    both = jnp.concatenate(turned, axis=1)
    pairs = jnp.concatenate(
        [nn(both[:E], jnp.concatenate(lows, axis=0)), nn(both[E:], jnp.concatenate(probs, axis=0))],
        axis=0,
    )
    offsets = lax.broadcasted_iota(jnp.int32, (E, WIDE), 1) - (TABLE // 2 + PAD)
    terms = table_sum[...]
    tails = end_sum
    tails = tails[:, : 2 * B] + tails[:, 2 * B :]
    upper = jnp.sum(jnp.where(offsets >= clip, terms, 0.0), axis=1, keepdims=True)
    lower = jnp.sum(jnp.where(offsets <= -clip, terms, 0.0), axis=1, keepdims=True)
    upper = upper + jnp.sum(tails[:, B:], axis=1, keepdims=True)
    lower = lower + jnp.sum(tails[:, :B], axis=1, keepdims=True)
    table_sum[...] = jnp.where(offsets == clip, upper, jnp.where(offsets == -clip, lower, terms))
    first = place[1] % 2 == 0
    for slot in range(2 ** len(STRIDES)):
        block = table_sum[:, pl.ds(slot_column(place, slot), B)]
        at = lane[:E] + (slot_column(place, slot) - (TABLE // 2 + PAD))
        block = jnp.where(jnp.abs(at) <= clip, block, 0.0)
        top, end = block[: E // 2], block[E // 2 :]
        left = jnp.concatenate([top[:, :E], end[:, :E]], axis=1)
        right = jnp.concatenate([top[:, E:], end[:, E:]], axis=1)
        keep_out[slot] = jnp.where(first, left, right)
        send_out[slot] = jnp.where(first, right, left).astype(BF)
    for y in range(G):
        far_out[y] = pairs[:, y * B : (y + 1) * B].T.astype(BF)


def gradients(place, near, far, scores, parts, table):
    return pl.pallas_call(
        grads_kernel,
        in_specs=[SCALARS] + [ARRAY] * 5,
        out_specs=[ARRAY] * 4,
        out_shape=(
            jax.ShapeDtypeStruct((G, B, B), BF),
            jax.ShapeDtypeStruct((G, E, B), BF),
            jax.ShapeDtypeStruct((32, E // 2, B), F32),
            jax.ShapeDtypeStruct((32, E // 2, B), BF),
        ),
        scratch_shapes=[
            pltpu.VMEM((G, B, E), F32),
            pltpu.VMEM((E, WIDE), F32),
            pltpu.VMEM((G, B, N + 2 * SPAN * B), F32),
        ],
        compiler_params=pltpu.CompilerParams(vmem_limit_bytes=LIMIT),
        name="gradients",
    )(place, near, far, scores, parts, table)


def unproject_kernel(far_ref, near_ref, weights_ref, out_ref):
    pairs = jnp.sum(far_ref[...].astype(F32), axis=0).astype(BF)
    packed = jnp.sum(near_ref[...].astype(F32), axis=0).astype(BF)
    query = jnp.concatenate([packed[:, :E], packed[:, E:]], axis=0)
    terms = nn(query, weights_ref[:E]) + nn(pairs, weights_ref[E:])
    for h in range(G):
        out_ref[h] = terms[:, h * B : (h + 1) * B].astype(BF)


def unproject(far, near, weights):
    return pl.pallas_call(
        unproject_kernel,
        out_shape=jax.ShapeDtypeStruct((G, B, B), BF),
        compiler_params=pltpu.CompilerParams(vmem_limit_bytes=LIMIT),
        name="unproject",
    )(far, near, weights)


def exchange(parts, axis):
    return lax.all_to_all(parts, axis, 0, 0, tiled=True)


def to_all(shard):
    return jnp.broadcast_to(shard[None], (G,) + shard.shape)


def across(shard, stride):
    return lax.ppermute(shard, ("far", "near"), [(i, i ^ stride) for i in range(G * G)])


def shards(frames, weights, offset_table, clip_range, valid_frames, context_grad):
    weight_rows = weights.reshape(3 * E, G * B)
    place = jnp.stack([lax.axis_index("far"), lax.axis_index("near"), clip_range[0]])
    turned = offset_table.T
    mine = jnp.concatenate([turned[: E // 2], turned[E // 2 :]], axis=1)[None]
    for stride in STRIDES:
        mine = jnp.concatenate([mine, across(mine, stride)], axis=0)
    theirs = across(mine, 1)
    gathered = exchange(to_all(frames), "head")
    near, far = project(gathered, weight_rows, context_grad)
    near = exchange(near, "near")
    far = exchange(far, "far")
    scores, stats, table = statistics(place, valid_frames, near, far, mine, theirs)
    parts = exchange(to_all(stats), "near")
    far, near, keep, send = gradients(place, near, far, scores, parts, table)
    total = keep + across(send, 1).astype(F32)
    for stride in reversed(STRIDES):
        half = total.shape[0] // 2
        arrived = across(total[half:].astype(BF), stride)
        total = total[:half] + arrived.astype(F32)
    terms = unproject(exchange(far, "far"), exchange(near, "near"), weight_rows)
    table_grad = total[0].reshape(E // 2, 2, E).transpose(2, 1, 0).reshape(E, E)
    terms = exchange(terms, "head")
    input_grad = jnp.sum(terms.astype(F32), axis=0).astype(BF)
    return (input_grad, table_grad)


def solution(mesh):
    split = Mesh(mesh.devices.reshape(G, G, G), ("far", "near", "head"))
    seq = ("far", "near")
    placed = (
        P(seq, "head"),
        P(None, "head", None),
        P(seq, "head"),
        P("head"),
        P(),
        P(seq, "head"),
    )
    return jax.shard_map(
        shards,
        mesh=split,
        in_specs=placed,
        out_specs=(P(seq, "head"), P(seq, "head")),
        check_vma=False,
    )
```

time: 158 us -> 153 us (0.968)
  the two profiles are of different devices: /device:TPU:64 before, /device:TPU:120 now
where the time goes in v2:
time: 153 us; the launch traced here: 152 us
  starting transfers between devices  86.8 us (57%)
  waiting for transfers between devices  33.8 us (22%)
  Pallas kernels  15.2 us (10%)
  blocking collectives  7.72 us (5%)
  local copies, waits for them, and re-layouts  5.7 us (4%)
  between operations  1.57 us (1%)
    all_to_all x6, starting transfers between devices, exchange(): return lax.all_to_all(parts, axis, 0, 0, tiled=True)  44.2 us
    ppermute x12, starting transfers between devices, across(): lax.ppermute(shard, ('far', 'near'), [(i, i ^ stride) for i in range(G *...  42.7 us
    ppermute x12, waiting for transfers between devices, across(): lax.ppermute(shard, ('far', 'near'), [(i, i ^ stride) for i in range(G *...  25.5 us
    all_to_all x6, waiting for transfers between devices, exchange(): return lax.all_to_all(parts, axis, 0, 0, tiled=True)  8.35 us
    all_to_all x1, blocking collectives, exchange(): return lax.all_to_all(parts, axis, 0, 0, tiled=True)  7.72 us
    pallas_call x1, Pallas kernels, gradients(): pl.pallas_call(grads_kernel, in_specs=[SCALARS] + [ARRAY] * 5, out_specs=...  7.18 us
    pallas_call x1, Pallas kernels, statistics(): pl.pallas_call(stats_kernel, in_specs=[SCALARS] * 2 + [ARRAY] * 4, out_sp...  5.83 us
    unnamed x13, local copies, waits for them, and re-layouts  4.02 us
  transfers between devices with their start and end apart: 18, of which 11 were waited for; matrix products, arithmetic and copies ran while one was open for 2% of the time, Pallas kernels for 1%

profile of v2, /device:TPU:120, one launch (start us, length us, event | category | flops | bytes accessed | tf_op | source)
XLA Modules:
  0.0 151.8 jit_solution(9519313246855366184)
XLA Ops:
  0.6 1.5 broadcast_in_dim.6
  2.1 11.8 %all-to-all-start = ((bf16[8,128,128]{2,1,0:T(8,128)(2,1)}), bf16[8,128,128]{2,1,0:T(8,128)(2,1)S(1)}, u32[]{:S(2)}, u32[]{:S(2)}) async-start(bf16[8,128,128]{2,1,0:T(8,128)(2,1)} %broadcast_in_dim.6), calls=%async_computation | async-start | bytes 524288 | tf_op jit(solution)/shard_map/all_to_all | solution.py:306
  14.0 0.8 copy.12
  14.8 0.1 constant_dynamic-update-slice_fusion.4
  14.8 4.7 %collective-permute-start = (bf16[1,32,128]{2,1,0:T(8,128)(2,1)S(1)}, bf16[1,32,128]{2,1,0:T(8,128)(2,1)S(1)}, u32[]{:S(2)}, u32[]{:S(2)}) collective-permute-start(bf16[1,32,128]{2,1,0:T(8,128)(2,1)S(1)} %get-tuple-element.23), channel_id=1, source_target_pairs={{0,256},{8,264},{16,272},{24,280},{32,288},{40,296},{48,304},{56,3... | collective-permute-start | bytes 24584 | tf_op jit(solution)/shard_map/ppermute | solution.py:314
  19.6 0.8 copy.11.grad_ref
  20.4 3.9 %collective-permute-done = bf16[1,32,128]{2,1,0:T(8,128)(2,1)S(1)} collective-permute-done((bf16[1,32,128]{2,1,0:T(8,128)(2,1)S(1)}, bf16[1,32,128]{2,1,0:T(8,128)(2,1)S(1)}, u32[]{:S(2)}, u32[]{:S(2)}) %collective-permute-start) | collective-permute-done | bytes 8224 | tf_op jit(solution)/shard_map/ppermute | solution.py:314
  24.3 4.0 %collective-permute-start.1 = (bf16[2,32,128]{2,1,0:T(8,128)(2,1)S(1)}, bf16[2,32,128]{2,1,0:T(8,128)(2,1)S(1)}, u32[]{:S(2)}, u32[]{:S(2)}) collective-permute-start(bf16[2,32,128]{2,1,0:T(8,128)(2,1)S(1)} %pad_maximum_fusion.2), channel_id=1, source_target_pairs={{0,128},{8,136},{16,144},{24,152},{32,160},{40,168},{48,176},{56,1... | collective-permute-start | bytes 49160 | tf_op jit(solution)/shard_map/ppermute | solution.py:314
  28.4 2.5 %collective-permute-done.1 = bf16[2,32,128]{2,1,0:T(8,128)(2,1)S(1)} collective-permute-done((bf16[2,32,128]{2,1,0:T(8,128)(2,1)S(1)}, bf16[2,32,128]{2,1,0:T(8,128)(2,1)S(1)}, u32[]{:S(2)}, u32[]{:S(2)}) %collective-permute-start.1) | collective-permute-done | bytes 16416 | tf_op jit(solution)/shard_map/ppermute | solution.py:314
  30.8 3.2 %collective-permute-start.2 = (bf16[4,32,128]{2,1,0:T(8,128)(2,1)S(1)}, bf16[4,32,128]{2,1,0:T(8,128)(2,1)S(1)}, u32[]{:S(2)}, u32[]{:S(2)}) collective-permute-start(bf16[4,32,128]{2,1,0:T(8,128)(2,1)S(1)} %pad_maximum_fusion.1), channel_id=1, source_target_pairs={{0,64},{8,72},{16,80},{24,88},{32,96},{40,104},{48,112},{56,120},{... | collective-permute-start | bytes 98312 | tf_op jit(solution)/shard_map/ppermute | solution.py:314
  34.1 0.0 all-to-all-done.frames_ref
  34.1 0.0 copy-start
  34.1 1.0 copy-done
  35.1 1.2 project.1
  36.3 5.1 %all-to-all-start.1 = ((bf16[8,128,128]{2,1,0:T(8,128)(2,1)}), bf16[8,128,128]{2,1,0:T(8,128)(2,1)S(1)}, u32[]{:S(2)}, u32[]{:S(2)}) async-start(bf16[8,128,128]{2,1,0:T(8,128)(2,1)} %get-tuple-element.11), calls=%async_computation.1 | async-start | bytes 524288 | tf_op jit(solution)/shard_map/all_to_all | solution.py:306
  41.4 0.0 collective-permute-done.2
  41.5 4.3 %collective-permute-start.3 = (bf16[8,32,128]{2,1,0:T(8,128)(2,1)S(1)}, bf16[8,32,128]{2,1,0:T(8,128)(2,1)S(1)}, u32[]{:S(2)}, u32[]{:S(2)}) collective-permute-start(bf16[8,32,128]{2,1,0:T(8,128)(2,1)S(1)} %pad_maximum_fusion), channel_id=1, source_target_pairs={{0,32},{8,40},{16,48},{24,56},{32,0},{40,8},{48,16},{56,24},{64,96... | collective-permute-start | bytes 196616 | tf_op jit(solution)/shard_map/ppermute | solution.py:314
  45.8 4.9 %collective-permute-done.3 = bf16[8,32,128]{2,1,0:T(8,128)(2,1)S(1)} collective-permute-done((bf16[8,32,128]{2,1,0:T(8,128)(2,1)S(1)}, bf16[8,32,128]{2,1,0:T(8,128)(2,1)S(1)}, u32[]{:S(2)}, u32[]{:S(2)}) %collective-permute-start.3) | collective-permute-done | bytes 65568 | tf_op jit(solution)/shard_map/ppermute | solution.py:314
  50.7 5.2 %collective-permute-start.4 = (bf16[16,32,128]{2,1,0:T(8,128)(2,1)S(1)}, bf16[16,32,128]{2,1,0:T(8,128)(2,1)S(1)}, u32[]{:S(2)}, u32[]{:S(2)}) collective-permute-start(bf16[16,32,128]{2,1,0:T(8,128)(2,1)S(1)} %get-tuple-element.24), channel_id=1, source_target_pairs={{0,16},{8,24},{16,0},{24,8},{32,48},{40,56},{48,32},{56,40},{64,80... | collective-permute-start | bytes 393224 | tf_op jit(solution)/shard_map/ppermute | solution.py:314
  55.9 6.3 %all-to-all-start.2 = ((bf16[8,128,128]{2,1,0:T(8,128)(2,1)}), bf16[8,128,128]{2,1,0:T(8,128)(2,1)S(1)}, u32[]{:S(2)}, u32[]{:S(2)}) async-start(bf16[8,128,128]{2,1,0:T(8,128)(2,1)} %get-tuple-element.12), calls=%async_computation.2 | async-start | bytes 524288 | tf_op jit(solution)/shard_map/all_to_all | solution.py:306
  62.2 1.9 %collective-permute-start.5 = (bf16[32,32,128]{2,1,0:T(8,128)(2,1)S(1)}, bf16[32,32,128]{2,1,0:T(8,128)(2,1)S(1)}, u32[]{:S(2)}, u32[]{:S(2)}) collective-permute-start(bf16[32,32,128]{2,1,0:T(8,128)(2,1)S(1)} %constant_dynamic-update-slice_fusion.5.mine_ref), channel_id=1, source_target_pairs={{0,8},{8,0},{16,24},{24,16},{32,40},{40,32},{48,56},{56,48},{64,72... | collective-permute-start | bytes 786440 | tf_op jit(solution)/shard_map/ppermute | solution.py:314
  64.8 0.1 pad_add_fusion.place
  64.9 0.8 collective-permute-done.5.theirs_ref
  65.7 4.2 %all-to-all-done.2.far_ref = bf16[8,128,128]{2,1,0:T(8,128)(2,1)S(1)} async-done(((bf16[8,128,128]{2,1,0:T(8,128)(2,1)}), bf16[8,128,128]{2,1,0:T(8,128)(2,1)S(1)}, u32[]{:S(2)}, u32[]{:S(2)}) %all-to-all-start.2) | async-done | bytes 262176 | tf_op jit(solution)/shard_map/all_to_all | solution.py:306
  69.9 0.7 copy-done.2
  70.5 5.8 %statistics.1 = (f32[1024,1024]{1,0:T(8,128)S(1)}, f32[16,128]{1,0:T(8,128)S(1)}, bf16[64,4608]{1,0:T(8,128)(2,1)S(1)}) custom-call(s32[3]{0:T(128)S(1)} %pad_add_fusion.place, s32[64]{0:T(128)S(1)} %copy-done.2, bf16[8,128,128]{2,1,0:T(8,128)(2,1)S(1)} %all-to-all-done.1.near_ref, bf16[8,128,128]{2,1,0:T(8,128)(2,1)S(1)} %all-to-all-done.2.far_ref, ...), custom_call_target="tpu_custom_call" | custom-call | tf_op jit(solution)/shard_map/statistics/pallas_call | solution.py:143
  76.4 7.7 %all_to_all.35.parts_ref = f32[8,16,128]{2,1,0:T(8,128)S(1)} all-to-all(f32[8,16,128]{2,1,0:T(8,128)S(1)} %broadcast_in_dim.8), channel_id=1, replica_groups=mesh['far'=8,'near'=8,'head'=8] {'near'}, dimensions={0} | all-to-all | bytes 131072 | tf_op jit(solution)/shard_map/all_to_all | solution.py:306
  84.1 7.2 %gradients.1 = (bf16[8,128,128]{2,1,0:T(8,128)(2,1)}, bf16[8,64,128]{2,1,0:T(8,128)(2,1)}, f32[32,32,128]{2,1,0:T(8,128)S(1)}, bf16[32,32,128]{2,1,0:T(8,128)(2,1)S(1)}) custom-call(s32[3]{0:T(128)S(1)} %pad_add_fusion.place, bf16[8,128,128]{2,1,0:T(8,128)(2,1)S(1)} %all-to-all-done.1.near_ref, bf16[8,128,128]{2,1,0:T(8,128)(2,1)S(1)} %all-to-all-done.2.far_ref, ...), custom_call_target="tpu_custom_call" | custom-call | tf_op jit(solution)/shard_map/gradients/pallas_call | solution.py:267
  91.3 1.9 %collective-permute-start.6 = (bf16[32,32,128]{2,1,0:T(8,128)(2,1)S(1)}, bf16[32,32,128]{2,1,0:T(8,128)(2,1)S(1)}, u32[]{:S(2)}, u32[]{:S(2)}) collective-permute-start(bf16[32,32,128]{2,1,0:T(8,128)(2,1)S(1)} %get-tuple-element.19), channel_id=1, source_target_pairs={{0,8},{8,0},{16,24},{24,16},{32,40},{40,32},{48,56},{56,48},{64,72... | collective-permute-start | bytes 786440 | tf_op jit(solution)/shard_map/ppermute | solution.py:314
  93.2 1.5 collective-permute-done.6
  94.7 0.1 convert_add_fusion
  94.8 3.2 %collective-permute-start.7 = (bf16[16,32,128]{2,1,0:T(8,128)(2,1)S(1)}, bf16[16,32,128]{2,1,0:T(8,128)(2,1)S(1)}, u32[]{:S(2)}, u32[]{:S(2)}) collective-permute-start(bf16[16,32,128]{2,1,0:T(8,128)(2,1)S(1)} %slice.75), channel_id=1, source_target_pairs={{0,16},{8,24},{16,0},{24,8},{32,48},{40,56},{48,32},{56,40},{64,80... | collective-permute-start | bytes 393224 | tf_op jit(solution)/shard_map/ppermute | solution.py:314
  98.0 4.0 %all-to-all-start.5 = ((bf16[8,64,128]{2,1,0:T(8,128)(2,1)}), bf16[8,64,128]{2,1,0:T(8,128)(2,1)S(1)}, u32[]{:S(2)}, u32[]{:S(2)}) async-start(bf16[8,64,128]{2,1,0:T(8,128)(2,1)} %get-tuple-element.17), calls=%async_computation.5 | async-start | bytes 262144 | tf_op jit(solution)/shard_map/all_to_all | solution.py:306
  102.0 0.2 collective-permute-done.7
  102.3 4.1 %collective-permute-start.8 = (bf16[8,32,128]{2,1,0:T(8,128)(2,1)S(1)}, bf16[8,32,128]{2,1,0:T(8,128)(2,1)S(1)}, u32[]{:S(2)}, u32[]{:S(2)}) collective-permute-start(bf16[8,32,128]{2,1,0:T(8,128)(2,1)S(1)} %slice.76), channel_id=1, source_target_pairs={{0,32},{8,40},{16,48},{24,56},{32,0},{40,8},{48,16},{56,24},{64,96... | collective-permute-start | bytes 196616 | tf_op jit(solution)/shard_map/ppermute | solution.py:314
  106.4 1.4 all-to-all-done.5.near_ref
  107.8 7.3 %all-to-all-start.4 = ((bf16[8,128,128]{2,1,0:T(8,128)(2,1)}), bf16[8,128,128]{2,1,0:T(8,128)(2,1)S(1)}, u32[]{:S(2)}, u32[]{:S(2)}) async-start(bf16[8,128,128]{2,1,0:T(8,128)(2,1)} %get-tuple-element.16), calls=%async_computation.4 | async-start | bytes 524288 | tf_op jit(solution)/shard_map/all_to_all | solution.py:306
  115.1 3.4 %collective-permute-start.9 = (bf16[4,32,128]{2,1,0:T(8,128)(2,1)S(1)}, bf16[4,32,128]{2,1,0:T(8,128)(2,1)S(1)}, u32[]{:S(2)}, u32[]{:S(2)}) collective-permute-start(bf16[4,32,128]{2,1,0:T(8,128)(2,1)S(1)} %slice.77), channel_id=1, source_target_pairs={{0,64},{8,72},{16,80},{24,88},{32,96},{40,104},{48,112},{56,120},{... | collective-permute-start | bytes 98312 | tf_op jit(solution)/shard_map/ppermute | solution.py:314
  118.5 4.4 %collective-permute-done.9 = bf16[4,32,128]{2,1,0:T(8,128)(2,1)S(1)} collective-permute-done((bf16[4,32,128]{2,1,0:T(8,128)(2,1)S(1)}, bf16[4,32,128]{2,1,0:T(8,128)(2,1)S(1)}, u32[]{:S(2)}, u32[]{:S(2)}) %collective-permute-start.9) | collective-permute-done | bytes 32800 | tf_op jit(solution)/shard_map/ppermute | solution.py:314
  122.9 4.6 %collective-permute-start.10 = (bf16[2,32,128]{2,1,0:T(8,128)(2,1)S(1)}, bf16[2,32,128]{2,1,0:T(8,128)(2,1)S(1)}, u32[]{:S(2)}, u32[]{:S(2)}) collective-permute-start(bf16[2,32,128]{2,1,0:T(8,128)(2,1)S(1)} %slice.78), channel_id=1, source_target_pairs={{0,128},{8,136},{16,144},{24,152},{32,160},{40,168},{48,176},{56,1... | collective-permute-start | bytes 49160 | tf_op jit(solution)/shard_map/ppermute | solution.py:314
  127.5 1.0 unproject.1
  128.5 9.6 %all-to-all-start.6 = ((bf16[8,128,128]{2,1,0:T(8,128)(2,1)}), bf16[8,128,128]{2,1,0:T(8,128)(2,1)S(1)}, u32[]{:S(2)}, u32[]{:S(2)}) async-start(bf16[8,128,128]{2,1,0:T(8,128)(2,1)} %unproject.1), calls=%async_computation.6 | async-start | bytes 524288 | tf_op jit(solution)/shard_map/all_to_all | solution.py:306
  138.2 2.2 %collective-permute-start.11 = (bf16[1,32,128]{2,1,0:T(8,128)(2,1)S(1)}, bf16[1,32,128]{2,1,0:T(8,128)(2,1)S(1)}, u32[]{:S(2)}, u32[]{:S(2)}) collective-permute-start(bf16[1,32,128]{2,1,0:T(8,128)(2,1)S(1)} %slice.79), channel_id=1, source_target_pairs={{0,256},{8,264},{16,272},{24,280},{32,288},{40,296},{48,304},{56,3... | collective-permute-start | bytes 24584 | tf_op jit(solution)/shard_map/ppermute | solution.py:314
  140.3 7.3 %collective-permute-done.11 = bf16[1,32,128]{2,1,0:T(8,128)(2,1)S(1)} collective-permute-done((bf16[1,32,128]{2,1,0:T(8,128)(2,1)S(1)}, bf16[1,32,128]{2,1,0:T(8,128)(2,1)S(1)}, u32[]{:S(2)}, u32[]{:S(2)}) %collective-permute-start.11) | collective-permute-done | bytes 8224 | tf_op jit(solution)/shard_map/ppermute | solution.py:314
  147.6 0.1 reshape_squeeze.3
  147.7 0.7 copy.14
  148.4 2.7 %all-to-all-done.6 = bf16[8,128,128]{2,1,0:T(8,128)(2,1)S(1)} async-done(((bf16[8,128,128]{2,1,0:T(8,128)(2,1)}), bf16[8,128,128]{2,1,0:T(8,128)(2,1)S(1)}, u32[]{:S(2)}, u32[]{:S(2)}) %all-to-all-start.6) | async-done | bytes 262176 | tf_op jit(solution)/shard_map/all_to_all | solution.py:306
  151.2 0.7 reduce_sum.12
  (30 shorter events, 0.3 us)
Async XLA Ops:
  2.1 32.0 %all-to-all-start = ((bf16[8,128,128]{2,1,0:T(8,128)(2,1)}), bf16[8,128,128]{2,1,0:T(8,128)(2,1)S(1)}, u32[]{:S(2)}, u32[]{:S(2)}) async-start(bf16[8,128,128]{2,1,0:T(8,128)(2,1)} %broadcast_in_dim.6), calls=%async_computation | async-start | bytes 524288 | tf_op jit(solution)/shard_map/all_to_all | solution.py:306
  14.8 9.4 %collective-permute-start = (bf16[1,32,128]{2,1,0:T(8,128)(2,1)S(1)}, bf16[1,32,128]{2,1,0:T(8,128)(2,1)S(1)}, u32[]{:S(2)}, u32[]{:S(2)}) collective-permute-start(bf16[1,32,128]{2,1,0:T(8,128)(2,1)S(1)} %get-tuple-element.23), channel_id=1, source_target_pairs={{0,256},{8,264},{16,272},{24,280},{32,288},{40,296},{48,304},{56,3... | collective-permute-start | bytes 24584 | tf_op jit(solution)/shard_map/ppermute | solution.py:314
  24.3 6.5 %collective-permute-start.1 = (bf16[2,32,128]{2,1,0:T(8,128)(2,1)S(1)}, bf16[2,32,128]{2,1,0:T(8,128)(2,1)S(1)}, u32[]{:S(2)}, u32[]{:S(2)}) collective-permute-start(bf16[2,32,128]{2,1,0:T(8,128)(2,1)S(1)} %pad_maximum_fusion.2), channel_id=1, source_target_pairs={{0,128},{8,136},{16,144},{24,152},{32,160},{40,168},{48,176},{56,1... | collective-permute-start | bytes 49160 | tf_op jit(solution)/shard_map/ppermute | solution.py:314
  30.8 10.6 %collective-permute-start.2 = (bf16[4,32,128]{2,1,0:T(8,128)(2,1)S(1)}, bf16[4,32,128]{2,1,0:T(8,128)(2,1)S(1)}, u32[]{:S(2)}, u32[]{:S(2)}) collective-permute-start(bf16[4,32,128]{2,1,0:T(8,128)(2,1)S(1)} %pad_maximum_fusion.1), channel_id=1, source_target_pairs={{0,64},{8,72},{16,80},{24,88},{32,96},{40,104},{48,112},{56,120},{... | collective-permute-start | bytes 98312 | tf_op jit(solution)/shard_map/ppermute | solution.py:314
  34.1 1.0 copy-start
  36.3 19.6 %all-to-all-start.1 = ((bf16[8,128,128]{2,1,0:T(8,128)(2,1)}), bf16[8,128,128]{2,1,0:T(8,128)(2,1)S(1)}, u32[]{:S(2)}, u32[]{:S(2)}) async-start(bf16[8,128,128]{2,1,0:T(8,128)(2,1)} %get-tuple-element.11), calls=%async_computation.1 | async-start | bytes 524288 | tf_op jit(solution)/shard_map/all_to_all | solution.py:306
  41.5 9.2 %collective-permute-start.3 = (bf16[8,32,128]{2,1,0:T(8,128)(2,1)S(1)}, bf16[8,32,128]{2,1,0:T(8,128)(2,1)S(1)}, u32[]{:S(2)}, u32[]{:S(2)}) collective-permute-start(bf16[8,32,128]{2,1,0:T(8,128)(2,1)S(1)} %pad_maximum_fusion), channel_id=1, source_target_pairs={{0,32},{8,40},{16,48},{24,56},{32,0},{40,8},{48,16},{56,24},{64,96... | collective-permute-start | bytes 196616 | tf_op jit(solution)/shard_map/ppermute | solution.py:314
  50.7 11.5 %collective-permute-start.4 = (bf16[16,32,128]{2,1,0:T(8,128)(2,1)S(1)}, bf16[16,32,128]{2,1,0:T(8,128)(2,1)S(1)}, u32[]{:S(2)}, u32[]{:S(2)}) collective-permute-start(bf16[16,32,128]{2,1,0:T(8,128)(2,1)S(1)} %get-tuple-element.24), channel_id=1, source_target_pairs={{0,16},{8,24},{16,0},{24,8},{32,48},{40,56},{48,32},{56,40},{64,80... | collective-permute-start | bytes 393224 | tf_op jit(solution)/shard_map/ppermute | solution.py:314
  55.9 14.0 %all-to-all-start.2 = ((bf16[8,128,128]{2,1,0:T(8,128)(2,1)}), bf16[8,128,128]{2,1,0:T(8,128)(2,1)S(1)}, u32[]{:S(2)}, u32[]{:S(2)}) async-start(bf16[8,128,128]{2,1,0:T(8,128)(2,1)} %get-tuple-element.12), calls=%async_computation.2 | async-start | bytes 524288 | tf_op jit(solution)/shard_map/all_to_all | solution.py:306
  62.2 3.4 %collective-permute-start.5 = (bf16[32,32,128]{2,1,0:T(8,128)(2,1)S(1)}, bf16[32,32,128]{2,1,0:T(8,128)(2,1)S(1)}, u32[]{:S(2)}, u32[]{:S(2)}) collective-permute-start(bf16[32,32,128]{2,1,0:T(8,128)(2,1)S(1)} %constant_dynamic-update-slice_fusion.5.mine_ref), channel_id=1, source_target_pairs={{0,8},{8,0},{16,24},{24,16},{32,40},{40,32},{48,56},{56,48},{64,72... | collective-permute-start | bytes 786440 | tf_op jit(solution)/shard_map/ppermute | solution.py:314
  69.9 0.7 copy-start.2
  84.1 43.4 %copy-start.1 = (bf16[3,64,1024]{2,1,0:T(8,128)(2,1)S(1)}, bf16[3,64,1024]{2,1,0:T(8,128)(2,1)}, u32[]{:S(2)}) copy-start(bf16[3,64,1024]{2,1,0:T(8,128)(2,1)} %param.7) | copy-start | bytes 1179652
  91.3 3.4 %collective-permute-start.6 = (bf16[32,32,128]{2,1,0:T(8,128)(2,1)S(1)}, bf16[32,32,128]{2,1,0:T(8,128)(2,1)S(1)}, u32[]{:S(2)}, u32[]{:S(2)}) collective-permute-start(bf16[32,32,128]{2,1,0:T(8,128)(2,1)S(1)} %get-tuple-element.19), channel_id=1, source_target_pairs={{0,8},{8,0},{16,24},{24,16},{32,40},{40,32},{48,56},{56,48},{64,72... | collective-permute-start | bytes 786440 | tf_op jit(solution)/shard_map/ppermute | solution.py:314
  94.8 7.4 %collective-permute-start.7 = (bf16[16,32,128]{2,1,0:T(8,128)(2,1)S(1)}, bf16[16,32,128]{2,1,0:T(8,128)(2,1)S(1)}, u32[]{:S(2)}, u32[]{:S(2)}) collective-permute-start(bf16[16,32,128]{2,1,0:T(8,128)(2,1)S(1)} %slice.75), channel_id=1, source_target_pairs={{0,16},{8,24},{16,0},{24,8},{32,48},{40,56},{48,32},{56,40},{64,80... | collective-permute-start | bytes 393224 | tf_op jit(solution)/shard_map/ppermute | solution.py:314
  98.0 9.8 %all-to-all-start.5 = ((bf16[8,64,128]{2,1,0:T(8,128)(2,1)}), bf16[8,64,128]{2,1,0:T(8,128)(2,1)S(1)}, u32[]{:S(2)}, u32[]{:S(2)}) async-start(bf16[8,64,128]{2,1,0:T(8,128)(2,1)} %get-tuple-element.17), calls=%async_computation.5 | async-start | bytes 262144 | tf_op jit(solution)/shard_map/all_to_all | solution.py:306
  102.3 12.8 %collective-permute-start.8 = (bf16[8,32,128]{2,1,0:T(8,128)(2,1)S(1)}, bf16[8,32,128]{2,1,0:T(8,128)(2,1)S(1)}, u32[]{:S(2)}, u32[]{:S(2)}) collective-permute-start(bf16[8,32,128]{2,1,0:T(8,128)(2,1)S(1)} %slice.76), channel_id=1, source_target_pairs={{0,32},{8,40},{16,48},{24,56},{32,0},{40,8},{48,16},{56,24},{64,96... | collective-permute-start | bytes 196616 | tf_op jit(solution)/shard_map/ppermute | solution.py:314
  107.8 19.7 %all-to-all-start.4 = ((bf16[8,128,128]{2,1,0:T(8,128)(2,1)}), bf16[8,128,128]{2,1,0:T(8,128)(2,1)S(1)}, u32[]{:S(2)}, u32[]{:S(2)}) async-start(bf16[8,128,128]{2,1,0:T(8,128)(2,1)} %get-tuple-element.16), calls=%async_computation.4 | async-start | bytes 524288 | tf_op jit(solution)/shard_map/all_to_all | solution.py:306
  115.1 7.8 %collective-permute-start.9 = (bf16[4,32,128]{2,1,0:T(8,128)(2,1)S(1)}, bf16[4,32,128]{2,1,0:T(8,128)(2,1)S(1)}, u32[]{:S(2)}, u32[]{:S(2)}) collective-permute-start(bf16[4,32,128]{2,1,0:T(8,128)(2,1)S(1)} %slice.77), channel_id=1, source_target_pairs={{0,64},{8,72},{16,80},{24,88},{32,96},{40,104},{48,112},{56,120},{... | collective-permute-start | bytes 98312 | tf_op jit(solution)/shard_map/ppermute | solution.py:314
  122.9 15.2 %collective-permute-start.10 = (bf16[2,32,128]{2,1,0:T(8,128)(2,1)S(1)}, bf16[2,32,128]{2,1,0:T(8,128)(2,1)S(1)}, u32[]{:S(2)}, u32[]{:S(2)}) collective-permute-start(bf16[2,32,128]{2,1,0:T(8,128)(2,1)S(1)} %slice.78), channel_id=1, source_target_pairs={{0,128},{8,136},{16,144},{24,152},{32,160},{40,168},{48,176},{56,1... | collective-permute-start | bytes 49160 | tf_op jit(solution)/shard_map/ppermute | solution.py:314
  128.5 22.6 %all-to-all-start.6 = ((bf16[8,128,128]{2,1,0:T(8,128)(2,1)}), bf16[8,128,128]{2,1,0:T(8,128)(2,1)S(1)}, u32[]{:S(2)}, u32[]{:S(2)}) async-start(bf16[8,128,128]{2,1,0:T(8,128)(2,1)} %unproject.1), calls=%async_computation.6 | async-start | bytes 524288 | tf_op jit(solution)/shard_map/all_to_all | solution.py:306
  138.2 9.5 %collective-permute-start.11 = (bf16[1,32,128]{2,1,0:T(8,128)(2,1)S(1)}, bf16[1,32,128]{2,1,0:T(8,128)(2,1)S(1)}, u32[]{:S(2)}, u32[]{:S(2)}) collective-permute-start(bf16[1,32,128]{2,1,0:T(8,128)(2,1)S(1)} %slice.79), channel_id=1, source_target_pairs={{0,256},{8,264},{16,272},{24,280},{32,288},{40,296},{48,304},{56,3... | collective-permute-start | bytes 24584 | tf_op jit(solution)/shard_map/ppermute | solution.py:314

commit v3 on v2

--- a/solution.py
+++ b/solution.py
@@ -16,7 +16,9 @@
 WIDE = TABLE + 2 * PAD
 SCALE = E ** (-0.5)
 SPAN = 2
-STRIDES = (32, 16, 8, 4, 2)
+STRIDES = (4, 2)
+SLOTS = 32
+ROWS = B + E // 2
 HIDDEN = -1e30
 BF = jnp.bfloat16
 F32 = jnp.float32
@@ -31,7 +33,7 @@
     return lax.dot_general(a, b, (((1,), (0,)), ((), ())), preferred_element_type=F32)
 
 
-def project_kernel(frames_ref, weights_ref, grad_ref, near_ref, far_ref):
+def project_kernel(frames_ref, weights_ref, grad_ref, chunk_ref, near_ref, far_ref):
     total = jnp.zeros((B, 3 * E), F32)
     for h in range(G):
         total = total + nt(frames_ref[h], weights_ref[:, h * B : (h + 1) * B])
@@ -40,22 +42,23 @@
     paired = jnp.concatenate([scaled, grad_ref[...]], axis=1)
     for g in range(G):
         near_ref[g] = paired
-        far_ref[g] = low[:, E:]
-
-
-def project(frames, weights, grad):
+        far_ref[g, :B] = low[:, E:]
+        far_ref[g, B:] = chunk_ref[...]
+
+
+def project(frames, weights, grad, chunk):
     return pl.pallas_call(
         project_kernel,
-        out_shape=(jax.ShapeDtypeStruct((G, B, B), BF), jax.ShapeDtypeStruct((G, B, B), BF)),
+        out_shape=(jax.ShapeDtypeStruct((G, B, B), BF), jax.ShapeDtypeStruct((G, ROWS, B), BF)),
         compiler_params=pltpu.CompilerParams(vmem_limit_bytes=LIMIT),
         name="project",
-    )(frames, weights, grad)
+    )(frames, weights, grad, chunk)
 
 
 def slot_column(place, slot):
-    bits = sum(((slot >> k) & 1) * (STRIDES[k] // 2) for k in range(len(STRIDES)))
-    own = place[0] * (G // 2) + place[1] // 2
-    return pl.multiple_of(PAD + jnp.bitwise_xor(own, bits) * B, B)
+    turn, y = slot // G, slot % G
+    block = 4 * y + jnp.bitwise_xor(place[1] // 2, (turn % 2) * 2 + turn // 2)
+    return pl.multiple_of(PAD + block * B, B)
 
 
 def near_tiles(place, u):
@@ -73,13 +76,23 @@
 
 
 def stats_kernel(
-    place, valid, near_ref, far_ref, mine_ref, theirs_ref, scores_ref, stats_ref, table_ref, shifts
+    place,
+    valid,
+    near_ref,
+    far_ref,
+    mine_ref,
+    theirs_ref,
+    weight_ref,
+    stats_ref,
+    tops_ref,
+    table_ref,
+    shifts,
 ):
     clip = place[2]
     table_ref[:, :PAD] = jnp.zeros((E, PAD), BF)
     table_ref[:, WIDE - PAD :] = jnp.zeros((E, PAD), BF)
     first = place[1] % 2 == 0
-    for slot in range(2 ** len(STRIDES)):
+    for slot in range(SLOTS):
         mine = mine_ref[slot].astype(F32)
         theirs = theirs_ref[slot].astype(F32)
         left = jnp.where(first, mine, theirs)
@@ -95,8 +108,8 @@
     rows = jnp.where(offsets >= clip, upper, jnp.where(offsets <= -clip, lower, rows))
     table_ref[...] = rows.astype(BF)
 
-    keys = far_ref[:, :, :E].reshape(N, E)
-    values = far_ref[:, :, E:].reshape(N, E)
+    keys = far_ref[:, :B, :E].reshape(N, E)
+    values = far_ref[:, :B, E:].reshape(N, E)
     ends = jnp.concatenate([table_ref[:, :B], table_ref[:, WIDE - B :]], axis=1)
     lane = lax.broadcasted_iota(jnp.int32, (B, B), 1)
     row = lax.broadcasted_iota(jnp.int32, (B, B), 0)
@@ -124,15 +137,16 @@
             both = content[:, v * B : (v + 1) * B] + shifts[u, :, at : at + B]
             pieces.append(jnp.where(lane < valid[G * v + place[1]], both, HIDDEN))
         scores = jnp.concatenate(pieces, axis=1)
-        scores_ref[u * B : (u + 1) * B, :] = scores
         top = jnp.max(scores, axis=1, keepdims=True)
         weight = jnp.exp(scores - top)
+        weight_ref[u * B : (u + 1) * B, :] = weight
         amount = jnp.sum(weight, axis=1, keepdims=True)
         mean = jnp.sum(weight * slope, axis=1, keepdims=True) / amount
-        both = jnp.where(lane == 0, top + jnp.log(amount), jnp.where(lane == 1, mean, 0.0))
+        both = jnp.where(lane == 0, top + jnp.log(amount), jnp.where(lane == 1, mean, top))
         turned = both.T
         stats_ref[u : u + 1, :] = turned[0:1]
         stats_ref[G + u : G + u + 1, :] = turned[1:2]
+        tops_ref[u : u + 1, :] = turned[2:3]
 
 
 SCALARS = pl.BlockSpec(memory_space=pltpu.SMEM)
@@ -143,10 +157,11 @@
     return pl.pallas_call(
         stats_kernel,
         in_specs=[SCALARS] * 2 + [ARRAY] * 4,
-        out_specs=[ARRAY] * 3,
+        out_specs=[ARRAY] * 4,
         out_shape=(
             jax.ShapeDtypeStruct((N, N), F32),
             jax.ShapeDtypeStruct((2 * G, B), F32),
+            jax.ShapeDtypeStruct((G, B), F32),
             jax.ShapeDtypeStruct((E, WIDE), BF),
         ),
         scratch_shapes=[pltpu.VMEM((G, B, N + 2 * SPAN * B), F32)],
@@ -159,7 +174,8 @@
     place,
     near_ref,
     far_ref,
-    scores_ref,
+    weight_ref,
+    tops_ref,
     parts_ref,
     table_ref,
     far_out,
@@ -177,13 +193,13 @@
     total = top + jnp.log(jnp.sum(jnp.exp(each - top[None]), axis=0))
     mean = jnp.sum(jnp.exp(each - total[None]) * parts[:, G:], axis=0)
     rest = jnp.zeros((B - 2 * G, B), F32)
-    columns = jnp.concatenate([total, mean, rest], axis=0).T
+    columns = jnp.concatenate([jnp.exp(tops_ref[...] - total), mean, rest], axis=0).T
     table_sum[...] = jnp.zeros_like(table_sum)
     held[:, :, : SPAN * B] = jnp.zeros((G, B, SPAN * B), F32)
     held[:, :, SPAN * B + N :] = jnp.zeros((G, B, SPAN * B), F32)
 
-    keys = far_ref[:, :, :E].reshape(N, E)
-    values = far_ref[:, :, E:].reshape(N, E)
+    keys = far_ref[:, :B, :E].reshape(N, E)
+    values = far_ref[:, :B, E:].reshape(N, E)
     low_end, high_end = table_ref[:, :B], table_ref[:, WIDE - B :]
     ends = jnp.concatenate([low_end, high_end, low_end, high_end], axis=1)
     row = lax.broadcasted_iota(jnp.int32, (B, B), 0)
@@ -205,10 +221,10 @@
         paired = near_ref[u]
         flipped = paired.astype(F32).T.astype(BF)
         turned.append(flipped)
-        total = columns[:, u : u + 1]
+        factor = columns[:, u : u + 1]
         mean = columns[:, G + u : G + u + 1]
         slope = nt(paired[:, E:], values)
-        prob = jnp.exp(scores_ref[u * B : (u + 1) * B, :] - total)
+        prob = weight_ref[u * B : (u + 1) * B, :] * factor
         low = (prob * (slope - mean)).astype(BF)
         wide = low.astype(F32)
         held[u, :, SPAN * B : SPAN * B + N] = wide
@@ -250,7 +266,7 @@
     lower = lower + jnp.sum(tails[:, :B], axis=1, keepdims=True)
     table_sum[...] = jnp.where(offsets == clip, upper, jnp.where(offsets == -clip, lower, terms))
     first = place[1] % 2 == 0
-    for slot in range(2 ** len(STRIDES)):
+    for slot in range(SLOTS):
         block = table_sum[:, pl.ds(slot_column(place, slot), B)]
         at = lane[:E] + (slot_column(place, slot) - (TABLE // 2 + PAD))
         block = jnp.where(jnp.abs(at) <= clip, block, 0.0)
@@ -259,17 +275,18 @@
         right = jnp.concatenate([top[:, E:], end[:, E:]], axis=1)
         keep_out[slot] = jnp.where(first, left, right)
         send_out[slot] = jnp.where(first, right, left).astype(BF)
+    far_out[:, B:] = jnp.zeros((G, E // 2, B), BF)
     for y in range(G):
-        far_out[y] = pairs[:, y * B : (y + 1) * B].T.astype(BF)
-
-
-def gradients(place, near, far, scores, parts, table):
+        far_out[y, :B] = pairs[:, y * B : (y + 1) * B].T.astype(BF)
+
+
+def gradients(place, near, far, weight, tops, parts, table):
     return pl.pallas_call(
         grads_kernel,
-        in_specs=[SCALARS] + [ARRAY] * 5,
+        in_specs=[SCALARS] + [ARRAY] * 6,
         out_specs=[ARRAY] * 4,
         out_shape=(
-            jax.ShapeDtypeStruct((G, B, B), BF),
+            jax.ShapeDtypeStruct((G, ROWS, B), BF),
             jax.ShapeDtypeStruct((G, E, B), BF),
             jax.ShapeDtypeStruct((32, E // 2, B), F32),
             jax.ShapeDtypeStruct((32, E // 2, B), BF),
@@ -281,11 +298,13 @@
         ],
         compiler_params=pltpu.CompilerParams(vmem_limit_bytes=LIMIT),
         name="gradients",
-    )(place, near, far, scores, parts, table)
-
-
-def unproject_kernel(far_ref, near_ref, weights_ref, out_ref):
-    pairs = jnp.sum(far_ref[...].astype(F32), axis=0).astype(BF)
+    )(place, near, far, weight, tops, parts, table)
+
+
+def unproject_kernel(far_ref, near_ref, weights_ref, out_ref, table_ref):
+    total = jnp.sum(far_ref[...].astype(F32), axis=0)
+    pairs = total[:B].astype(BF)
+    table_ref[...] = total[B:]
     packed = jnp.sum(near_ref[...].astype(F32), axis=0).astype(BF)
     query = jnp.concatenate([packed[:, :E], packed[:, E:]], axis=0)
     terms = nn(query, weights_ref[:E]) + nn(pairs, weights_ref[E:])
@@ -296,7 +315,10 @@
 def unproject(far, near, weights):
     return pl.pallas_call(
         unproject_kernel,
-        out_shape=jax.ShapeDtypeStruct((G, B, B), BF),
+        out_shape=(
+            jax.ShapeDtypeStruct((G, B, B), BF),
+            jax.ShapeDtypeStruct((E // 2, B), F32),
+        ),
         compiler_params=pltpu.CompilerParams(vmem_limit_bytes=LIMIT),
         name="unproject",
     )(far, near, weights)
@@ -311,31 +333,33 @@
 
 
 def across(shard, stride):
-    return lax.ppermute(shard, ("far", "near"), [(i, i ^ stride) for i in range(G * G)])
+    return lax.ppermute(shard, "near", [(i, i ^ stride) for i in range(G)])
 
 
 def shards(frames, weights, offset_table, clip_range, valid_frames, context_grad):
     weight_rows = weights.reshape(3 * E, G * B)
     place = jnp.stack([lax.axis_index("far"), lax.axis_index("near"), clip_range[0]])
     turned = offset_table.T
-    mine = jnp.concatenate([turned[: E // 2], turned[E // 2 :]], axis=1)[None]
+    chunk = jnp.concatenate([turned[: E // 2], turned[E // 2 :]], axis=1)
+    gathered = exchange(to_all(frames), "head")
+    near, far = project(gathered, weight_rows, context_grad, chunk)
+    far = exchange(far, "far")
+    mine = far[:, B:]
     for stride in STRIDES:
         mine = jnp.concatenate([mine, across(mine, stride)], axis=0)
     theirs = across(mine, 1)
-    gathered = exchange(to_all(frames), "head")
-    near, far = project(gathered, weight_rows, context_grad)
     near = exchange(near, "near")
-    far = exchange(far, "far")
-    scores, stats, table = statistics(place, valid_frames, near, far, mine, theirs)
+    weight, stats, tops, table = statistics(place, valid_frames, near, far, mine, theirs)
     parts = exchange(to_all(stats), "near")
-    far, near, keep, send = gradients(place, near, far, scores, parts, table)
+    far, near, keep, send = gradients(place, near, far, weight, tops, parts, table)
     total = keep + across(send, 1).astype(F32)
     for stride in reversed(STRIDES):
         half = total.shape[0] // 2
         arrived = across(total[half:].astype(BF), stride)
         total = total[:half] + arrived.astype(F32)
-    terms = unproject(exchange(far, "far"), exchange(near, "near"), weight_rows)
-    table_grad = total[0].reshape(E // 2, 2, E).transpose(2, 1, 0).reshape(E, E)
+    far = far.at[:, B:].set(total.astype(BF))
+    terms, table_part = unproject(exchange(far, "far"), exchange(near, "near"), weight_rows)
+    table_grad = table_part.reshape(E // 2, 2, E).transpose(2, 1, 0).reshape(E, E)
     terms = exchange(terms, "head")
     input_grad = jnp.sum(terms.astype(F32), axis=0).astype(BF)
     return (input_grad, table_grad)

time: 153 us -> 154 us (level)
  the two profiles are of different devices: /device:TPU:120 before, /device:TPU:64 now
where the time goes in v3:
time: 154 us; the launch traced here: 153 us
  waiting for transfers between devices  45.4 us (29%)
  blocking collectives  42.7 us (28%)
  starting transfers between devices  42 us (27%)
  Pallas kernels  14.8 us (10%)
  local copies, waits for them, and re-layouts  5.61 us (4%)
    all_to_all x3, blocking collectives, exchange(): return lax.all_to_all(parts, axis, 0, 0, tiled=True)  42.7 us
    all_to_all x4, waiting for transfers between devices, exchange(): return lax.all_to_all(parts, axis, 0, 0, tiled=True)  34.9 us
    all_to_all x4, starting transfers between devices, exchange(): return lax.all_to_all(parts, axis, 0, 0, tiled=True)  25.9 us
    ppermute x6, starting transfers between devices, across(): return lax.ppermute(shard, 'near', [(i, i ^ stride) for i in range(G)])  16.1 us
    ppermute x6, waiting for transfers between devices, across(): return lax.ppermute(shard, 'near', [(i, i ^ stride) for i in range(G)])  10.5 us
    pallas_call x1, Pallas kernels, gradients(): pl.pallas_call(grads_kernel, in_specs=[SCALARS] + [ARRAY] * 6, out_specs=...  6.97 us
    pallas_call x1, Pallas kernels, statistics(): pl.pallas_call(stats_kernel, in_specs=[SCALARS] * 2 + [ARRAY] * 4, out_sp...  5.69 us
    unnamed x9, local copies, waits for them, and re-layouts  3.99 us
  transfers between devices with their start and end apart: 10, of which 7 were waited for; matrix products, arithmetic and copies ran while one was open for 2% of the time, Pallas kernels for 0%

profile of v3, /device:TPU:64, one launch (start us, length us, event | category | flops | bytes accessed | tf_op | source)
XLA Modules:
  0.0 152.8 jit_solution(8442032249254522213)
XLA Ops:
  0.6 1.5 broadcast_in_dim.4
  2.1 11.8 %all-to-all-start = ((bf16[8,128,128]{2,1,0:T(8,128)(2,1)}), bf16[8,128,128]{2,1,0:T(8,128)(2,1)S(1)}, u32[]{:S(2)}, u32[]{:S(2)}) async-start(bf16[8,128,128]{2,1,0:T(8,128)(2,1)} %broadcast_in_dim.4), calls=%async_computation | async-start | bytes 524288 | tf_op jit(solution)/shard_map/all_to_all | solution.py:328
  14.0 0.8 copy.11
  14.8 0.8 copy.12.grad_ref
  15.6 0.1 pad_maximum_fusion.2.chunk_ref
  15.7 12.1 %all-to-all-done.frames_ref = bf16[8,128,128]{2,1,0:T(8,128)(2,1)S(1)} async-done(((bf16[8,128,128]{2,1,0:T(8,128)(2,1)}), bf16[8,128,128]{2,1,0:T(8,128)(2,1)S(1)}, u32[]{:S(2)}, u32[]{:S(2)}) %all-to-all-start) | async-done | bytes 262176 | tf_op jit(solution)/shard_map/all_to_all | solution.py:328
  27.8 0.0 copy-start
  27.8 1.0 copy-done
  28.8 1.1 project.1
  29.9 18.1 %all_to_all.35.far_ref = bf16[8,160,128]{2,1,0:T(8,128)(2,1)S(1)} all-to-all(bf16[8,160,128]{2,1,0:T(8,128)(2,1)S(1)} %get-tuple-element.27), channel_id=1, replica_groups=mesh['far'=8,'near'=8,'head'=8] {'far'}, dimensions={0} | all-to-all | bytes 655360 | tf_op jit(solution)/shard_map/all_to_all | solution.py:328
  48.0 2.3 %collective-permute-start = (bf16[8,32,128]{2,1,0:T(8,128)(2,1)S(1)}, bf16[8,32,128]{2,1,0:T(8,128)(2,1)S(1)}, u32[]{:S(2)}, u32[]{:S(2)}) collective-permute-start(bf16[8,32,128]{2,1,0:T(8,128)(2,1)S(1)} %slice.54), channel_id=1, source_target_pairs={{0,32},{8,40},{16,48},{24,56},{32,0},{40,8},{48,16},{56,24},{1,33}... | collective-permute-start | bytes 196616 | tf_op jit(solution)/shard_map/ppermute | solution.py:336
  50.3 4.7 %collective-permute-done = bf16[8,32,128]{2,1,0:T(8,128)(2,1)S(1)} collective-permute-done((bf16[8,32,128]{2,1,0:T(8,128)(2,1)S(1)}, bf16[8,32,128]{2,1,0:T(8,128)(2,1)S(1)}, u32[]{:S(2)}, u32[]{:S(2)}) %collective-permute-start) | collective-permute-done | bytes 65568 | tf_op jit(solution)/shard_map/ppermute | solution.py:336
  55.1 4.0 %collective-permute-start.1 = (bf16[16,32,128]{2,1,0:T(8,128)(2,1)S(1)}, bf16[16,32,128]{2,1,0:T(8,128)(2,1)S(1)}, u32[]{:S(2)}, u32[]{:S(2)}) collective-permute-start(bf16[16,32,128]{2,1,0:T(8,128)(2,1)S(1)} %pad_maximum_fusion.1), channel_id=1, source_target_pairs={{0,16},{8,24},{16,0},{24,8},{32,48},{40,56},{48,32},{56,40},{1,17}... | collective-permute-start | bytes 393224 | tf_op jit(solution)/shard_map/ppermute | solution.py:336
  59.1 5.7 %all-to-all-start.1 = ((bf16[8,128,128]{2,1,0:T(8,128)(2,1)}), bf16[8,128,128]{2,1,0:T(8,128)(2,1)S(1)}, u32[]{:S(2)}, u32[]{:S(2)}) async-start(bf16[8,128,128]{2,1,0:T(8,128)(2,1)} %get-tuple-element.26), calls=%async_computation.1 | async-start | bytes 524288 | tf_op jit(solution)/shard_map/all_to_all | solution.py:328
  64.8 0.0 collective-permute-done.1
  64.8 2.1 %collective-permute-start.2 = (bf16[32,32,128]{2,1,0:T(8,128)(2,1)S(1)}, bf16[32,32,128]{2,1,0:T(8,128)(2,1)S(1)}, u32[]{:S(2)}, u32[]{:S(2)}) collective-permute-start(bf16[32,32,128]{2,1,0:T(8,128)(2,1)S(1)} %pad_maximum_fusion.mine_ref), channel_id=1, source_target_pairs={{0,8},{8,0},{16,24},{24,16},{32,40},{40,32},{48,56},{56,48},{1,9},... | collective-permute-start | bytes 786440 | tf_op jit(solution)/shard_map/ppermute | solution.py:336
  67.6 0.1 pad_add_fusion.place
  67.6 5.1 %all-to-all-done.1.near_ref = bf16[8,128,128]{2,1,0:T(8,128)(2,1)S(1)} async-done(((bf16[8,128,128]{2,1,0:T(8,128)(2,1)}), bf16[8,128,128]{2,1,0:T(8,128)(2,1)S(1)}, u32[]{:S(2)}, u32[]{:S(2)}) %all-to-all-start.1) | async-done | bytes 262176 | tf_op jit(solution)/shard_map/all_to_all | solution.py:328
  72.7 0.0 collective-permute-done.2.theirs_ref
  72.7 0.0 copy-start.2
  72.7 0.7 copy-done.2
  73.4 5.7 %statistics.1 = (f32[1024,1024]{1,0:T(8,128)S(1)}, f32[16,128]{1,0:T(8,128)S(1)}, f32[8,128]{1,0:T(8,128)S(1)}, bf16[64,4608]{1,0:T(8,128)(2,1)S(1)}) custom-call(s32[3]{0:T(128)S(1)} %pad_add_fusion.place, s32[64]{0:T(128)S(1)} %copy-done.2, bf16[8,128,128]{2,1,0:T(8,128)(2,1)S(1)} %all-to-all-done.1.near_ref, bf16[8,160,128]{2,1,0:T(8,128)(2,1)S(1)} %all_to_all.35.far_ref, ...), custom_call_target="tpu_custom_call" | custom-call | tf_op jit(solution)/shard_map/statistics/pallas_call | solution.py:157
  79.1 8.9 %all_to_all.36.parts_ref = f32[8,16,128]{2,1,0:T(8,128)S(1)} all-to-all(f32[8,16,128]{2,1,0:T(8,128)S(1)} %broadcast_in_dim.5), channel_id=1, replica_groups=mesh['far'=8,'near'=8,'head'=8] {'near'}, dimensions={0} | all-to-all | bytes 131072 | tf_op jit(solution)/shard_map/all_to_all | solution.py:328
  87.9 0.0 copy-start.1
  87.9 7.0 %gradients.1 = (bf16[8,160,128]{2,1,0:T(8,128)(2,1)S(1)}, bf16[8,64,128]{2,1,0:T(8,128)(2,1)}, f32[32,32,128]{2,1,0:T(8,128)S(1)}, bf16[32,32,128]{2,1,0:T(8,128)(2,1)S(1)}) custom-call(s32[3]{0:T(128)S(1)} %pad_add_fusion.place, bf16[8,128,128]{2,1,0:T(8,128)(2,1)S(1)} %all-to-all-done.1.near_ref, bf16[8,160,128]{2,1,0:T(8,128)(2,1)S(1)} %all_to_all.35.far_ref, ...), custom_call_target="tpu_custom_call" | custom-call | tf_op jit(solution)/shard_map/gradients/pallas_call | solution.py:284
  94.9 1.9 %collective-permute-start.3 = (bf16[32,32,128]{2,1,0:T(8,128)(2,1)S(1)}, bf16[32,32,128]{2,1,0:T(8,128)(2,1)S(1)}, u32[]{:S(2)}, u32[]{:S(2)}) collective-permute-start(bf16[32,32,128]{2,1,0:T(8,128)(2,1)S(1)} %get-tuple-element.34), channel_id=1, source_target_pairs={{0,8},{8,0},{16,24},{24,16},{32,40},{40,32},{48,56},{56,48},{1,9},... | collective-permute-start | bytes 786440 | tf_op jit(solution)/shard_map/ppermute | solution.py:336
  96.8 1.5 collective-permute-done.3
  98.3 0.1 convert_add_fusion
  98.4 3.2 %collective-permute-start.4 = (bf16[16,32,128]{2,1,0:T(8,128)(2,1)S(1)}, bf16[16,32,128]{2,1,0:T(8,128)(2,1)S(1)}, u32[]{:S(2)}, u32[]{:S(2)}) collective-permute-start(bf16[16,32,128]{2,1,0:T(8,128)(2,1)S(1)} %slice.67), channel_id=1, source_target_pairs={{0,16},{8,24},{16,0},{24,8},{32,48},{40,56},{48,32},{56,40},{1,17}... | collective-permute-start | bytes 393224 | tf_op jit(solution)/shard_map/ppermute | solution.py:336
  101.6 4.2 %collective-permute-done.4 = bf16[16,32,128]{2,1,0:T(8,128)(2,1)S(1)} collective-permute-done((bf16[16,32,128]{2,1,0:T(8,128)(2,1)S(1)}, bf16[16,32,128]{2,1,0:T(8,128)(2,1)S(1)}, u32[]{:S(2)}, u32[]{:S(2)}) %collective-permute-start.4) | collective-permute-done | bytes 131104 | tf_op jit(solution)/shard_map/ppermute | solution.py:336
  105.9 2.6 %collective-permute-start.5 = (bf16[8,32,128]{2,1,0:T(8,128)(2,1)S(1)}, bf16[8,32,128]{2,1,0:T(8,128)(2,1)S(1)}, u32[]{:S(2)}, u32[]{:S(2)}) collective-permute-start(bf16[8,32,128]{2,1,0:T(8,128)(2,1)S(1)} %slice.68), channel_id=1, source_target_pairs={{0,32},{8,40},{16,48},{24,56},{32,0},{40,8},{48,16},{56,24},{1,33}... | collective-permute-start | bytes 196616 | tf_op jit(solution)/shard_map/ppermute | solution.py:336
  108.5 5.0 %all-to-all-start.5 = ((bf16[8,64,128]{2,1,0:T(8,128)(2,1)}), bf16[8,64,128]{2,1,0:T(8,128)(2,1)S(1)}, u32[]{:S(2)}, u32[]{:S(2)}) async-start(bf16[8,64,128]{2,1,0:T(8,128)(2,1)} %get-tuple-element.35), calls=%async_computation.5 | async-start | bytes 262144 | tf_op jit(solution)/shard_map/all_to_all | solution.py:328
  113.5 0.0 collective-permute-done.5
  113.5 5.6 %all-to-all-done.5.near_ref = bf16[8,64,128]{2,1,0:T(8,128)(2,1)S(1)} async-done(((bf16[8,64,128]{2,1,0:T(8,128)(2,1)}), bf16[8,64,128]{2,1,0:T(8,128)(2,1)S(1)}, u32[]{:S(2)}, u32[]{:S(2)}) %all-to-all-start.5) | async-done | bytes 131104 | tf_op jit(solution)/shard_map/all_to_all | solution.py:328
  119.2 15.7 %all_to_all.37.far_ref = bf16[8,160,128]{2,1,0:T(8,128)(2,1)S(1)} all-to-all(bf16[8,160,128]{2,1,0:T(8,128)(2,1)S(1)} %fusion.1), channel_id=1, replica_groups=mesh['far'=8,'near'=8,'head'=8] {'far'}, dimensions={0} | all-to-all | bytes 655360 | tf_op jit(solution)/shard_map/all_to_all | solution.py:328
  134.9 0.0 copy-done.1
  134.9 1.0 unproject.1
  135.9 3.4 %all-to-all-start.6 = ((bf16[8,128,128]{2,1,0:T(8,128)(2,1)}), bf16[8,128,128]{2,1,0:T(8,128)(2,1)S(1)}, u32[]{:S(2)}, u32[]{:S(2)}) async-start(bf16[8,128,128]{2,1,0:T(8,128)(2,1)} %get-tuple-element.36), calls=%async_computation.6 | async-start | bytes 524288 | tf_op jit(solution)/shard_map/all_to_all | solution.py:328
  139.3 0.1 reshape.47
  139.4 0.7 copy.14
  140.1 12.1 %all-to-all-done.6 = bf16[8,128,128]{2,1,0:T(8,128)(2,1)S(1)} async-done(((bf16[8,128,128]{2,1,0:T(8,128)(2,1)}), bf16[8,128,128]{2,1,0:T(8,128)(2,1)S(1)}, u32[]{:S(2)}, u32[]{:S(2)}) %all-to-all-start.6) | async-done | bytes 262176 | tf_op jit(solution)/shard_map/all_to_all | solution.py:328
  152.2 0.7 reduce_sum.12
  (10 shorter events, 0.2 us)
Async XLA Ops:
  2.1 25.7 %all-to-all-start = ((bf16[8,128,128]{2,1,0:T(8,128)(2,1)}), bf16[8,128,128]{2,1,0:T(8,128)(2,1)S(1)}, u32[]{:S(2)}, u32[]{:S(2)}) async-start(bf16[8,128,128]{2,1,0:T(8,128)(2,1)} %broadcast_in_dim.4), calls=%async_computation | async-start | bytes 524288 | tf_op jit(solution)/shard_map/all_to_all | solution.py:328
  27.8 1.0 copy-start
  48.0 7.1 %collective-permute-start = (bf16[8,32,128]{2,1,0:T(8,128)(2,1)S(1)}, bf16[8,32,128]{2,1,0:T(8,128)(2,1)S(1)}, u32[]{:S(2)}, u32[]{:S(2)}) collective-permute-start(bf16[8,32,128]{2,1,0:T(8,128)(2,1)S(1)} %slice.54), channel_id=1, source_target_pairs={{0,32},{8,40},{16,48},{24,56},{32,0},{40,8},{48,16},{56,24},{1,33}... | collective-permute-start | bytes 196616 | tf_op jit(solution)/shard_map/ppermute | solution.py:336
  55.1 9.7 %collective-permute-start.1 = (bf16[16,32,128]{2,1,0:T(8,128)(2,1)S(1)}, bf16[16,32,128]{2,1,0:T(8,128)(2,1)S(1)}, u32[]{:S(2)}, u32[]{:S(2)}) collective-permute-start(bf16[16,32,128]{2,1,0:T(8,128)(2,1)S(1)} %pad_maximum_fusion.1), channel_id=1, source_target_pairs={{0,16},{8,24},{16,0},{24,8},{32,48},{40,56},{48,32},{56,40},{1,17}... | collective-permute-start | bytes 393224 | tf_op jit(solution)/shard_map/ppermute | solution.py:336
  59.1 13.6 %all-to-all-start.1 = ((bf16[8,128,128]{2,1,0:T(8,128)(2,1)}), bf16[8,128,128]{2,1,0:T(8,128)(2,1)S(1)}, u32[]{:S(2)}, u32[]{:S(2)}) async-start(bf16[8,128,128]{2,1,0:T(8,128)(2,1)} %get-tuple-element.26), calls=%async_computation.1 | async-start | bytes 524288 | tf_op jit(solution)/shard_map/all_to_all | solution.py:328
  64.8 7.9 %collective-permute-start.2 = (bf16[32,32,128]{2,1,0:T(8,128)(2,1)S(1)}, bf16[32,32,128]{2,1,0:T(8,128)(2,1)S(1)}, u32[]{:S(2)}, u32[]{:S(2)}) collective-permute-start(bf16[32,32,128]{2,1,0:T(8,128)(2,1)S(1)} %pad_maximum_fusion.mine_ref), channel_id=1, source_target_pairs={{0,8},{8,0},{16,24},{24,16},{32,40},{40,32},{48,56},{56,48},{1,9},... | collective-permute-start | bytes 786440 | tf_op jit(solution)/shard_map/ppermute | solution.py:336
  72.7 0.7 copy-start.2
  87.9 47.0 %copy-start.1 = (bf16[3,64,1024]{2,1,0:T(8,128)(2,1)S(1)}, bf16[3,64,1024]{2,1,0:T(8,128)(2,1)}, u32[]{:S(2)}) copy-start(bf16[3,64,1024]{2,1,0:T(8,128)(2,1)} %param.9) | copy-start | bytes 1179652
  94.9 3.4 %collective-permute-start.3 = (bf16[32,32,128]{2,1,0:T(8,128)(2,1)S(1)}, bf16[32,32,128]{2,1,0:T(8,128)(2,1)S(1)}, u32[]{:S(2)}, u32[]{:S(2)}) collective-permute-start(bf16[32,32,128]{2,1,0:T(8,128)(2,1)S(1)} %get-tuple-element.34), channel_id=1, source_target_pairs={{0,8},{8,0},{16,24},{24,16},{32,40},{40,32},{48,56},{56,48},{1,9},... | collective-permute-start | bytes 786440 | tf_op jit(solution)/shard_map/ppermute | solution.py:336
  98.4 7.4 %collective-permute-start.4 = (bf16[16,32,128]{2,1,0:T(8,128)(2,1)S(1)}, bf16[16,32,128]{2,1,0:T(8,128)(2,1)S(1)}, u32[]{:S(2)}, u32[]{:S(2)}) collective-permute-start(bf16[16,32,128]{2,1,0:T(8,128)(2,1)S(1)} %slice.67), channel_id=1, source_target_pairs={{0,16},{8,24},{16,0},{24,8},{32,48},{40,56},{48,32},{56,40},{1,17}... | collective-permute-start | bytes 393224 | tf_op jit(solution)/shard_map/ppermute | solution.py:336
  105.9 7.6 %collective-permute-start.5 = (bf16[8,32,128]{2,1,0:T(8,128)(2,1)S(1)}, bf16[8,32,128]{2,1,0:T(8,128)(2,1)S(1)}, u32[]{:S(2)}, u32[]{:S(2)}) collective-permute-start(bf16[8,32,128]{2,1,0:T(8,128)(2,1)S(1)} %slice.68), channel_id=1, source_target_pairs={{0,32},{8,40},{16,48},{24,56},{32,0},{40,8},{48,16},{56,24},{1,33}... | collective-permute-start | bytes 196616 | tf_op jit(solution)/shard_map/ppermute | solution.py:336
  108.5 10.7 %all-to-all-start.5 = ((bf16[8,64,128]{2,1,0:T(8,128)(2,1)}), bf16[8,64,128]{2,1,0:T(8,128)(2,1)S(1)}, u32[]{:S(2)}, u32[]{:S(2)}) async-start(bf16[8,64,128]{2,1,0:T(8,128)(2,1)} %get-tuple-element.35), calls=%async_computation.5 | async-start | bytes 262144 | tf_op jit(solution)/shard_map/all_to_all | solution.py:328
  135.9 16.3 %all-to-all-start.6 = ((bf16[8,128,128]{2,1,0:T(8,128)(2,1)}), bf16[8,128,128]{2,1,0:T(8,128)(2,1)S(1)}, u32[]{:S(2)}, u32[]{:S(2)}) async-start(bf16[8,128,128]{2,1,0:T(8,128)(2,1)} %get-tuple-element.36), calls=%async_computation.6 | async-start | bytes 524288 | tf_op jit(solution)/shard_map/all_to_all | solution.py:328

commit v4 on v3

--- a/solution.py
+++ b/solution.py
@@ -16,8 +16,9 @@
 WIDE = TABLE + 2 * PAD
 SCALE = E ** (-0.5)
 SPAN = 2
-STRIDES = (4, 2)
-SLOTS = 32
+HALF = B // 2
+SHARE = HALF + B
+CHUNK = E // 2
 ROWS = B + E // 2
 HIDDEN = -1e30
 BF = jnp.bfloat16
@@ -41,7 +42,8 @@
     scaled = (low[:, :E].astype(F32) * SCALE).astype(BF)
     paired = jnp.concatenate([scaled, grad_ref[...]], axis=1)
     for g in range(G):
-        near_ref[g] = paired
+        near_ref[g, :HALF] = paired[(g % 2) * HALF : (g % 2 + 1) * HALF]
+        near_ref[g, HALF:] = jnp.zeros((B, B), BF)
         far_ref[g, :B] = low[:, E:]
         far_ref[g, B:] = chunk_ref[...]
 
@@ -49,16 +51,13 @@
 def project(frames, weights, grad, chunk):
     return pl.pallas_call(
         project_kernel,
-        out_shape=(jax.ShapeDtypeStruct((G, B, B), BF), jax.ShapeDtypeStruct((G, ROWS, B), BF)),
+        out_shape=(
+            jax.ShapeDtypeStruct((G, SHARE, B), BF),
+            jax.ShapeDtypeStruct((G, ROWS, B), BF),
+        ),
         compiler_params=pltpu.CompilerParams(vmem_limit_bytes=LIMIT),
         name="project",
     )(frames, weights, grad, chunk)
-
-
-def slot_column(place, slot):
-    turn, y = slot // G, slot % G
-    block = 4 * y + jnp.bitwise_xor(place[1] // 2, (turn % 2) * 2 + turn // 2)
-    return pl.multiple_of(PAD + block * B, B)
 
 
 def near_tiles(place, u):
@@ -78,11 +77,11 @@
 def stats_kernel(
     place,
     valid,
-    near_ref,
-    far_ref,
     mine_ref,
     theirs_ref,
+    far_ref,
     weight_ref,
+    near_ref,
     stats_ref,
     tops_ref,
     table_ref,
@@ -92,15 +91,23 @@
     table_ref[:, :PAD] = jnp.zeros((E, PAD), BF)
     table_ref[:, WIDE - PAD :] = jnp.zeros((E, PAD), BF)
     first = place[1] % 2 == 0
-    for slot in range(SLOTS):
-        mine = mine_ref[slot].astype(F32)
-        theirs = theirs_ref[slot].astype(F32)
-        left = jnp.where(first, mine, theirs)
-        right = jnp.where(first, theirs, mine)
-        top = jnp.concatenate([left[:, :E], right[:, :E]], axis=1)
-        end = jnp.concatenate([left[:, E:], right[:, E:]], axis=1)
-        block = jnp.concatenate([top, end], axis=0)
-        table_ref[:, pl.ds(slot_column(place, slot), B)] = block.astype(BF)
+    for g in range(G):
+        mine = mine_ref[g, :HALF].astype(F32)
+        theirs = theirs_ref[g, :HALF].astype(F32)
+        near_ref[g, :HALF] = jnp.where(first, mine, theirs).astype(BF)
+        near_ref[g, HALF:] = jnp.where(first, theirs, mine).astype(BF)
+    for y in range(G):
+        rows = slice(HALF + CHUNK * (y % 4), HALF + CHUNK * (y % 4 + 1))
+        own = first if y < 4 else jnp.logical_not(first)
+        for k in range(4):
+            left, right = (
+                jnp.where(own, mine_ref[g, rows].astype(F32), theirs_ref[g, rows].astype(F32))
+                for g in (2 * k, 2 * k + 1)
+            )
+            top = jnp.concatenate([left[:, :E], right[:, :E]], axis=1)
+            end = jnp.concatenate([left[:, E:], right[:, E:]], axis=1)
+            at = PAD + (4 * y + k) * B
+            table_ref[:, at : at + B] = jnp.concatenate([top, end], axis=0).astype(BF)
     offsets = lax.broadcasted_iota(jnp.int32, (E, WIDE), 1) - (TABLE // 2 + PAD)
     rows = table_ref[...].astype(F32)
     upper = jnp.sum(jnp.where(offsets == clip, rows, 0.0), axis=1, keepdims=True)
@@ -153,13 +160,14 @@
 ARRAY = pl.BlockSpec(memory_space=pltpu.VMEM)
 
 
-def statistics(place, valid, near, far, mine, theirs):
+def statistics(place, valid, mine, theirs, far):
     return pl.pallas_call(
         stats_kernel,
-        in_specs=[SCALARS] * 2 + [ARRAY] * 4,
-        out_specs=[ARRAY] * 4,
+        in_specs=[SCALARS] * 2 + [ARRAY] * 3,
+        out_specs=[ARRAY] * 5,
         out_shape=(
             jax.ShapeDtypeStruct((N, N), F32),
+            jax.ShapeDtypeStruct((G, B, B), BF),
             jax.ShapeDtypeStruct((2 * G, B), F32),
             jax.ShapeDtypeStruct((G, B), F32),
             jax.ShapeDtypeStruct((E, WIDE), BF),
@@ -167,7 +175,7 @@
         scratch_shapes=[pltpu.VMEM((G, B, N + 2 * SPAN * B), F32)],
         compiler_params=pltpu.CompilerParams(vmem_limit_bytes=LIMIT),
         name="statistics",
-    )(place, valid, near, far, mine, theirs)
+    )(place, valid, mine, theirs, far)
 
 
 def grads_kernel(
@@ -250,7 +258,7 @@
     query_sum[place[1]] += add_band(place[1], place[0] + 2, 2 * G, flipped)
     for u in range(G):
         query_low = (query_sum[u] * SCALE).astype(BF)
-        near_out[u] = jnp.concatenate([query_low[:E], query_low[E:]], axis=1)
+        near_out[u, :HALF] = jnp.concatenate([query_low[:E], query_low[E:]], axis=1)
     both = jnp.concatenate(turned, axis=1)
     pairs = jnp.concatenate(
         [nn(both[:E], jnp.concatenate(lows, axis=0)), nn(both[E:], jnp.concatenate(probs, axis=0))],
@@ -266,18 +274,25 @@
     lower = lower + jnp.sum(tails[:, :B], axis=1, keepdims=True)
     table_sum[...] = jnp.where(offsets == clip, upper, jnp.where(offsets == -clip, lower, terms))
     first = place[1] % 2 == 0
-    for slot in range(SLOTS):
-        block = table_sum[:, pl.ds(slot_column(place, slot), B)]
-        at = lane[:E] + (slot_column(place, slot) - (TABLE // 2 + PAD))
-        block = jnp.where(jnp.abs(at) <= clip, block, 0.0)
-        top, end = block[: E // 2], block[E // 2 :]
-        left = jnp.concatenate([top[:, :E], end[:, :E]], axis=1)
-        right = jnp.concatenate([top[:, E:], end[:, E:]], axis=1)
-        keep_out[slot] = jnp.where(first, left, right)
-        send_out[slot] = jnp.where(first, right, left).astype(BF)
-    far_out[:, B:] = jnp.zeros((G, E // 2, B), BF)
+    for k in range(4):
+        pieces = []
+        for y in range(G):
+            at = PAD + (4 * y + k) * B
+            block = table_sum[:, at : at + B]
+            block = jnp.where(jnp.abs(lane[:E] + (at - TABLE // 2 - PAD)) <= clip, block, 0.0)
+            top, end = block[:CHUNK], block[CHUNK:]
+            left = jnp.concatenate([top[:, :E], end[:, :E]], axis=1)
+            right = jnp.concatenate([top[:, E:], end[:, E:]], axis=1)
+            pieces.append((left, right))
+        for y in range(4):
+            rows = slice(CHUNK * y, CHUNK * (y + 1))
+            for side in range(2):
+                early_half, late_half = pieces[y][side], pieces[y + 4][side]
+                keep_out[2 * k + side, rows] = jnp.where(first, early_half, late_half)
+                send_out[2 * k + side, rows] = jnp.where(first, late_half, early_half).astype(BF)
+    near_out[:, HALF:] = jnp.zeros((G, B, B), BF)
     for y in range(G):
-        far_out[y, :B] = pairs[:, y * B : (y + 1) * B].T.astype(BF)
+        far_out[y] = pairs[:, y * B : (y + 1) * B].T.astype(BF)
 
 
 def gradients(place, near, far, weight, tops, parts, table):
@@ -286,10 +301,10 @@
         in_specs=[SCALARS] + [ARRAY] * 6,
         out_specs=[ARRAY] * 4,
         out_shape=(
-            jax.ShapeDtypeStruct((G, ROWS, B), BF),
-            jax.ShapeDtypeStruct((G, E, B), BF),
-            jax.ShapeDtypeStruct((32, E // 2, B), F32),
-            jax.ShapeDtypeStruct((32, E // 2, B), BF),
+            jax.ShapeDtypeStruct((G, B, B), BF),
+            jax.ShapeDtypeStruct((G, SHARE, B), BF),
+            jax.ShapeDtypeStruct((G, B, B), F32),
+            jax.ShapeDtypeStruct((G, B, B), BF),
         ),
         scratch_shapes=[
             pltpu.VMEM((G, B, E), F32),
@@ -301,18 +316,37 @@
     )(place, near, far, weight, tops, parts, table)
 
 
-def unproject_kernel(far_ref, near_ref, weights_ref, out_ref, table_ref):
+def fold_kernel(near_ref, pairs_ref, query_ref, far_ref):
+    packed = jnp.sum(near_ref[:, :HALF].astype(F32), axis=0).astype(BF)
+    query_ref[...] = jnp.concatenate([packed[:, :E], packed[:, E:]], axis=0)
+    for side in range(2):
+        total = near_ref[side, HALF:].astype(F32)
+        for k in range(1, 4):
+            total = total + near_ref[2 * k + side, HALF:].astype(F32)
+        for y in range(4):
+            far_ref[4 * side + y, B:] = total[CHUNK * y : CHUNK * (y + 1)].astype(BF)
+    far_ref[:, :B] = pairs_ref[...]
+
+
+def fold(near, pairs):
+    return pl.pallas_call(
+        fold_kernel,
+        out_shape=(jax.ShapeDtypeStruct((B, E), BF), jax.ShapeDtypeStruct((G, ROWS, B), BF)),
+        compiler_params=pltpu.CompilerParams(vmem_limit_bytes=LIMIT),
+        name="fold",
+    )(near, pairs)
+
+
+def unproject_kernel(far_ref, query_ref, weights_ref, out_ref, table_ref):
     total = jnp.sum(far_ref[...].astype(F32), axis=0)
     pairs = total[:B].astype(BF)
     table_ref[...] = total[B:]
-    packed = jnp.sum(near_ref[...].astype(F32), axis=0).astype(BF)
-    query = jnp.concatenate([packed[:, :E], packed[:, E:]], axis=0)
-    terms = nn(query, weights_ref[:E]) + nn(pairs, weights_ref[E:])
+    terms = nn(query_ref[...], weights_ref[:E]) + nn(pairs, weights_ref[E:])
     for h in range(G):
         out_ref[h] = terms[:, h * B : (h + 1) * B].astype(BF)
 
 
-def unproject(far, near, weights):
+def unproject(far, query, weights):
     return pl.pallas_call(
         unproject_kernel,
         out_shape=(
@@ -321,7 +355,7 @@
         ),
         compiler_params=pltpu.CompilerParams(vmem_limit_bytes=LIMIT),
         name="unproject",
-    )(far, near, weights)
+    )(far, query, weights)
 
 
 def exchange(parts, axis):
@@ -332,8 +366,8 @@
     return jnp.broadcast_to(shard[None], (G,) + shard.shape)
 
 
-def across(shard, stride):
-    return lax.ppermute(shard, "near", [(i, i ^ stride) for i in range(G)])
+def other_core(shard):
+    return lax.ppermute(shard, "near", [(i, i ^ 1) for i in range(G)])
 
 
 def shards(frames, weights, offset_table, clip_range, valid_frames, context_grad):
@@ -344,21 +378,15 @@
     gathered = exchange(to_all(frames), "head")
     near, far = project(gathered, weight_rows, context_grad, chunk)
     far = exchange(far, "far")
-    mine = far[:, B:]
-    for stride in STRIDES:
-        mine = jnp.concatenate([mine, across(mine, stride)], axis=0)
-    theirs = across(mine, 1)
-    near = exchange(near, "near")
-    weight, stats, tops, table = statistics(place, valid_frames, near, far, mine, theirs)
+    chunks = jnp.broadcast_to(far[:, B:].reshape(1, 2, B, B), (4, 2, B, B)).reshape(G, B, B)
+    mine = exchange(near.at[:, HALF:].set(chunks), "near")
+    theirs = other_core(mine)
+    weight, near, stats, tops, table = statistics(place, valid_frames, mine, theirs, far)
     parts = exchange(to_all(stats), "near")
-    far, near, keep, send = gradients(place, near, far, weight, tops, parts, table)
-    total = keep + across(send, 1).astype(F32)
-    for stride in reversed(STRIDES):
-        half = total.shape[0] // 2
-        arrived = across(total[half:].astype(BF), stride)
-        total = total[:half] + arrived.astype(F32)
-    far = far.at[:, B:].set(total.astype(BF))
-    terms, table_part = unproject(exchange(far, "far"), exchange(near, "near"), weight_rows)
+    pairs, near, keep, send = gradients(place, near, far, weight, tops, parts, table)
+    halves = (keep + other_core(send).astype(F32)).astype(BF)
+    query, far = fold(exchange(near.at[:, HALF:].set(halves), "near"), pairs)
+    terms, table_part = unproject(exchange(far, "far"), query, weight_rows)
     table_grad = table_part.reshape(E // 2, 2, E).transpose(2, 1, 0).reshape(E, E)
     terms = exchange(terms, "head")
     input_grad = jnp.sum(terms.astype(F32), axis=0).astype(BF)

time: 154 us -> 142 us (0.922)
  blocking collectives: 42.7 us -> 73.5 us
  starting transfers between devices: 42 us -> 19.1 us
  waiting for transfers between devices: 45.4 us -> 27.2 us
    all_to_all x3 -> x5, blocking collectives: 42.7 us -> 73.5 us  [exchange(): return lax.all_to_all(parts, axis, 0, 0, tiled=True)]
    ppermute x6 -> x2, starting transfers between devices: 16.1 us -> 3.83 us  [other_core(): return lax.ppermute(shard, 'near', [(i, i ^ 1) for i in range(G)])]
    all_to_all x4 -> x2, starting transfers between devices: 25.9 us -> 15.3 us  [exchange(): return lax.all_to_all(parts, axis, 0, 0, tiled=True)]
    all_to_all x4 -> x2, waiting for transfers between devices: 34.9 us -> 24.7 us  [exchange(): return lax.all_to_all(parts, axis, 0, 0, tiled=True)]
    ppermute x6 -> x2, waiting for transfers between devices: 10.5 us -> 2.46 us  [other_core(): return lax.ppermute(shard, 'near', [(i, i ^ 1) for i in range(G)])]
    pallas_call x2 -> x3, Pallas kernels: 6.8 us -> 6.16 us  [the longest x1 5.61 us: statistics(): pl.pallas_call(stats_kernel, in_specs=[SCALARS] * 2 + [ARRAY] * 3, out_sp...]
  transfers between devices with their start and end apart: 10 -> 4, of which waited for: 7 -> 4; matrix products, arithmetic and copies ran while one was open for 2% -> 2% of each run, Pallas kernels for 0% -> 0%
where the time goes in v4:
time: 142 us; the launch traced here: 141 us
  blocking collectives  73.5 us (52%)
  waiting for transfers between devices  27.2 us (19%)
  starting transfers between devices  19.1 us (13%)
  Pallas kernels  13.6 us (10%)
  local copies, waits for them, and re-layouts  5.66 us (4%)
    all_to_all x5, blocking collectives, exchange(): return lax.all_to_all(parts, axis, 0, 0, tiled=True)  73.5 us
    all_to_all x2, waiting for transfers between devices, exchange(): return lax.all_to_all(parts, axis, 0, 0, tiled=True)  24.7 us
    all_to_all x2, starting transfers between devices, exchange(): return lax.all_to_all(parts, axis, 0, 0, tiled=True)  15.3 us
    pallas_call x1, Pallas kernels, gradients(): pl.pallas_call(grads_kernel, in_specs=[SCALARS] + [ARRAY] * 6, out_specs=...  6.47 us
    pallas_call x1, Pallas kernels, statistics(): pl.pallas_call(stats_kernel, in_specs=[SCALARS] * 2 + [ARRAY] * 3, out_sp...  5.61 us
    unnamed x9, local copies, waits for them, and re-layouts  3.99 us
    ppermute x2, starting transfers between devices, other_core(): return lax.ppermute(shard, 'near', [(i, i ^ 1) for i in range(G)])  3.83 us
  transfers between devices with their start and end apart: 4, of which 4 were waited for; matrix products, arithmetic and copies ran while one was open for 2% of the time, Pallas kernels for 0%

profile of v4, /device:TPU:64, one launch (start us, length us, event | category | flops | bytes accessed | tf_op | source)
XLA Modules:
  0.0 141.3 jit_solution(16010776424232655690)
XLA Ops:
  0.6 1.5 %broadcast_in_dim.8 = bf16[8,128,128]{2,1,0:T(8,128)(2,1)} broadcast(bf16[128,128]{1,0:T(8,128)(2,1)} %param.10), dimensions={1,2} | broadcast | bytes 294912 | tf_op jit(solution)/shard_map/broadcast_in_dim | solution.py:366
  2.1 11.8 %all-to-all-start = ((bf16[8,128,128]{2,1,0:T(8,128)(2,1)}), bf16[8,128,128]{2,1,0:T(8,128)(2,1)S(1)}, u32[]{:S(2)}, u32[]{:S(2)}) async-start(bf16[8,128,128]{2,1,0:T(8,128)(2,1)} %broadcast_in_dim.8), calls=%async_computation | async-start | bytes 524288 | tf_op jit(solution)/shard_map/all_to_all | solution.py:362
  14.0 0.8 copy.11
  14.8 0.8 copy.12.grad_ref
  15.6 0.1 pad_maximum_fusion.chunk_ref
  15.7 12.1 %all-to-all-done.frames_ref = bf16[8,128,128]{2,1,0:T(8,128)(2,1)S(1)} async-done(((bf16[8,128,128]{2,1,0:T(8,128)(2,1)}), bf16[8,128,128]{2,1,0:T(8,128)(2,1)S(1)}, u32[]{:S(2)}, u32[]{:S(2)}) %all-to-all-start) | async-done | bytes 262176 | tf_op jit(solution)/shard_map/all_to_all | solution.py:362
  27.8 0.0 copy-start
  27.8 1.0 copy-done
  28.8 0.5 project.1
  29.3 18.1 %all_to_all.35.far_ref = bf16[8,160,128]{2,1,0:T(8,128)(2,1)S(1)} all-to-all(bf16[8,160,128]{2,1,0:T(8,128)(2,1)S(1)} %get-tuple-element.42), channel_id=1, replica_groups=mesh['far'=8,'near'=8,'head'=8] {'far'}, dimensions={0} | all-to-all | bytes 655360 | tf_op jit(solution)/shard_map/all_to_all | solution.py:362
  47.5 16.4 %all_to_all.36.mine_ref = bf16[8,192,128]{2,1,0:T(8,128)(2,1)S(1)} all-to-all(bf16[8,192,128]{2,1,0:T(8,128)(2,1)S(1)} %constant_dynamic-update-slice_fusion), channel_id=1, replica_groups=mesh['far'=8,'near'=8,'head'=8] {'near'}, dimensions={0} | all-to-all | bytes 786432 | tf_op jit(solution)/shard_map/all_to_all | solution.py:362
  63.9 1.9 %collective-permute-start = (bf16[8,192,128]{2,1,0:T(8,128)(2,1)S(1)}, bf16[8,192,128]{2,1,0:T(8,128)(2,1)S(1)}, u32[]{:S(2)}, u32[]{:S(2)}) collective-permute-start(bf16[8,192,128]{2,1,0:T(8,128)(2,1)S(1)} %all_to_all.36.mine_ref), channel_id=1, source_target_pairs={{0,8},{8,0},{16,24},{24,16},{32,40},{40,32},{48,56},{56,48},{1,9},... | collective-permute-start | bytes 1179656 | tf_op jit(solution)/shard_map/ppermute | solution.py:370
  66.5 0.1 pad_add_fusion.place
  66.5 1.0 collective-permute-done.theirs_ref
  67.5 0.0 copy-start.2
  67.5 0.7 copy-done.2
  68.2 5.6 %statistics.1 = (f32[1024,1024]{1,0:T(8,128)S(1)}, bf16[8,128,128]{2,1,0:T(8,128)(2,1)S(1)}, f32[16,128]{1,0:T(8,128)S(1)}, f32[8,128]{1,0:T(8,128)S(1)}, bf16[64,4608]{1,0:T(8,128)(2,1)S(1)}) custom-call(s32[3]{0:T(128)S(1)} %pad_add_fusion.place, s32[64]{0:T(128)S(1)} %copy-done.2, bf16[8,192,128]{2,1,0:T(8,128)(2,1)S(1)} %all_to_all.36.mine_ref, ...), custom_call_target="tpu_custom_call" | custom-call | tf_op jit(solution)/shard_map/statistics/pallas_call | solution.py:164
  73.8 8.8 %all_to_all.37.parts_ref = f32[8,16,128]{2,1,0:T(8,128)S(1)} all-to-all(f32[8,16,128]{2,1,0:T(8,128)S(1)} %broadcast_in_dim.22), channel_id=1, replica_groups=mesh['far'=8,'near'=8,'head'=8] {'near'}, dimensions={0} | all-to-all | bytes 131072 | tf_op jit(solution)/shard_map/all_to_all | solution.py:362
  82.6 0.0 copy-start.1
  82.6 6.5 %gradients.1 = (bf16[8,128,128]{2,1,0:T(8,128)(2,1)S(1)}, bf16[8,192,128]{2,1,0:T(8,128)(2,1)S(1)}, f32[8,128,128]{2,1,0:T(8,128)S(1)}, bf16[8,128,128]{2,1,0:T(8,128)(2,1)S(1)}) custom-call(s32[3]{0:T(128)S(1)} %pad_add_fusion.place, bf16[8,128,128]{2,1,0:T(8,128)(2,1)S(1)} %get-tuple-element.43.near_ref, bf16[8,160,128]{2,1,0:T(8,128)(2,1)S(1)} %all_to_all.35.far_ref, ...), custom_call_target="tpu_custom_call" | custom-call | tf_op jit(solution)/shard_map/gradients/pallas_call | solution.py:299
  89.1 1.9 %collective-permute-start.1 = (bf16[8,128,128]{2,1,0:T(8,128)(2,1)S(1)}, bf16[8,128,128]{2,1,0:T(8,128)(2,1)S(1)}, u32[]{:S(2)}, u32[]{:S(2)}) collective-permute-start(bf16[8,128,128]{2,1,0:T(8,128)(2,1)S(1)} %get-tuple-element.50), channel_id=1, source_target_pairs={{0,8},{8,0},{16,24},{24,16},{32,40},{40,32},{48,56},{56,48},{1,9},... | collective-permute-start | bytes 786440 | tf_op jit(solution)/shard_map/ppermute | solution.py:370
  91.0 1.5 %collective-permute-done.1 = bf16[8,128,128]{2,1,0:T(8,128)(2,1)S(1)} collective-permute-done((bf16[8,128,128]{2,1,0:T(8,128)(2,1)S(1)}, bf16[8,128,128]{2,1,0:T(8,128)(2,1)S(1)}, u32[]{:S(2)}, u32[]{:S(2)}) %collective-permute-start.1) | collective-permute-done | bytes 262176 | tf_op jit(solution)/shard_map/ppermute | solution.py:370
  92.5 0.1 fusion
  92.6 14.4 %all_to_all.38.near_ref = bf16[8,192,128]{2,1,0:T(8,128)(2,1)S(1)} all-to-all(bf16[8,192,128]{2,1,0:T(8,128)(2,1)S(1)} %fusion), channel_id=1, replica_groups=mesh['far'=8,'near'=8,'head'=8] {'near'}, dimensions={0} | all-to-all | bytes 786432 | tf_op jit(solution)/shard_map/all_to_all | solution.py:362
  107.0 0.1 fold.1
  107.1 15.7 %all_to_all.39.far_ref = bf16[8,160,128]{2,1,0:T(8,128)(2,1)S(1)} all-to-all(bf16[8,160,128]{2,1,0:T(8,128)(2,1)S(1)} %get-tuple-element.52), channel_id=1, replica_groups=mesh['far'=8,'near'=8,'head'=8] {'far'}, dimensions={0} | all-to-all | bytes 655360 | tf_op jit(solution)/shard_map/all_to_all | solution.py:362
  122.8 0.0 copy-done.1
  122.8 1.0 unproject.1
  123.8 3.4 %all-to-all-start.6 = ((bf16[8,128,128]{2,1,0:T(8,128)(2,1)}), bf16[8,128,128]{2,1,0:T(8,128)(2,1)S(1)}, u32[]{:S(2)}, u32[]{:S(2)}) async-start(bf16[8,128,128]{2,1,0:T(8,128)(2,1)} %get-tuple-element.54), calls=%async_computation.6 | async-start | bytes 524288 | tf_op jit(solution)/shard_map/all_to_all | solution.py:362
  127.2 0.1 reshape.81
  127.3 0.7 copy.14
  128.0 12.6 %all-to-all-done.6 = bf16[8,128,128]{2,1,0:T(8,128)(2,1)S(1)} async-done(((bf16[8,128,128]{2,1,0:T(8,128)(2,1)}), bf16[8,128,128]{2,1,0:T(8,128)(2,1)S(1)}, u32[]{:S(2)}, u32[]{:S(2)}) %all-to-all-start.6) | async-done | bytes 262176 | tf_op jit(solution)/shard_map/all_to_all | solution.py:362
  140.6 0.7 reduce_sum.12
  (6 shorter events, 0.1 us)
Async XLA Ops:
  2.1 25.7 %all-to-all-start = ((bf16[8,128,128]{2,1,0:T(8,128)(2,1)}), bf16[8,128,128]{2,1,0:T(8,128)(2,1)S(1)}, u32[]{:S(2)}, u32[]{:S(2)}) async-start(bf16[8,128,128]{2,1,0:T(8,128)(2,1)} %broadcast_in_dim.8), calls=%async_computation | async-start | bytes 524288 | tf_op jit(solution)/shard_map/all_to_all | solution.py:362
  27.8 1.0 copy-start
  63.9 3.6 %collective-permute-start = (bf16[8,192,128]{2,1,0:T(8,128)(2,1)S(1)}, bf16[8,192,128]{2,1,0:T(8,128)(2,1)S(1)}, u32[]{:S(2)}, u32[]{:S(2)}) collective-permute-start(bf16[8,192,128]{2,1,0:T(8,128)(2,1)S(1)} %all_to_all.36.mine_ref), channel_id=1, source_target_pairs={{0,8},{8,0},{16,24},{24,16},{32,40},{40,32},{48,56},{56,48},{1,9},... | collective-permute-start | bytes 1179656 | tf_op jit(solution)/shard_map/ppermute | solution.py:370
  67.5 0.7 copy-start.2
  82.6 40.2 %copy-start.1 = (bf16[3,64,1024]{2,1,0:T(8,128)(2,1)S(1)}, bf16[3,64,1024]{2,1,0:T(8,128)(2,1)}, u32[]{:S(2)}) copy-start(bf16[3,64,1024]{2,1,0:T(8,128)(2,1)} %param.11) | copy-start | bytes 1179652
  89.1 3.4 %collective-permute-start.1 = (bf16[8,128,128]{2,1,0:T(8,128)(2,1)S(1)}, bf16[8,128,128]{2,1,0:T(8,128)(2,1)S(1)}, u32[]{:S(2)}, u32[]{:S(2)}) collective-permute-start(bf16[8,128,128]{2,1,0:T(8,128)(2,1)S(1)} %get-tuple-element.50), channel_id=1, source_target_pairs={{0,8},{8,0},{16,24},{24,16},{32,40},{40,32},{48,56},{56,48},{1,9},... | collective-permute-start | bytes 786440 | tf_op jit(solution)/shard_map/ppermute | solution.py:370
  123.8 16.8 %all-to-all-start.6 = ((bf16[8,128,128]{2,1,0:T(8,128)(2,1)}), bf16[8,128,128]{2,1,0:T(8,128)(2,1)S(1)}, u32[]{:S(2)}, u32[]{:S(2)}) async-start(bf16[8,128,128]{2,1,0:T(8,128)(2,1)} %get-tuple-element.54), calls=%async_computation.6 | async-start | bytes 524288 | tf_op jit(solution)/shard_map/all_to_all | solution.py:362

commit v5 on v4

--- a/solution.py
+++ b/solution.py
@@ -24,6 +24,8 @@
 BF = jnp.bfloat16
 F32 = jnp.float32
 LIMIT = 32 * 1024 * 1024
+SCALARS = pl.BlockSpec(memory_space=pltpu.SMEM)
+ARRAY = pl.BlockSpec(memory_space=pltpu.VMEM)
 
 
 def nt(a, b):
@@ -32,6 +34,46 @@
 
 def nn(a, b):
     return lax.dot_general(a, b, (((1,), (0,)), ((), ())), preferred_element_type=F32)
+
+
+def spread_kernel(frames_ref, out_ref, done):
+    copies = [pltpu.make_async_copy(frames_ref, out_ref.at[g], done.at[g]) for g in range(G)]
+    for copy in copies:
+        copy.start()
+    for copy in copies:
+        copy.wait()
+
+
+def spread(frames):
+    return pl.pallas_call(
+        spread_kernel,
+        in_specs=[pl.BlockSpec(memory_space=pl.ANY)],
+        out_specs=pl.BlockSpec(memory_space=pl.ANY),
+        out_shape=jax.ShapeDtypeStruct((G,) + frames.shape, frames.dtype),
+        scratch_shapes=[pltpu.SemaphoreType.DMA((G,))],
+        name="spread",
+    )(frames)
+
+
+def prepare_kernel(place, valid, weights_ref, copy_ref, live_ref):
+    copy_ref[...] = weights_ref[...]
+    lane = lax.broadcasted_iota(jnp.int32, (1, B), 1)
+    for v in range(G):
+        live_ref[v : v + 1, :] = jnp.where(lane < valid[G * v + place[1]], 1.0, 0.0)
+
+
+def prepare(place, valid, weights):
+    return pl.pallas_call(
+        prepare_kernel,
+        in_specs=[SCALARS] * 2 + [ARRAY],
+        out_specs=[ARRAY] * 2,
+        out_shape=(
+            jax.ShapeDtypeStruct(weights.shape, BF),
+            jax.ShapeDtypeStruct((G, B), F32),
+        ),
+        cost_estimate=pl.CostEstimate(flops=0, bytes_accessed=1 << 21, transcendentals=0),
+        name="prepare",
+    )(place, valid, weights)
 
 
 def project_kernel(frames_ref, weights_ref, grad_ref, chunk_ref, near_ref, far_ref):
@@ -76,16 +118,18 @@
 
 def stats_kernel(
     place,
-    valid,
+    live_ref,
     mine_ref,
     theirs_ref,
     far_ref,
     weight_ref,
+    slope_ref,
     near_ref,
     stats_ref,
     tops_ref,
     table_ref,
     shifts,
+    content_ref,
 ):
     clip = place[2]
     table_ref[:, :PAD] = jnp.zeros((E, PAD), BF)
@@ -133,22 +177,26 @@
             at = (v + SPAN) * B
             shifts[u, :, at : at + B] = jnp.where(v > place[0], edges[:, B:], edges[:, :B])
     put_band(place[1], place[0] + 2, 2 * G)
+    queries = near_ref[:, :, :E].reshape(N, E)
+    grads = near_ref[:, :, E:].reshape(N, E)
+    for at in range(0, N, 2 * B):
+        content_ref[:, at : at + 2 * B] = nt(queries, keys[at : at + 2 * B])
+        slope_ref[:, at : at + 2 * B] = nt(grads, values[at : at + 2 * B])
     for u in range(G):
-        content = nt(near_ref[u, :, :E], keys)
-        slope = nt(near_ref[u, :, E:], values)
+        rows = slice(u * B, (u + 1) * B)
         for v, apart in near_tiles(place, u):
             put_band(u, v, apart)
         pieces = []
         for v in range(G):
             at = (v + SPAN) * B
-            both = content[:, v * B : (v + 1) * B] + shifts[u, :, at : at + B]
-            pieces.append(jnp.where(lane < valid[G * v + place[1]], both, HIDDEN))
+            both = content_ref[rows, v * B : (v + 1) * B] + shifts[u, :, at : at + B]
+            pieces.append(jnp.where(live_ref[v : v + 1, :] > 0.0, both, HIDDEN))
         scores = jnp.concatenate(pieces, axis=1)
         top = jnp.max(scores, axis=1, keepdims=True)
         weight = jnp.exp(scores - top)
-        weight_ref[u * B : (u + 1) * B, :] = weight
+        weight_ref[rows, :] = weight
         amount = jnp.sum(weight, axis=1, keepdims=True)
-        mean = jnp.sum(weight * slope, axis=1, keepdims=True) / amount
+        mean = jnp.sum(weight * slope_ref[rows, :], axis=1, keepdims=True) / amount
         both = jnp.where(lane == 0, top + jnp.log(amount), jnp.where(lane == 1, mean, top))
         turned = both.T
         stats_ref[u : u + 1, :] = turned[0:1]
@@ -156,26 +204,23 @@
         tops_ref[u : u + 1, :] = turned[2:3]
 
 
-SCALARS = pl.BlockSpec(memory_space=pltpu.SMEM)
-ARRAY = pl.BlockSpec(memory_space=pltpu.VMEM)
-
-
-def statistics(place, valid, mine, theirs, far):
+def statistics(place, live, mine, theirs, far):
     return pl.pallas_call(
         stats_kernel,
-        in_specs=[SCALARS] * 2 + [ARRAY] * 3,
-        out_specs=[ARRAY] * 5,
+        in_specs=[SCALARS] + [ARRAY] * 4,
+        out_specs=[ARRAY] * 6,
         out_shape=(
+            jax.ShapeDtypeStruct((N, N), F32),
             jax.ShapeDtypeStruct((N, N), F32),
             jax.ShapeDtypeStruct((G, B, B), BF),
             jax.ShapeDtypeStruct((2 * G, B), F32),
             jax.ShapeDtypeStruct((G, B), F32),
             jax.ShapeDtypeStruct((E, WIDE), BF),
         ),
-        scratch_shapes=[pltpu.VMEM((G, B, N + 2 * SPAN * B), F32)],
+        scratch_shapes=[pltpu.VMEM((G, B, N + 2 * SPAN * B), F32), pltpu.VMEM((N, N), F32)],
         compiler_params=pltpu.CompilerParams(vmem_limit_bytes=LIMIT),
         name="statistics",
-    )(place, valid, mine, theirs, far)
+    )(place, live, mine, theirs, far)
 
 
 def grads_kernel(
@@ -183,6 +228,7 @@
     near_ref,
     far_ref,
     weight_ref,
+    slope_ref,
     tops_ref,
     parts_ref,
     table_ref,
@@ -193,6 +239,9 @@
     query_sum,
     table_sum,
     held,
+    lows,
+    probs,
+    outers,
 ):
     clip = place[2]
     parts = parts_ref[...]
@@ -207,15 +256,13 @@
     held[:, :, SPAN * B + N :] = jnp.zeros((G, B, SPAN * B), F32)
 
     keys = far_ref[:, :B, :E].reshape(N, E)
-    values = far_ref[:, :B, E:].reshape(N, E)
     low_end, high_end = table_ref[:, :B], table_ref[:, WIDE - B :]
     ends = jnp.concatenate([low_end, high_end, low_end, high_end], axis=1)
     row = lax.broadcasted_iota(jnp.int32, (B, B), 0)
     lane = lax.broadcasted_iota(jnp.int32, (B, B), 1)
     turn = (lane + row) % B
     early = lane + row < B
-    lows, probs, turned = [], [], []
-    end_sum = jnp.zeros((E, 4 * B), F32)
+    turned = []
 
     def add_band(u, v, apart, flipped):
         spun = jnp.take_along_axis(held[u, :, block_at(v)], turn, axis=1)
@@ -231,9 +278,11 @@
         turned.append(flipped)
         factor = columns[:, u : u + 1]
         mean = columns[:, G + u : G + u + 1]
-        slope = nt(paired[:, E:], values)
-        prob = weight_ref[u * B : (u + 1) * B, :] * factor
-        low = (prob * (slope - mean)).astype(BF)
+        rows = slice(u * B, (u + 1) * B)
+        prob = weight_ref[rows, :] * factor
+        low = (prob * (slope_ref[rows, :] - mean)).astype(BF)
+        lows[rows, :] = low
+        probs[rows, :] = prob.astype(BF)
         wide = low.astype(F32)
         held[u, :, SPAN * B : SPAN * B + N] = wide
         lower = jnp.zeros((B, B), F32)
@@ -246,27 +295,19 @@
         outer = jnp.concatenate([lower, upper], axis=1)
         coarse = outer.astype(BF)
         fine = (outer - coarse.astype(F32)).astype(BF)
-        outer = jnp.concatenate([coarse, fine], axis=1)
-        end_sum = end_sum + nn(flipped[:E], outer)
-        query_grad = nn(low, keys) + nt(outer, ends)
-        for v, apart in near_tiles(place, u):
-            query_grad = query_grad + add_band(u, v, apart, flipped)
-        query_sum[u] = query_grad
-        lows.append(low)
-        probs.append(prob.astype(BF))
+        outers[rows, :] = jnp.concatenate([coarse, fine], axis=1)
+        query_sum[u] = sum(add_band(u, v, apart, flipped) for v, apart in near_tiles(place, u))
     flipped = near_ref[place[1]].astype(F32).T.astype(BF)
     query_sum[place[1]] += add_band(place[1], place[0] + 2, 2 * G, flipped)
+    both = jnp.concatenate(turned, axis=1)
+    main = nn(lows[...], keys) + nt(outers[...], ends)
+    tails = nn(both[:E], outers[...])
     for u in range(G):
-        query_low = (query_sum[u] * SCALE).astype(BF)
+        query_low = ((query_sum[u] + main[u * B : (u + 1) * B]) * SCALE).astype(BF)
         near_out[u, :HALF] = jnp.concatenate([query_low[:E], query_low[E:]], axis=1)
-    both = jnp.concatenate(turned, axis=1)
-    pairs = jnp.concatenate(
-        [nn(both[:E], jnp.concatenate(lows, axis=0)), nn(both[E:], jnp.concatenate(probs, axis=0))],
-        axis=0,
-    )
+    pairs = jnp.concatenate([nn(both[:E], lows[...]), nn(both[E:], probs[...])], axis=0)
     offsets = lax.broadcasted_iota(jnp.int32, (E, WIDE), 1) - (TABLE // 2 + PAD)
     terms = table_sum[...]
-    tails = end_sum
     tails = tails[:, : 2 * B] + tails[:, 2 * B :]
     upper = jnp.sum(jnp.where(offsets >= clip, terms, 0.0), axis=1, keepdims=True)
     lower = jnp.sum(jnp.where(offsets <= -clip, terms, 0.0), axis=1, keepdims=True)
@@ -295,10 +336,10 @@
         far_out[y] = pairs[:, y * B : (y + 1) * B].T.astype(BF)
 
 
-def gradients(place, near, far, weight, tops, parts, table):
+def gradients(place, near, far, weight, slope, tops, parts, table):
     return pl.pallas_call(
         grads_kernel,
-        in_specs=[SCALARS] + [ARRAY] * 6,
+        in_specs=[SCALARS] + [ARRAY] * 7,
         out_specs=[ARRAY] * 4,
         out_shape=(
             jax.ShapeDtypeStruct((G, B, B), BF),
@@ -310,10 +351,13 @@
             pltpu.VMEM((G, B, E), F32),
             pltpu.VMEM((E, WIDE), F32),
             pltpu.VMEM((G, B, N + 2 * SPAN * B), F32),
+            pltpu.VMEM((N, N), BF),
+            pltpu.VMEM((N, N), BF),
+            pltpu.VMEM((N, 4 * B), BF),
         ],
         compiler_params=pltpu.CompilerParams(vmem_limit_bytes=LIMIT),
         name="gradients",
-    )(place, near, far, weight, tops, parts, table)
+    )(place, near, far, weight, slope, tops, parts, table)
 
 
 def fold_kernel(near_ref, pairs_ref, query_ref, far_ref):
@@ -375,15 +419,18 @@
     place = jnp.stack([lax.axis_index("far"), lax.axis_index("near"), clip_range[0]])
     turned = offset_table.T
     chunk = jnp.concatenate([turned[: E // 2], turned[E // 2 :]], axis=1)
-    gathered = exchange(to_all(frames), "head")
-    near, far = project(gathered, weight_rows, context_grad, chunk)
+    early_weights, live = prepare(place, valid_frames, weight_rows)
+    gathered = exchange(spread(frames), "head")
+    near, far = project(gathered, early_weights, context_grad, chunk)
     far = exchange(far, "far")
     chunks = jnp.broadcast_to(far[:, B:].reshape(1, 2, B, B), (4, 2, B, B)).reshape(G, B, B)
     mine = exchange(near.at[:, HALF:].set(chunks), "near")
     theirs = other_core(mine)
-    weight, near, stats, tops, table = statistics(place, valid_frames, mine, theirs, far)
+    weight, slope, near, stats, tops, table = statistics(place, live, mine, theirs, far)
     parts = exchange(to_all(stats), "near")
-    pairs, near, keep, send = gradients(place, near, far, weight, tops, parts, table)
+    pairs, near, keep, send = gradients(
+        place, near, far, weight, slope, tops, parts, table
+    )
     halves = (keep + other_core(send).astype(F32)).astype(BF)
     query, far = fold(exchange(near.at[:, HALF:].set(halves), "near"), pairs)
     terms, table_part = unproject(exchange(far, "far"), query, weight_rows)

time: 142 us -> 149 us (1.049)
  Pallas kernels: 13.6 us -> 23.5 us
  waiting for transfers between devices: 27.2 us -> 24.8 us
    pallas_call x2 -> x4, Pallas kernels: 12.1 us -> 22 us  [the longest x1 9.11 us: spread(): pl.pallas_call(spread_kernel, in_specs=[pl.BlockSpec(memory_space=pl.ANY)...]
    all_to_all x2, waiting for transfers between devices: 24.7 us -> 21.6 us  [exchange(): return lax.all_to_all(parts, axis, 0, 0, tiled=True)]
    broadcast_in_dim x2 -> x1, local copies, waits for them, and re-layouts: 1.5 us -> 0.01 us  [to_all(): return jnp.broadcast_to(shard[None], (G,) + shard.shape)]
    unnamed x9 -> x11, local copies, waits for them, and re-layouts: 3.99 us -> 4.68 us
  transfers between devices with their start and end apart: 4 -> 4, of which waited for: 4 -> 4; matrix products, arithmetic and copies ran while one was open for 2% -> 2% of each run, Pallas kernels for 0% -> 1%
where the time goes in v5:
time: 149 us
  blocking collectives  73.5 us (49%)
  waiting for transfers between devices  24.8 us (17%)
  Pallas kernels  23.5 us (16%)
  starting transfers between devices  19.1 us (13%)
  local copies, waits for them, and re-layouts  4.86 us (3%)
    all_to_all x5, blocking collectives, exchange(): return lax.all_to_all(parts, axis, 0, 0, tiled=True)  73.5 us
    all_to_all x2, waiting for transfers between devices, exchange(): return lax.all_to_all(parts, axis, 0, 0, tiled=True)  21.6 us
    all_to_all x2, starting transfers between devices, exchange(): return lax.all_to_all(parts, axis, 0, 0, tiled=True)  15.3 us
    pallas_call x1, Pallas kernels, spread(): pl.pallas_call(spread_kernel, in_specs=[pl.BlockSpec(memory_space=pl.ANY)...  9.11 us
    pallas_call x1, Pallas kernels, gradients(): pl.pallas_call(grads_kernel, in_specs=[SCALARS] + [ARRAY] * 7, out_specs=...  5.55 us
    pallas_call x1, Pallas kernels, statistics(): pl.pallas_call(stats_kernel, in_specs=[SCALARS] + [ARRAY] * 4, out_specs=...  5.54 us
    unnamed x11, local copies, waits for them, and re-layouts  4.68 us
    ppermute x2, starting transfers between devices, other_core(): return lax.ppermute(shard, 'near', [(i, i ^ 1) for i in range(G)])  3.83 us
  transfers between devices with their start and end apart: 4, of which 4 were waited for; matrix products, arithmetic and copies ran while one was open for 2% of the time, Pallas kernels for 1%

profile of v5, /device:TPU:64, one launch (start us, length us, event | category | flops | bytes accessed | tf_op | source)
XLA Modules:
  0.0 148.6 jit_solution(14701280492749243663)
XLA Ops:
  0.6 9.1 %spread.1 = bf16[8,128,128]{2,1,0:T(8,128)(2,1)} custom-call(bf16[128,128]{1,0:T(8,128)(2,1)} %frames_ref.1), custom_call_target="tpu_custom_call" | custom-call | tf_op jit(solution)/shard_map/spread/pallas_call | solution.py:48
  9.7 11.9 %all-to-all-start = ((bf16[8,128,128]{2,1,0:T(8,128)(2,1)}), bf16[8,128,128]{2,1,0:T(8,128)(2,1)S(1)}, u32[]{:S(2)}, u32[]{:S(2)}) async-start(bf16[8,128,128]{2,1,0:T(8,128)(2,1)} %spread.1), calls=%async_computation | async-start | bytes 524288 | tf_op jit(solution)/shard_map/all_to_all | solution.py:406
  22.3 0.8 copy.11
  23.1 0.8 copy.12.grad_ref
  23.9 0.7 pad_add_fusion.place
  24.6 1.8 %prepare.1 = (bf16[192,1024]{1,0:T(8,128)(2,1)}, f32[8,128]{1,0:T(8,128)}) custom-call(s32[3]{0:T(128)} %pad_add_fusion.place, s32[64]{0:T(128)} %valid.1, bf16[192,1024]{1,0:T(8,128)(2,1)} %bitcast.9), custom_call_target="tpu_custom_call" | custom-call | bytes 2097152 | tf_op jit(solution)/shard_map/prepare/pallas_call | solution.py:66
  26.3 0.1 pad_maximum_fusion.chunk_ref
  26.4 9.0 %all-to-all-done.frames_ref = bf16[8,128,128]{2,1,0:T(8,128)(2,1)S(1)} async-done(((bf16[8,128,128]{2,1,0:T(8,128)(2,1)}), bf16[8,128,128]{2,1,0:T(8,128)(2,1)S(1)}, u32[]{:S(2)}, u32[]{:S(2)}) %all-to-all-start) | async-done | bytes 262176 | tf_op jit(solution)/shard_map/all_to_all | solution.py:406
  35.5 0.0 copy-start.1
  35.5 1.0 copy-done.1
  36.5 0.5 project.1
  36.9 18.1 %all_to_all.35.far_ref = bf16[8,160,128]{2,1,0:T(8,128)(2,1)S(1)} all-to-all(bf16[8,160,128]{2,1,0:T(8,128)(2,1)S(1)} %get-tuple-element.47), channel_id=1, replica_groups=mesh['far'=8,'near'=8,'head'=8] {'far'}, dimensions={0} | all-to-all | bytes 655360 | tf_op jit(solution)/shard_map/all_to_all | solution.py:406
  55.1 16.5 %all_to_all.36.mine_ref = bf16[8,192,128]{2,1,0:T(8,128)(2,1)S(1)} all-to-all(bf16[8,192,128]{2,1,0:T(8,128)(2,1)S(1)} %constant_dynamic-update-slice_fusion), channel_id=1, replica_groups=mesh['far'=8,'near'=8,'head'=8] {'near'}, dimensions={0} | all-to-all | bytes 786432 | tf_op jit(solution)/shard_map/all_to_all | solution.py:406
  71.5 1.9 %collective-permute-start = (bf16[8,192,128]{2,1,0:T(8,128)(2,1)S(1)}, bf16[8,192,128]{2,1,0:T(8,128)(2,1)S(1)}, u32[]{:S(2)}, u32[]{:S(2)}) collective-permute-start(bf16[8,192,128]{2,1,0:T(8,128)(2,1)S(1)} %all_to_all.36.mine_ref), channel_id=1, source_target_pairs={{0,8},{8,0},{16,24},{24,16},{32,40},{40,32},{48,56},{56,48},{1,9},... | collective-permute-start | bytes 1179656 | tf_op jit(solution)/shard_map/ppermute | solution.py:414
  73.5 1.7 %collective-permute-done.theirs_ref = bf16[8,192,128]{2,1,0:T(8,128)(2,1)S(1)} collective-permute-done((bf16[8,192,128]{2,1,0:T(8,128)(2,1)S(1)}, bf16[8,192,128]{2,1,0:T(8,128)(2,1)S(1)}, u32[]{:S(2)}, u32[]{:S(2)}) %collective-permute-start) | collective-permute-done | bytes 393248 | tf_op jit(solution)/shard_map/ppermute | solution.py:414
  75.2 0.0 copy-start.2
  75.2 0.7 copy-done.2
  75.8 0.0 copy-start.3
  75.8 0.7 copy-done.3
  76.5 5.5 %statistics.1 = (f32[1024,1024]{1,0:T(8,128)S(1)}, f32[1024,1024]{1,0:T(8,128)S(1)}, bf16[8,128,128]{2,1,0:T(8,128)(2,1)S(1)}, f32[16,128]{1,0:T(8,128)S(1)}, f3...) custom-call(s32[3]{0:T(128)S(1)} %copy-done.2, f32[8,128]{1,0:T(8,128)S(1)} %copy-done.3, ...), custom_call_target="tpu_custom_call" | custom-call | tf_op jit(solution)/shard_map/statistics/pallas_call | solution.py:208
  82.1 8.8 %all_to_all.37.parts_ref = f32[8,16,128]{2,1,0:T(8,128)S(1)} all-to-all(f32[8,16,128]{2,1,0:T(8,128)S(1)} %broadcast_in_dim.15), channel_id=1, replica_groups=mesh['far'=8,'near'=8,'head'=8] {'near'}, dimensions={0} | all-to-all | bytes 131072 | tf_op jit(solution)/shard_map/all_to_all | solution.py:406
  90.9 0.0 copy-start
  90.9 5.6 %gradients.1 = (bf16[8,128,128]{2,1,0:T(8,128)(2,1)S(1)}, bf16[8,192,128]{2,1,0:T(8,128)(2,1)S(1)}, f32[8,128,128]{2,1,0:T(8,128)S(1)}, bf16[8,128,128]{2,1,0:T(8,128)(2,1)S(1)}) custom-call(s32[3]{0:T(128)S(1)} %copy-done.2, bf16[8,128,128]{2,1,0:T(8,128)(2,1)S(1)} %get-tuple-element.48.near_ref, bf16[8,160,128]{2,1,0:T(8,128)(2,1)S(1)} %all_to_all.35.far_ref, ...), custom_call_target="tpu_custom_call" | custom-call | tf_op jit(solution)/shard_map/gradients/pallas_call | solution.py:340
  96.4 1.9 %collective-permute-start.1 = (bf16[8,128,128]{2,1,0:T(8,128)(2,1)S(1)}, bf16[8,128,128]{2,1,0:T(8,128)(2,1)S(1)}, u32[]{:S(2)}, u32[]{:S(2)}) collective-permute-start(bf16[8,128,128]{2,1,0:T(8,128)(2,1)S(1)} %get-tuple-element.56), channel_id=1, source_target_pairs={{0,8},{8,0},{16,24},{24,16},{32,40},{40,32},{48,56},{56,48},{1,9},... | collective-permute-start | bytes 786440 | tf_op jit(solution)/shard_map/ppermute | solution.py:414
  98.3 1.5 %collective-permute-done.1 = bf16[8,128,128]{2,1,0:T(8,128)(2,1)S(1)} collective-permute-done((bf16[8,128,128]{2,1,0:T(8,128)(2,1)S(1)}, bf16[8,128,128]{2,1,0:T(8,128)(2,1)S(1)}, u32[]{:S(2)}, u32[]{:S(2)}) %collective-permute-start.1) | collective-permute-done | bytes 262176 | tf_op jit(solution)/shard_map/ppermute | solution.py:414
  99.9 0.1 fusion
  99.9 14.4 %all_to_all.38.near_ref = bf16[8,192,128]{2,1,0:T(8,128)(2,1)S(1)} all-to-all(bf16[8,192,128]{2,1,0:T(8,128)(2,1)S(1)} %fusion), channel_id=1, replica_groups=mesh['far'=8,'near'=8,'head'=8] {'near'}, dimensions={0} | all-to-all | bytes 786432 | tf_op jit(solution)/shard_map/all_to_all | solution.py:406
  114.4 0.1 fold.1
  114.5 15.7 %all_to_all.39.far_ref = bf16[8,160,128]{2,1,0:T(8,128)(2,1)S(1)} all-to-all(bf16[8,160,128]{2,1,0:T(8,128)(2,1)S(1)} %get-tuple-element.58), channel_id=1, replica_groups=mesh['far'=8,'near'=8,'head'=8] {'far'}, dimensions={0} | all-to-all | bytes 655360 | tf_op jit(solution)/shard_map/all_to_all | solution.py:406
  130.2 0.0 copy-done
  130.2 1.0 unproject.1
  131.2 3.4 %all-to-all-start.6 = ((bf16[8,128,128]{2,1,0:T(8,128)(2,1)}), bf16[8,128,128]{2,1,0:T(8,128)(2,1)S(1)}, u32[]{:S(2)}, u32[]{:S(2)}) async-start(bf16[8,128,128]{2,1,0:T(8,128)(2,1)} %get-tuple-element.60), calls=%async_computation.6 | async-start | bytes 524288 | tf_op jit(solution)/shard_map/all_to_all | solution.py:406
  134.6 0.1 reshape.80
  134.7 0.7 copy.14
  135.4 12.6 %all-to-all-done.6 = bf16[8,128,128]{2,1,0:T(8,128)(2,1)S(1)} async-done(((bf16[8,128,128]{2,1,0:T(8,128)(2,1)}), bf16[8,128,128]{2,1,0:T(8,128)(2,1)S(1)}, u32[]{:S(2)}, u32[]{:S(2)}) %all-to-all-start.6) | async-done | bytes 262176 | tf_op jit(solution)/shard_map/all_to_all | solution.py:406
  148.0 0.7 reduce_sum.12
  (6 shorter events, 0.1 us)
Async XLA Ops:
  9.7 25.7 %all-to-all-start = ((bf16[8,128,128]{2,1,0:T(8,128)(2,1)}), bf16[8,128,128]{2,1,0:T(8,128)(2,1)S(1)}, u32[]{:S(2)}, u32[]{:S(2)}) async-start(bf16[8,128,128]{2,1,0:T(8,128)(2,1)} %spread.1), calls=%async_computation | async-start | bytes 524288 | tf_op jit(solution)/shard_map/all_to_all | solution.py:406
  35.5 1.0 copy-start.1
  71.5 3.6 %collective-permute-start = (bf16[8,192,128]{2,1,0:T(8,128)(2,1)S(1)}, bf16[8,192,128]{2,1,0:T(8,128)(2,1)S(1)}, u32[]{:S(2)}, u32[]{:S(2)}) collective-permute-start(bf16[8,192,128]{2,1,0:T(8,128)(2,1)S(1)} %all_to_all.36.mine_ref), channel_id=1, source_target_pairs={{0,8},{8,0},{16,24},{24,16},{32,40},{40,32},{48,56},{56,48},{1,9},... | collective-permute-start | bytes 1179656 | tf_op jit(solution)/shard_map/ppermute | solution.py:414
  75.2 0.7 copy-start.2
  75.8 0.7 copy-start.3
  90.9 39.3 %copy-start = (bf16[3,64,1024]{2,1,0:T(8,128)(2,1)S(1)}, bf16[3,64,1024]{2,1,0:T(8,128)(2,1)}, u32[]{:S(2)}) copy-start(bf16[3,64,1024]{2,1,0:T(8,128)(2,1)} %param.11) | copy-start | bytes 1179652
  96.4 3.4 %collective-permute-start.1 = (bf16[8,128,128]{2,1,0:T(8,128)(2,1)S(1)}, bf16[8,128,128]{2,1,0:T(8,128)(2,1)S(1)}, u32[]{:S(2)}, u32[]{:S(2)}) collective-permute-start(bf16[8,128,128]{2,1,0:T(8,128)(2,1)S(1)} %get-tuple-element.56), channel_id=1, source_target_pairs={{0,8},{8,0},{16,24},{24,16},{32,40},{40,32},{48,56},{56,48},{1,9},... | collective-permute-start | bytes 786440 | tf_op jit(solution)/shard_map/ppermute | solution.py:414
  131.2 16.8 %all-to-all-start.6 = ((bf16[8,128,128]{2,1,0:T(8,128)(2,1)}), bf16[8,128,128]{2,1,0:T(8,128)(2,1)S(1)}, u32[]{:S(2)}, u32[]{:S(2)}) async-start(bf16[8,128,128]{2,1,0:T(8,128)(2,1)} %get-tuple-element.60), calls=%async_computation.6 | async-start | bytes 524288 | tf_op jit(solution)/shard_map/all_to_all | solution.py:406

commit v6 on v5

--- a/solution.py
+++ b/solution.py
@@ -36,46 +36,6 @@
     return lax.dot_general(a, b, (((1,), (0,)), ((), ())), preferred_element_type=F32)
 
 
-def spread_kernel(frames_ref, out_ref, done):
-    copies = [pltpu.make_async_copy(frames_ref, out_ref.at[g], done.at[g]) for g in range(G)]
-    for copy in copies:
-        copy.start()
-    for copy in copies:
-        copy.wait()
-
-
-def spread(frames):
-    return pl.pallas_call(
-        spread_kernel,
-        in_specs=[pl.BlockSpec(memory_space=pl.ANY)],
-        out_specs=pl.BlockSpec(memory_space=pl.ANY),
-        out_shape=jax.ShapeDtypeStruct((G,) + frames.shape, frames.dtype),
-        scratch_shapes=[pltpu.SemaphoreType.DMA((G,))],
-        name="spread",
-    )(frames)
-
-
-def prepare_kernel(place, valid, weights_ref, copy_ref, live_ref):
-    copy_ref[...] = weights_ref[...]
-    lane = lax.broadcasted_iota(jnp.int32, (1, B), 1)
-    for v in range(G):
-        live_ref[v : v + 1, :] = jnp.where(lane < valid[G * v + place[1]], 1.0, 0.0)
-
-
-def prepare(place, valid, weights):
-    return pl.pallas_call(
-        prepare_kernel,
-        in_specs=[SCALARS] * 2 + [ARRAY],
-        out_specs=[ARRAY] * 2,
-        out_shape=(
-            jax.ShapeDtypeStruct(weights.shape, BF),
-            jax.ShapeDtypeStruct((G, B), F32),
-        ),
-        cost_estimate=pl.CostEstimate(flops=0, bytes_accessed=1 << 21, transcendentals=0),
-        name="prepare",
-    )(place, valid, weights)
-
-
 def project_kernel(frames_ref, weights_ref, grad_ref, chunk_ref, near_ref, far_ref):
     total = jnp.zeros((B, 3 * E), F32)
     for h in range(G):
@@ -118,7 +78,6 @@
 
 def stats_kernel(
     place,
-    live_ref,
     mine_ref,
     theirs_ref,
     far_ref,
@@ -190,7 +149,7 @@
         for v in range(G):
             at = (v + SPAN) * B
             both = content_ref[rows, v * B : (v + 1) * B] + shifts[u, :, at : at + B]
-            pieces.append(jnp.where(live_ref[v : v + 1, :] > 0.0, both, HIDDEN))
+            pieces.append(jnp.where(lane < place[3 + G * v + place[1]], both, HIDDEN))
         scores = jnp.concatenate(pieces, axis=1)
         top = jnp.max(scores, axis=1, keepdims=True)
         weight = jnp.exp(scores - top)
@@ -204,10 +163,10 @@
         tops_ref[u : u + 1, :] = turned[2:3]
 
 
-def statistics(place, live, mine, theirs, far):
+def statistics(place, mine, theirs, far):
     return pl.pallas_call(
         stats_kernel,
-        in_specs=[SCALARS] + [ARRAY] * 4,
+        in_specs=[SCALARS] + [ARRAY] * 3,
         out_specs=[ARRAY] * 6,
         out_shape=(
             jax.ShapeDtypeStruct((N, N), F32),
@@ -220,7 +179,7 @@
         scratch_shapes=[pltpu.VMEM((G, B, N + 2 * SPAN * B), F32), pltpu.VMEM((N, N), F32)],
         compiler_params=pltpu.CompilerParams(vmem_limit_bytes=LIMIT),
         name="statistics",
-    )(place, live, mine, theirs, far)
+    )(place, mine, theirs, far)
 
 
 def grads_kernel(
@@ -416,17 +375,17 @@
 
 def shards(frames, weights, offset_table, clip_range, valid_frames, context_grad):
     weight_rows = weights.reshape(3 * E, G * B)
-    place = jnp.stack([lax.axis_index("far"), lax.axis_index("near"), clip_range[0]])
+    own = jnp.stack([lax.axis_index("far"), lax.axis_index("near"), clip_range[0]])
+    place = jnp.concatenate([own, valid_frames])
     turned = offset_table.T
     chunk = jnp.concatenate([turned[: E // 2], turned[E // 2 :]], axis=1)
-    early_weights, live = prepare(place, valid_frames, weight_rows)
-    gathered = exchange(spread(frames), "head")
-    near, far = project(gathered, early_weights, context_grad, chunk)
+    gathered = exchange(to_all(frames), "head")
+    near, far = project(gathered, weight_rows, context_grad, chunk)
     far = exchange(far, "far")
     chunks = jnp.broadcast_to(far[:, B:].reshape(1, 2, B, B), (4, 2, B, B)).reshape(G, B, B)
     mine = exchange(near.at[:, HALF:].set(chunks), "near")
     theirs = other_core(mine)
-    weight, slope, near, stats, tops, table = statistics(place, live, mine, theirs, far)
+    weight, slope, near, stats, tops, table = statistics(place, mine, theirs, far)
     parts = exchange(to_all(stats), "near")
     pairs, near, keep, send = gradients(
         place, near, far, weight, slope, tops, parts, table

time: 149 us -> 141 us (0.946)
  Pallas kernels: 23.5 us -> 12.9 us
  waiting for transfers between devices: 24.8 us -> 26.5 us
    pallas_call x3 -> x1, Pallas kernels: 16.4 us -> 5.7 us  [statistics(): pl.pallas_call(stats_kernel, in_specs=[SCALARS] + [ARRAY] * 3, out_specs=...]
    all_to_all x2, waiting for transfers between devices: 21.6 us -> 24.7 us  [exchange(): return lax.all_to_all(parts, axis, 0, 0, tiled=True)]
    broadcast_in_dim x1 -> x2, local copies, waits for them, and re-layouts: 0.01 us -> 1.51 us  [to_all(): return jnp.broadcast_to(shard[None], (G,) + shard.shape)]
    unnamed x11 -> x7, local copies, waits for them, and re-layouts: 4.68 us -> 3.33 us
  transfers between devices with their start and end apart: 4 -> 4, of which waited for: 4 -> 4; matrix products, arithmetic and copies ran while one was open for 2% -> 2% of each run, Pallas kernels for 1% -> 0%
where the time goes in v6:
time: 141 us; the launch traced here: 140 us
  blocking collectives  73.5 us (52%)
  waiting for transfers between devices  26.5 us (19%)
  starting transfers between devices  19.1 us (14%)
  Pallas kernels  12.9 us (9%)
  local copies, waits for them, and re-layouts  5.01 us (4%)
  other arithmetic  1.55 us (1%)
    all_to_all x5, blocking collectives, exchange(): return lax.all_to_all(parts, axis, 0, 0, tiled=True)  73.5 us
    all_to_all x2, waiting for transfers between devices, exchange(): return lax.all_to_all(parts, axis, 0, 0, tiled=True)  24.7 us
    all_to_all x2, starting transfers between devices, exchange(): return lax.all_to_all(parts, axis, 0, 0, tiled=True)  15.3 us
    pallas_call x1, Pallas kernels, statistics(): pl.pallas_call(stats_kernel, in_specs=[SCALARS] + [ARRAY] * 3, out_specs=...  5.7 us
    pallas_call x1, Pallas kernels, gradients(): pl.pallas_call(grads_kernel, in_specs=[SCALARS] + [ARRAY] * 7, out_specs=...  5.64 us
    ppermute x2, starting transfers between devices, other_core(): return lax.ppermute(shard, 'near', [(i, i ^ 1) for i in range(G)])  3.83 us
    unnamed x7, local copies, waits for them, and re-layouts  3.33 us
  transfers between devices with their start and end apart: 4, of which 4 were waited for; matrix products, arithmetic and copies ran while one was open for 2% of the time, Pallas kernels for 0%

profile of v6, /device:TPU:64, one launch (start us, length us, event | category | flops | bytes accessed | tf_op | source)
XLA Modules:
  0.0 139.9 jit_solution(16982723075811806156)
XLA Ops:
  0.6 1.5 %broadcast_in_dim.8 = bf16[8,128,128]{2,1,0:T(8,128)(2,1)} broadcast(bf16[128,128]{1,0:T(8,128)(2,1)} %param.10), dimensions={1,2} | broadcast | bytes 294912 | tf_op jit(solution)/shard_map/broadcast_in_dim | solution.py:369
  2.1 11.8 %all-to-all-start = ((bf16[8,128,128]{2,1,0:T(8,128)(2,1)}), bf16[8,128,128]{2,1,0:T(8,128)(2,1)S(1)}, u32[]{:S(2)}, u32[]{:S(2)}) async-start(bf16[8,128,128]{2,1,0:T(8,128)(2,1)} %broadcast_in_dim.8), calls=%async_computation | async-start | bytes 524288 | tf_op jit(solution)/shard_map/all_to_all | solution.py:365
  14.0 0.8 copy.11
  14.8 0.8 copy.12.grad_ref
  15.6 0.1 pad_maximum_fusion.chunk_ref
  15.7 12.1 %all-to-all-done.frames_ref = bf16[8,128,128]{2,1,0:T(8,128)(2,1)S(1)} async-done(((bf16[8,128,128]{2,1,0:T(8,128)(2,1)}), bf16[8,128,128]{2,1,0:T(8,128)(2,1)S(1)}, u32[]{:S(2)}, u32[]{:S(2)}) %all-to-all-start) | async-done | bytes 262176 | tf_op jit(solution)/shard_map/all_to_all | solution.py:365
  27.8 0.0 copy-start
  27.8 1.0 copy-done
  28.8 0.5 project.1
  29.3 18.1 %all_to_all.35.far_ref = bf16[8,160,128]{2,1,0:T(8,128)(2,1)S(1)} all-to-all(bf16[8,160,128]{2,1,0:T(8,128)(2,1)S(1)} %get-tuple-element.43), channel_id=1, replica_groups=mesh['far'=8,'near'=8,'head'=8] {'far'}, dimensions={0} | all-to-all | bytes 655360 | tf_op jit(solution)/shard_map/all_to_all | solution.py:365
  47.5 16.4 %all_to_all.36.mine_ref = bf16[8,192,128]{2,1,0:T(8,128)(2,1)S(1)} all-to-all(bf16[8,192,128]{2,1,0:T(8,128)(2,1)S(1)} %constant_dynamic-update-slice_fusion), channel_id=1, replica_groups=mesh['far'=8,'near'=8,'head'=8] {'near'}, dimensions={0} | all-to-all | bytes 786432 | tf_op jit(solution)/shard_map/all_to_all | solution.py:365
  63.9 1.9 %collective-permute-start = (bf16[8,192,128]{2,1,0:T(8,128)(2,1)S(1)}, bf16[8,192,128]{2,1,0:T(8,128)(2,1)S(1)}, u32[]{:S(2)}, u32[]{:S(2)}) collective-permute-start(bf16[8,192,128]{2,1,0:T(8,128)(2,1)S(1)} %all_to_all.36.mine_ref), channel_id=1, source_target_pairs={{0,8},{8,0},{16,24},{24,16},{32,40},{40,32},{48,56},{56,48},{1,9},... | collective-permute-start | bytes 1179656 | tf_op jit(solution)/shard_map/ppermute | solution.py:373
  66.5 0.7 pad_add_fusion.place
  67.2 0.3 collective-permute-done.theirs_ref
  67.5 5.7 %statistics.1 = (f32[1024,1024]{1,0:T(8,128)S(1)}, f32[1024,1024]{1,0:T(8,128)S(1)}, bf16[8,128,128]{2,1,0:T(8,128)(2,1)S(1)}, f32[16,128]{1,0:T(8,128)S(1)}, f3...) custom-call(s32[67]{0:T(128)S(1)} %pad_add_fusion.place, bf16[8,192,128]{2,1,0:T(8,128)(2,1)S(1)} %all_to_all.36.mine_ref, ...), custom_call_target="tpu_custom_call" | custom-call | tf_op jit(solution)/shard_map/statistics/pallas_call | solution.py:167
  73.2 8.8 %all_to_all.37.parts_ref = f32[8,16,128]{2,1,0:T(8,128)S(1)} all-to-all(f32[8,16,128]{2,1,0:T(8,128)S(1)} %broadcast_in_dim.22), channel_id=1, replica_groups=mesh['far'=8,'near'=8,'head'=8] {'near'}, dimensions={0} | all-to-all | bytes 131072 | tf_op jit(solution)/shard_map/all_to_all | solution.py:365
  82.0 0.0 copy-start.1
  82.0 5.6 %gradients.1 = (bf16[8,128,128]{2,1,0:T(8,128)(2,1)S(1)}, bf16[8,192,128]{2,1,0:T(8,128)(2,1)S(1)}, f32[8,128,128]{2,1,0:T(8,128)S(1)}, bf16[8,128,128]{2,1,0:T(8,128)(2,1)S(1)}) custom-call(s32[67]{0:T(128)S(1)} %pad_add_fusion.place, bf16[8,128,128]{2,1,0:T(8,128)(2,1)S(1)} %get-tuple-element.44.near_ref, bf16[8,160,128]{2,1,0:T(8,128)(2,1)S(1)} %all_to_all.35.far_ref, ...), custom_call_target="tpu_custom_call" | custom-call | tf_op jit(solution)/shard_map/gradients/pallas_call | solution.py:299
  87.7 1.9 %collective-permute-start.1 = (bf16[8,128,128]{2,1,0:T(8,128)(2,1)S(1)}, bf16[8,128,128]{2,1,0:T(8,128)(2,1)S(1)}, u32[]{:S(2)}, u32[]{:S(2)}) collective-permute-start(bf16[8,128,128]{2,1,0:T(8,128)(2,1)S(1)} %get-tuple-element.52), channel_id=1, source_target_pairs={{0,8},{8,0},{16,24},{24,16},{32,40},{40,32},{48,56},{56,48},{1,9},... | collective-permute-start | bytes 786440 | tf_op jit(solution)/shard_map/ppermute | solution.py:373
  89.6 1.5 %collective-permute-done.1 = bf16[8,128,128]{2,1,0:T(8,128)(2,1)S(1)} collective-permute-done((bf16[8,128,128]{2,1,0:T(8,128)(2,1)S(1)}, bf16[8,128,128]{2,1,0:T(8,128)(2,1)S(1)}, u32[]{:S(2)}, u32[]{:S(2)}) %collective-permute-start.1) | collective-permute-done | bytes 262176 | tf_op jit(solution)/shard_map/ppermute | solution.py:373
  91.1 0.1 fusion
  91.2 14.4 %all_to_all.38.near_ref = bf16[8,192,128]{2,1,0:T(8,128)(2,1)S(1)} all-to-all(bf16[8,192,128]{2,1,0:T(8,128)(2,1)S(1)} %fusion), channel_id=1, replica_groups=mesh['far'=8,'near'=8,'head'=8] {'near'}, dimensions={0} | all-to-all | bytes 786432 | tf_op jit(solution)/shard_map/all_to_all | solution.py:365
  105.6 0.1 fold.1
  105.7 15.7 %all_to_all.39.far_ref = bf16[8,160,128]{2,1,0:T(8,128)(2,1)S(1)} all-to-all(bf16[8,160,128]{2,1,0:T(8,128)(2,1)S(1)} %get-tuple-element.54), channel_id=1, replica_groups=mesh['far'=8,'near'=8,'head'=8] {'far'}, dimensions={0} | all-to-all | bytes 655360 | tf_op jit(solution)/shard_map/all_to_all | solution.py:365
  121.5 0.0 copy-done.1
  121.5 1.0 unproject.1
  122.5 3.4 %all-to-all-start.6 = ((bf16[8,128,128]{2,1,0:T(8,128)(2,1)}), bf16[8,128,128]{2,1,0:T(8,128)(2,1)S(1)}, u32[]{:S(2)}, u32[]{:S(2)}) async-start(bf16[8,128,128]{2,1,0:T(8,128)(2,1)} %get-tuple-element.56), calls=%async_computation.6 | async-start | bytes 524288 | tf_op jit(solution)/shard_map/all_to_all | solution.py:365
  125.9 0.1 reshape.81
  126.0 0.7 copy.14
  126.7 12.6 %all-to-all-done.6 = bf16[8,128,128]{2,1,0:T(8,128)(2,1)S(1)} async-done(((bf16[8,128,128]{2,1,0:T(8,128)(2,1)}), bf16[8,128,128]{2,1,0:T(8,128)(2,1)S(1)}, u32[]{:S(2)}, u32[]{:S(2)}) %all-to-all-start.6) | async-done | bytes 262176 | tf_op jit(solution)/shard_map/all_to_all | solution.py:365
  139.3 0.7 reduce_sum.12
  (6 shorter events, 0.1 us)
Async XLA Ops:
  2.1 25.7 %all-to-all-start = ((bf16[8,128,128]{2,1,0:T(8,128)(2,1)}), bf16[8,128,128]{2,1,0:T(8,128)(2,1)S(1)}, u32[]{:S(2)}, u32[]{:S(2)}) async-start(bf16[8,128,128]{2,1,0:T(8,128)(2,1)} %broadcast_in_dim.8), calls=%async_computation | async-start | bytes 524288 | tf_op jit(solution)/shard_map/all_to_all | solution.py:365
  27.8 1.0 copy-start
  63.9 3.6 %collective-permute-start = (bf16[8,192,128]{2,1,0:T(8,128)(2,1)S(1)}, bf16[8,192,128]{2,1,0:T(8,128)(2,1)S(1)}, u32[]{:S(2)}, u32[]{:S(2)}) collective-permute-start(bf16[8,192,128]{2,1,0:T(8,128)(2,1)S(1)} %all_to_all.36.mine_ref), channel_id=1, source_target_pairs={{0,8},{8,0},{16,24},{24,16},{32,40},{40,32},{48,56},{56,48},{1,9},... | collective-permute-start | bytes 1179656 | tf_op jit(solution)/shard_map/ppermute | solution.py:373
  82.0 39.4 %copy-start.1 = (bf16[3,64,1024]{2,1,0:T(8,128)(2,1)S(1)}, bf16[3,64,1024]{2,1,0:T(8,128)(2,1)}, u32[]{:S(2)}) copy-start(bf16[3,64,1024]{2,1,0:T(8,128)(2,1)} %param.11) | copy-start | bytes 1179652
  87.7 3.4 %collective-permute-start.1 = (bf16[8,128,128]{2,1,0:T(8,128)(2,1)S(1)}, bf16[8,128,128]{2,1,0:T(8,128)(2,1)S(1)}, u32[]{:S(2)}, u32[]{:S(2)}) collective-permute-start(bf16[8,128,128]{2,1,0:T(8,128)(2,1)S(1)} %get-tuple-element.52), channel_id=1, source_target_pairs={{0,8},{8,0},{16,24},{24,16},{32,40},{40,32},{48,56},{56,48},{1,9},... | collective-permute-start | bytes 786440 | tf_op jit(solution)/shard_map/ppermute | solution.py:373
  122.5 16.8 %all-to-all-start.6 = ((bf16[8,128,128]{2,1,0:T(8,128)(2,1)}), bf16[8,128,128]{2,1,0:T(8,128)(2,1)S(1)}, u32[]{:S(2)}, u32[]{:S(2)}) async-start(bf16[8,128,128]{2,1,0:T(8,128)(2,1)} %get-tuple-element.56), calls=%async_computation.6 | async-start | bytes 524288 | tf_op jit(solution)/shard_map/all_to_all | solution.py:365

commit v7 on v6

--- a/solution.py
+++ b/solution.py
@@ -16,8 +16,9 @@
 WIDE = TABLE + 2 * PAD
 SCALE = E ** (-0.5)
 SPAN = 2
-HALF = B // 2
-SHARE = HALF + B
+PAIRS = 4
+SHARE = B + 4 * E
+BACK = E + 4 * E
 CHUNK = E // 2
 ROWS = B + E // 2
 HIDDEN = -1e30
@@ -43,9 +44,10 @@
     low = total.astype(BF)
     scaled = (low[:, :E].astype(F32) * SCALE).astype(BF)
     paired = jnp.concatenate([scaled, grad_ref[...]], axis=1)
+    for g in range(PAIRS):
+        near_ref[g, :B] = paired
+        near_ref[g, B:] = jnp.zeros((4 * E, B), BF)
     for g in range(G):
-        near_ref[g, :HALF] = paired[(g % 2) * HALF : (g % 2 + 1) * HALF]
-        near_ref[g, HALF:] = jnp.zeros((B, B), BF)
         far_ref[g, :B] = low[:, E:]
         far_ref[g, B:] = chunk_ref[...]
 
@@ -54,7 +56,7 @@
     return pl.pallas_call(
         project_kernel,
         out_shape=(
-            jax.ShapeDtypeStruct((G, SHARE, B), BF),
+            jax.ShapeDtypeStruct((PAIRS, SHARE, B), BF),
             jax.ShapeDtypeStruct((G, ROWS, B), BF),
         ),
         compiler_params=pltpu.CompilerParams(vmem_limit_bytes=LIMIT),
@@ -94,19 +96,17 @@
     table_ref[:, :PAD] = jnp.zeros((E, PAD), BF)
     table_ref[:, WIDE - PAD :] = jnp.zeros((E, PAD), BF)
     first = place[1] % 2 == 0
-    for g in range(G):
-        mine = mine_ref[g, :HALF].astype(F32)
-        theirs = theirs_ref[g, :HALF].astype(F32)
-        near_ref[g, :HALF] = jnp.where(first, mine, theirs).astype(BF)
-        near_ref[g, HALF:] = jnp.where(first, theirs, mine).astype(BF)
-    for y in range(G):
-        rows = slice(HALF + CHUNK * (y % 4), HALF + CHUNK * (y % 4 + 1))
-        own = first if y < 4 else jnp.logical_not(first)
-        for k in range(4):
-            left, right = (
-                jnp.where(own, mine_ref[g, rows].astype(F32), theirs_ref[g, rows].astype(F32))
-                for g in (2 * k, 2 * k + 1)
-            )
+    def sides(k, rows):
+        mine = mine_ref[k, rows].astype(F32)
+        theirs = theirs_ref[k, rows].astype(F32)
+        return jnp.where(first, mine, theirs), jnp.where(first, theirs, mine)
+
+    for k in range(PAIRS):
+        left, right = sides(k, slice(0, B))
+        near_ref[2 * k] = left.astype(BF)
+        near_ref[2 * k + 1] = right.astype(BF)
+        for y in range(G):
+            left, right = sides(k, slice(B + CHUNK * y, B + CHUNK * (y + 1)))
             top = jnp.concatenate([left[:, :E], right[:, :E]], axis=1)
             end = jnp.concatenate([left[:, E:], right[:, E:]], axis=1)
             at = PAD + (4 * y + k) * B
@@ -192,7 +192,6 @@
     parts_ref,
     table_ref,
     far_out,
-    near_out,
     keep_out,
     send_out,
     query_sum,
@@ -261,9 +260,18 @@
     both = jnp.concatenate(turned, axis=1)
     main = nn(lows[...], keys) + nt(outers[...], ends)
     tails = nn(both[:E], outers[...])
+    first = place[1] % 2 == 0
+
+    def split(k, rows, left, right):
+        keep_out[k, rows] = jnp.where(first, left, right)
+        send_out[k, rows] = jnp.where(first, right, left).astype(BF)
+
+    packed = []
     for u in range(G):
-        query_low = ((query_sum[u] + main[u * B : (u + 1) * B]) * SCALE).astype(BF)
-        near_out[u, :HALF] = jnp.concatenate([query_low[:E], query_low[E:]], axis=1)
+        query = (query_sum[u] + main[u * B : (u + 1) * B]) * SCALE
+        packed.append(jnp.concatenate([query[:E], query[E:]], axis=1))
+    for k in range(PAIRS):
+        split(k, slice(0, E), packed[2 * k], packed[2 * k + 1])
     pairs = jnp.concatenate([nn(both[:E], lows[...]), nn(both[E:], probs[...])], axis=0)
     offsets = lax.broadcasted_iota(jnp.int32, (E, WIDE), 1) - (TABLE // 2 + PAD)
     terms = table_sum[...]
@@ -273,9 +281,7 @@
     upper = upper + jnp.sum(tails[:, B:], axis=1, keepdims=True)
     lower = lower + jnp.sum(tails[:, :B], axis=1, keepdims=True)
     table_sum[...] = jnp.where(offsets == clip, upper, jnp.where(offsets == -clip, lower, terms))
-    first = place[1] % 2 == 0
-    for k in range(4):
-        pieces = []
+    for k in range(PAIRS):
         for y in range(G):
             at = PAD + (4 * y + k) * B
             block = table_sum[:, at : at + B]
@@ -283,14 +289,7 @@
             top, end = block[:CHUNK], block[CHUNK:]
             left = jnp.concatenate([top[:, :E], end[:, :E]], axis=1)
             right = jnp.concatenate([top[:, E:], end[:, E:]], axis=1)
-            pieces.append((left, right))
-        for y in range(4):
-            rows = slice(CHUNK * y, CHUNK * (y + 1))
-            for side in range(2):
-                early_half, late_half = pieces[y][side], pieces[y + 4][side]
-                keep_out[2 * k + side, rows] = jnp.where(first, early_half, late_half)
-                send_out[2 * k + side, rows] = jnp.where(first, late_half, early_half).astype(BF)
-    near_out[:, HALF:] = jnp.zeros((G, B, B), BF)
+            split(k, slice(E + CHUNK * y, E + CHUNK * (y + 1)), left, right)
     for y in range(G):
         far_out[y] = pairs[:, y * B : (y + 1) * B].T.astype(BF)
 
@@ -299,12 +298,11 @@
     return pl.pallas_call(
         grads_kernel,
         in_specs=[SCALARS] + [ARRAY] * 7,
-        out_specs=[ARRAY] * 4,
+        out_specs=[ARRAY] * 3,
         out_shape=(
             jax.ShapeDtypeStruct((G, B, B), BF),
-            jax.ShapeDtypeStruct((G, SHARE, B), BF),
-            jax.ShapeDtypeStruct((G, B, B), F32),
-            jax.ShapeDtypeStruct((G, B, B), BF),
+            jax.ShapeDtypeStruct((PAIRS, BACK, B), F32),
+            jax.ShapeDtypeStruct((PAIRS, BACK, B), BF),
         ),
         scratch_shapes=[
             pltpu.VMEM((G, B, E), F32),
@@ -320,14 +318,10 @@
 
 
 def fold_kernel(near_ref, pairs_ref, query_ref, far_ref):
-    packed = jnp.sum(near_ref[:, :HALF].astype(F32), axis=0).astype(BF)
-    query_ref[...] = jnp.concatenate([packed[:, :E], packed[:, E:]], axis=0)
-    for side in range(2):
-        total = near_ref[side, HALF:].astype(F32)
-        for k in range(1, 4):
-            total = total + near_ref[2 * k + side, HALF:].astype(F32)
-        for y in range(4):
-            far_ref[4 * side + y, B:] = total[CHUNK * y : CHUNK * (y + 1)].astype(BF)
+    total = jnp.sum(near_ref[...].astype(F32), axis=0).astype(BF)
+    query_ref[...] = jnp.concatenate([total[:E, :E], total[:E, E:]], axis=0)
+    for y in range(G):
+        far_ref[y, B:] = total[E + CHUNK * y : E + CHUNK * (y + 1)]
     far_ref[:, :B] = pairs_ref[...]
 
 
@@ -370,28 +364,28 @@
 
 
 def other_core(shard):
-    return lax.ppermute(shard, "near", [(i, i ^ 1) for i in range(G)])
+    return lax.ppermute(shard, "core", [(0, 1), (1, 0)])
 
 
 def shards(frames, weights, offset_table, clip_range, valid_frames, context_grad):
     weight_rows = weights.reshape(3 * E, G * B)
-    own = jnp.stack([lax.axis_index("far"), lax.axis_index("near"), clip_range[0]])
+    own = jnp.stack([lax.axis_index("far"), lax.axis_index(("pair", "core")), clip_range[0]])
     place = jnp.concatenate([own, valid_frames])
     turned = offset_table.T
     chunk = jnp.concatenate([turned[: E // 2], turned[E // 2 :]], axis=1)
     gathered = exchange(to_all(frames), "head")
     near, far = project(gathered, weight_rows, context_grad, chunk)
     far = exchange(far, "far")
-    chunks = jnp.broadcast_to(far[:, B:].reshape(1, 2, B, B), (4, 2, B, B)).reshape(G, B, B)
-    mine = exchange(near.at[:, HALF:].set(chunks), "near")
+    chunks = jnp.broadcast_to(far[:, B:].reshape(1, 4 * E, B), (PAIRS, 4 * E, B))
+    mine = exchange(near.at[:, B:].set(chunks), "pair")
     theirs = other_core(mine)
     weight, slope, near, stats, tops, table = statistics(place, mine, theirs, far)
-    parts = exchange(to_all(stats), "near")
-    pairs, near, keep, send = gradients(
+    parts = exchange(to_all(stats), ("pair", "core"))
+    pairs, keep, send = gradients(
         place, near, far, weight, slope, tops, parts, table
     )
     halves = (keep + other_core(send).astype(F32)).astype(BF)
-    query, far = fold(exchange(near.at[:, HALF:].set(halves), "near"), pairs)
+    query, far = fold(exchange(halves, "pair"), pairs)
     terms, table_part = unproject(exchange(far, "far"), query, weight_rows)
     table_grad = table_part.reshape(E // 2, 2, E).transpose(2, 1, 0).reshape(E, E)
     terms = exchange(terms, "head")
@@ -400,8 +394,8 @@
 
 
 def solution(mesh):
-    split = Mesh(mesh.devices.reshape(G, G, G), ("far", "near", "head"))
-    seq = ("far", "near")
+    split = Mesh(mesh.devices.reshape(G, PAIRS, 2, G), ("far", "pair", "core", "head"))
+    seq = ("far", "pair", "core")
     placed = (
         P(seq, "head"),
         P(None, "head", None),

time: 141 us -> 135 us (0.957)
  the two profiles are of different devices: /device:TPU:64 before, /device:TPU:8 now
where the time goes in v7:
time: 135 us; the launch traced here: 134 us
  blocking collectives  71.1 us (53%)
  waiting for transfers between devices  22.4 us (17%)
  starting transfers between devices  20 us (15%)
  Pallas kernels  13 us (10%)
  local copies, waits for them, and re-layouts  5 us (4%)
  other arithmetic  1.55 us (1%)
  between operations  1.36 us (1%)
    all_to_all x5, blocking collectives, exchange(): return lax.all_to_all(parts, axis, 0, 0, tiled=True)  71.1 us
    all_to_all x2, waiting for transfers between devices, exchange(): return lax.all_to_all(parts, axis, 0, 0, tiled=True)  20.5 us
    all_to_all x2, starting transfers between devices, exchange(): return lax.all_to_all(parts, axis, 0, 0, tiled=True)  16.2 us
    pallas_call x1, Pallas kernels, statistics(): pl.pallas_call(stats_kernel, in_specs=[SCALARS] + [ARRAY] * 3, out_specs=...  5.75 us
    pallas_call x1, Pallas kernels, gradients(): pl.pallas_call(grads_kernel, in_specs=[SCALARS] + [ARRAY] * 7, out_specs=...  5.66 us
    ppermute x2, starting transfers between devices, other_core(): return lax.ppermute(shard, 'core', [(0, 1), (1, 0)])  3.83 us
    unnamed x7, local copies, waits for them, and re-layouts  3.33 us
  transfers between devices with their start and end apart: 4, of which 4 were waited for; matrix products, arithmetic and copies ran while one was open for 2% of the time, Pallas kernels for 0%

profile of v7, /device:TPU:8, one launch (start us, length us, event | category | flops | bytes accessed | tf_op | source)
XLA Modules:
  0.0 134.3 jit_solution(13901825727543550997)
XLA Ops:
  0.6 1.5 %broadcast_in_dim.6 = bf16[8,128,128]{2,1,0:T(8,128)(2,1)} broadcast(bf16[128,128]{1,0:T(8,128)(2,1)} %param.8), dimensions={1,2} | broadcast | bytes 294912 | tf_op jit(solution)/shard_map/broadcast_in_dim | solution.py:363
  2.1 12.7 %all-to-all-start = ((bf16[8,128,128]{2,1,0:T(8,128)(2,1)}), bf16[8,128,128]{2,1,0:T(8,128)(2,1)S(1)}, u32[]{:S(2)}, u32[]{:S(2)}) async-start(bf16[8,128,128]{2,1,0:T(8,128)(2,1)} %broadcast_in_dim.6), calls=%async_computation | async-start | bytes 524288 | tf_op jit(solution)/shard_map/all_to_all | solution.py:359
  14.9 0.8 copy.11
  15.7 0.8 copy.12.grad_ref
  16.5 0.1 pad_maximum_fusion.chunk_ref
  16.6 10.2 %all-to-all-done.frames_ref = bf16[8,128,128]{2,1,0:T(8,128)(2,1)S(1)} async-done(((bf16[8,128,128]{2,1,0:T(8,128)(2,1)}), bf16[8,128,128]{2,1,0:T(8,128)(2,1)S(1)}, u32[]{:S(2)}, u32[]{:S(2)}) %all-to-all-start) | async-done | bytes 262176 | tf_op jit(solution)/shard_map/all_to_all | solution.py:359
  26.8 0.0 copy-start
  26.8 1.0 copy-done
  27.8 0.5 project.1
  28.2 17.0 %all_to_all.35.far_ref = bf16[8,160,128]{2,1,0:T(8,128)(2,1)S(1)} all-to-all(bf16[8,160,128]{2,1,0:T(8,128)(2,1)S(1)} %get-tuple-element.30), channel_id=1, replica_groups=mesh['far'=8,'pair'=4,'core'=2,'head'=8] {'far'}, dimensions={0} | all-to-all | bytes 655360 | tf_op jit(solution)/shard_map/all_to_all | solution.py:359
  45.2 0.1 broadcast_dynamic-update-slice_fusion
  45.3 16.1 %all_to_all.36.mine_ref = bf16[4,384,128]{2,1,0:T(8,128)(2,1)S(1)} all-to-all(bf16[4,384,128]{2,1,0:T(8,128)(2,1)S(1)} %broadcast_dynamic-update-slice_fusion), channel_id=1, replica_groups=mesh['far'=8,'pair'=4,'core'=2,'head'=8] {'pair'}, dimensions={0} | all-to-all | bytes 786432 | tf_op jit(solution)/shard_map/all_to_all | solution.py:359
  61.4 1.9 %collective-permute-start = (bf16[4,384,128]{2,1,0:T(8,128)(2,1)S(1)}, bf16[4,384,128]{2,1,0:T(8,128)(2,1)S(1)}, u32[]{:S(2)}, u32[]{:S(2)}) collective-permute-start(bf16[4,384,128]{2,1,0:T(8,128)(2,1)S(1)} %all_to_all.36.mine_ref), channel_id=1, source_target_pairs={{0,8},{8,0},{1,9},{9,1},{2,10},{10,2},{3,11},{11,3},{4,12},{12,4},... | collective-permute-start | bytes 1179656 | tf_op jit(solution)/shard_map/ppermute | solution.py:367
  63.9 0.7 pad_add_fusion.place
  64.7 0.3 collective-permute-done.theirs_ref
  65.0 5.8 %statistics.1 = (f32[1024,1024]{1,0:T(8,128)S(1)}, f32[1024,1024]{1,0:T(8,128)S(1)}, bf16[8,128,128]{2,1,0:T(8,128)(2,1)S(1)}, f32[16,128]{1,0:T(8,128)S(1)}, f3...) custom-call(s32[67]{0:T(128)S(1)} %pad_add_fusion.place, bf16[4,384,128]{2,1,0:T(8,128)(2,1)S(1)} %all_to_all.36.mine_ref, ...), custom_call_target="tpu_custom_call" | custom-call | tf_op jit(solution)/shard_map/statistics/pallas_call | solution.py:167
  70.7 8.4 %all_to_all.37.parts_ref = f32[8,16,128]{2,1,0:T(8,128)S(1)} all-to-all(f32[8,16,128]{2,1,0:T(8,128)S(1)} %broadcast_in_dim.8), channel_id=1, replica_groups=mesh['far'=8,'pair'=4,'core'=2,'head'=8] {'pair','core'}, dimensions={0} | all-to-all | bytes 131072 | tf_op jit(solution)/shard_map/all_to_all | solution.py:359
  79.2 0.0 copy-start.1
  79.2 5.7 %gradients.1 = (bf16[8,128,128]{2,1,0:T(8,128)(2,1)S(1)}, f32[4,320,128]{2,1,0:T(8,128)S(1)}, bf16[4,320,128]{2,1,0:T(8,128)(2,1)S(1)}) custom-call(s32[67]{0:T(128)S(1)} %pad_add_fusion.place, bf16[8,128,128]{2,1,0:T(8,128)(2,1)S(1)} %get-tuple-element.31.near_ref, bf16[8,160,128]{2,1,0:T(8,128)(2,1)S(1)} %all_to_all.35.far_ref, ...), custom_call_target="tpu_custom_call" | custom-call | tf_op jit(solution)/shard_map/gradients/pallas_call | solution.py:298
  84.9 1.9 %collective-permute-start.1 = (bf16[4,320,128]{2,1,0:T(8,128)(2,1)S(1)}, bf16[4,320,128]{2,1,0:T(8,128)(2,1)S(1)}, u32[]{:S(2)}, u32[]{:S(2)}) collective-permute-start(bf16[4,320,128]{2,1,0:T(8,128)(2,1)S(1)} %get-tuple-element.38), channel_id=1, source_target_pairs={{0,8},{8,0},{1,9},{9,1},{2,10},{10,2},{3,11},{11,3},{4,12},{12,4},... | collective-permute-start | bytes 983048 | tf_op jit(solution)/shard_map/ppermute | solution.py:367
  86.8 1.6 %collective-permute-done.1 = bf16[4,320,128]{2,1,0:T(8,128)(2,1)S(1)} collective-permute-done((bf16[4,320,128]{2,1,0:T(8,128)(2,1)S(1)}, bf16[4,320,128]{2,1,0:T(8,128)(2,1)S(1)}, u32[]{:S(2)}, u32[]{:S(2)}) %collective-permute-start.1) | collective-permute-done | bytes 327712 | tf_op jit(solution)/shard_map/ppermute | solution.py:367
  88.4 0.1 add_convert_fusion
  88.5 13.2 %all_to_all.38.near_ref = bf16[4,320,128]{2,1,0:T(8,128)(2,1)S(1)} all-to-all(bf16[4,320,128]{2,1,0:T(8,128)(2,1)S(1)} %add_convert_fusion), channel_id=1, replica_groups=mesh['far'=8,'pair'=4,'core'=2,'head'=8] {'pair'}, dimensions={0} | all-to-all | bytes 655360 | tf_op jit(solution)/shard_map/all_to_all | solution.py:359
  101.7 0.1 fold.1
  101.8 16.4 %all_to_all.39.far_ref = bf16[8,160,128]{2,1,0:T(8,128)(2,1)S(1)} all-to-all(bf16[8,160,128]{2,1,0:T(8,128)(2,1)S(1)} %get-tuple-element.40), channel_id=1, replica_groups=mesh['far'=8,'pair'=4,'core'=2,'head'=8] {'far'}, dimensions={0} | all-to-all | bytes 655360 | tf_op jit(solution)/shard_map/all_to_all | solution.py:359
  118.2 0.0 copy-done.1
  118.2 1.0 unproject.1
  119.2 3.4 %all-to-all-start.6 = ((bf16[8,128,128]{2,1,0:T(8,128)(2,1)}), bf16[8,128,128]{2,1,0:T(8,128)(2,1)S(1)}, u32[]{:S(2)}, u32[]{:S(2)}) async-start(bf16[8,128,128]{2,1,0:T(8,128)(2,1)} %get-tuple-element.42), calls=%async_computation.6 | async-start | bytes 524288 | tf_op jit(solution)/shard_map/all_to_all | solution.py:359
  122.6 0.1 reshape.47
  122.7 0.7 copy.14
  123.4 10.3 %all-to-all-done.6 = bf16[8,128,128]{2,1,0:T(8,128)(2,1)S(1)} async-done(((bf16[8,128,128]{2,1,0:T(8,128)(2,1)}), bf16[8,128,128]{2,1,0:T(8,128)(2,1)S(1)}, u32[]{:S(2)}, u32[]{:S(2)}) %all-to-all-start.6) | async-done | bytes 262176 | tf_op jit(solution)/shard_map/all_to_all | solution.py:359
  133.7 0.7 reduce_sum.12
  (4 shorter events, 0.0 us)
Async XLA Ops:
  2.1 24.6 %all-to-all-start = ((bf16[8,128,128]{2,1,0:T(8,128)(2,1)}), bf16[8,128,128]{2,1,0:T(8,128)(2,1)S(1)}, u32[]{:S(2)}, u32[]{:S(2)}) async-start(bf16[8,128,128]{2,1,0:T(8,128)(2,1)} %broadcast_in_dim.6), calls=%async_computation | async-start | bytes 524288 | tf_op jit(solution)/shard_map/all_to_all | solution.py:359
  26.8 1.0 copy-start
  61.4 3.6 %collective-permute-start = (bf16[4,384,128]{2,1,0:T(8,128)(2,1)S(1)}, bf16[4,384,128]{2,1,0:T(8,128)(2,1)S(1)}, u32[]{:S(2)}, u32[]{:S(2)}) collective-permute-start(bf16[4,384,128]{2,1,0:T(8,128)(2,1)S(1)} %all_to_all.36.mine_ref), channel_id=1, source_target_pairs={{0,8},{8,0},{1,9},{9,1},{2,10},{10,2},{3,11},{11,3},{4,12},{12,4},... | collective-permute-start | bytes 1179656 | tf_op jit(solution)/shard_map/ppermute | solution.py:367
  79.2 39.0 %copy-start.1 = (bf16[3,64,1024]{2,1,0:T(8,128)(2,1)S(1)}, bf16[3,64,1024]{2,1,0:T(8,128)(2,1)}, u32[]{:S(2)}) copy-start(bf16[3,64,1024]{2,1,0:T(8,128)(2,1)} %param.9) | copy-start | bytes 1179652
  84.9 3.5 %collective-permute-start.1 = (bf16[4,320,128]{2,1,0:T(8,128)(2,1)S(1)}, bf16[4,320,128]{2,1,0:T(8,128)(2,1)S(1)}, u32[]{:S(2)}, u32[]{:S(2)}) collective-permute-start(bf16[4,320,128]{2,1,0:T(8,128)(2,1)S(1)} %get-tuple-element.38), channel_id=1, source_target_pairs={{0,8},{8,0},{1,9},{9,1},{2,10},{10,2},{3,11},{11,3},{4,12},{12,4},... | collective-permute-start | bytes 983048 | tf_op jit(solution)/shard_map/ppermute | solution.py:367
  119.2 14.5 %all-to-all-start.6 = ((bf16[8,128,128]{2,1,0:T(8,128)(2,1)}), bf16[8,128,128]{2,1,0:T(8,128)(2,1)S(1)}, u32[]{:S(2)}, u32[]{:S(2)}) async-start(bf16[8,128,128]{2,1,0:T(8,128)(2,1)} %get-tuple-element.42), calls=%async_computation.6 | async-start | bytes 524288 | tf_op jit(solution)/shard_map/all_to_all | solution.py:359

commit v8 on v7

--- a/solution.py
+++ b/solution.py
@@ -40,7 +40,7 @@
 def project_kernel(frames_ref, weights_ref, grad_ref, chunk_ref, near_ref, far_ref):
     total = jnp.zeros((B, 3 * E), F32)
     for h in range(G):
-        total = total + nt(frames_ref[h], weights_ref[:, h * B : (h + 1) * B])
+        total = total + nt(frames_ref[h], weights_ref[h])
     low = total.astype(BF)
     scaled = (low[:, :E].astype(F32) * SCALE).astype(BF)
     paired = jnp.concatenate([scaled, grad_ref[...]], axis=1)
@@ -337,7 +337,7 @@
 def unproject_kernel(far_ref, query_ref, weights_ref, out_ref, table_ref):
     total = jnp.sum(far_ref[...].astype(F32), axis=0)
     pairs = total[:B].astype(BF)
-    table_ref[...] = total[B:]
+    table_ref[...] = jnp.concatenate([total[B:, :E], total[B:, E:]], axis=0)
     terms = nn(query_ref[...], weights_ref[:E]) + nn(pairs, weights_ref[E:])
     for h in range(G):
         out_ref[h] = terms[:, h * B : (h + 1) * B].astype(BF)
@@ -348,7 +348,7 @@
         unproject_kernel,
         out_shape=(
             jax.ShapeDtypeStruct((G, B, B), BF),
-            jax.ShapeDtypeStruct((E // 2, B), F32),
+            jax.ShapeDtypeStruct((E, E), F32),
         ),
         compiler_params=pltpu.CompilerParams(vmem_limit_bytes=LIMIT),
         name="unproject",
@@ -369,12 +369,13 @@
 
 def shards(frames, weights, offset_table, clip_range, valid_frames, context_grad):
     weight_rows = weights.reshape(3 * E, G * B)
+    by_slice = weight_rows.reshape(3 * E, G, B).transpose(1, 0, 2)
     own = jnp.stack([lax.axis_index("far"), lax.axis_index(("pair", "core")), clip_range[0]])
     place = jnp.concatenate([own, valid_frames])
     turned = offset_table.T
     chunk = jnp.concatenate([turned[: E // 2], turned[E // 2 :]], axis=1)
     gathered = exchange(to_all(frames), "head")
-    near, far = project(gathered, weight_rows, context_grad, chunk)
+    near, far = project(gathered, by_slice, context_grad, chunk)
     far = exchange(far, "far")
     chunks = jnp.broadcast_to(far[:, B:].reshape(1, 4 * E, B), (PAIRS, 4 * E, B))
     mine = exchange(near.at[:, B:].set(chunks), "pair")
@@ -387,10 +388,9 @@
     halves = (keep + other_core(send).astype(F32)).astype(BF)
     query, far = fold(exchange(halves, "pair"), pairs)
     terms, table_part = unproject(exchange(far, "far"), query, weight_rows)
-    table_grad = table_part.reshape(E // 2, 2, E).transpose(2, 1, 0).reshape(E, E)
     terms = exchange(terms, "head")
     input_grad = jnp.sum(terms.astype(F32), axis=0).astype(BF)
-    return (input_grad, table_grad)
+    return (input_grad, table_part.T)
 
 
 def solution(mesh):

time: 135 us -> 134 us (level)
    unnamed x7 -> x8, local copies, waits for them, and re-layouts: 3.33 us -> 3.41 us
  transfers between devices with their start and end apart: 4 -> 4, of which waited for: 4 -> 4; matrix products, arithmetic and copies ran while one was open for 2% -> 3% of each run, Pallas kernels for 0% -> 0%
where the time goes in v8:
time: 134 us; the launch traced here: 133 us
  blocking collectives  71.1 us (53%)
  waiting for transfers between devices  21.9 us (16%)
  starting transfers between devices  20 us (15%)
  Pallas kernels  13 us (10%)
  local copies, waits for them, and re-layouts  5.04 us (4%)
  between operations  1.38 us (1%)
    all_to_all x5, blocking collectives, exchange(): return lax.all_to_all(parts, axis, 0, 0, tiled=True)  71.1 us
    all_to_all x2, waiting for transfers between devices, exchange(): return lax.all_to_all(parts, axis, 0, 0, tiled=True)  19.4 us
    all_to_all x2, starting transfers between devices, exchange(): return lax.all_to_all(parts, axis, 0, 0, tiled=True)  16.2 us
    pallas_call x1, Pallas kernels, statistics(): pl.pallas_call(stats_kernel, in_specs=[SCALARS] + [ARRAY] * 3, out_specs=...  5.75 us
    pallas_call x1, Pallas kernels, gradients(): pl.pallas_call(grads_kernel, in_specs=[SCALARS] + [ARRAY] * 7, out_specs=...  5.66 us
    ppermute x2, starting transfers between devices, other_core(): return lax.ppermute(shard, 'core', [(0, 1), (1, 0)])  3.83 us
    unnamed x8, local copies, waits for them, and re-layouts  3.41 us
  transfers between devices with their start and end apart: 4, of which 4 were waited for; matrix products, arithmetic and copies ran while one was open for 3% of the time, Pallas kernels for 0%

profile of v8, /device:TPU:8, one launch (start us, length us, event | category | flops | bytes accessed | tf_op | source)
XLA Modules:
  0.0 133.3 jit_solution(3176780693113133296)
XLA Ops:
  0.6 0.0 copy-start.1
  0.6 1.5 %broadcast_in_dim.6 = bf16[8,128,128]{2,1,0:T(8,128)(2,1)} broadcast(bf16[128,128]{1,0:T(8,128)(2,1)} %param.8), dimensions={1,2} | broadcast | bytes 294912 | tf_op jit(solution)/shard_map/broadcast_in_dim | solution.py:363
  2.1 12.7 %all-to-all-start = ((bf16[8,128,128]{2,1,0:T(8,128)(2,1)}), bf16[8,128,128]{2,1,0:T(8,128)(2,1)S(1)}, u32[]{:S(2)}, u32[]{:S(2)}) async-start(bf16[8,128,128]{2,1,0:T(8,128)(2,1)} %broadcast_in_dim.6), calls=%async_computation | async-start | bytes 524288 | tf_op jit(solution)/shard_map/all_to_all | solution.py:359
  14.9 0.8 copy.12
  15.7 0.8 copy.13.grad_ref
  16.5 1.1 copy.15
  17.6 0.1 copy.17
  17.7 0.1 pad_maximum_fusion.chunk_ref
  17.8 9.0 %all-to-all-done.frames_ref = bf16[8,128,128]{2,1,0:T(8,128)(2,1)S(1)} async-done(((bf16[8,128,128]{2,1,0:T(8,128)(2,1)}), bf16[8,128,128]{2,1,0:T(8,128)(2,1)S(1)}, u32[]{:S(2)}, u32[]{:S(2)}) %all-to-all-start) | async-done | bytes 262176 | tf_op jit(solution)/shard_map/all_to_all | solution.py:359
  26.8 0.5 project.1
  27.2 17.0 %all_to_all.35.far_ref = bf16[8,160,128]{2,1,0:T(8,128)(2,1)S(1)} all-to-all(bf16[8,160,128]{2,1,0:T(8,128)(2,1)S(1)} %get-tuple-element.30), channel_id=1, replica_groups=mesh['far'=8,'pair'=4,'core'=2,'head'=8] {'far'}, dimensions={0} | all-to-all | bytes 655360 | tf_op jit(solution)/shard_map/all_to_all | solution.py:359
  44.2 0.1 broadcast_dynamic-update-slice_fusion
  44.3 16.1 %all_to_all.36.mine_ref = bf16[4,384,128]{2,1,0:T(8,128)(2,1)S(1)} all-to-all(bf16[4,384,128]{2,1,0:T(8,128)(2,1)S(1)} %broadcast_dynamic-update-slice_fusion), channel_id=1, replica_groups=mesh['far'=8,'pair'=4,'core'=2,'head'=8] {'pair'}, dimensions={0} | all-to-all | bytes 786432 | tf_op jit(solution)/shard_map/all_to_all | solution.py:359
  60.4 1.9 %collective-permute-start = (bf16[4,384,128]{2,1,0:T(8,128)(2,1)S(1)}, bf16[4,384,128]{2,1,0:T(8,128)(2,1)S(1)}, u32[]{:S(2)}, u32[]{:S(2)}) collective-permute-start(bf16[4,384,128]{2,1,0:T(8,128)(2,1)S(1)} %all_to_all.36.mine_ref), channel_id=1, source_target_pairs={{0,8},{8,0},{1,9},{9,1},{2,10},{10,2},{3,11},{11,3},{4,12},{12,4},... | collective-permute-start | bytes 1179656 | tf_op jit(solution)/shard_map/ppermute | solution.py:367
  63.0 0.0 copy-done.1
  63.0 0.1 pad_add_fusion.place
  63.0 0.9 collective-permute-done.theirs_ref
  64.0 5.8 %statistics.1 = (f32[1024,1024]{1,0:T(8,128)S(1)}, f32[1024,1024]{1,0:T(8,128)S(1)}, bf16[8,128,128]{2,1,0:T(8,128)(2,1)S(1)}, f32[16,128]{1,0:T(8,128)S(1)}, f3...) custom-call(s32[67]{0:T(128)S(1)} %pad_add_fusion.place, bf16[4,384,128]{2,1,0:T(8,128)(2,1)S(1)} %all_to_all.36.mine_ref, ...), custom_call_target="tpu_custom_call" | custom-call | tf_op jit(solution)/shard_map/statistics/pallas_call | solution.py:167
  69.8 8.5 %all_to_all.37.parts_ref = f32[8,16,128]{2,1,0:T(8,128)S(1)} all-to-all(f32[8,16,128]{2,1,0:T(8,128)S(1)} %broadcast_in_dim.8), channel_id=1, replica_groups=mesh['far'=8,'pair'=4,'core'=2,'head'=8] {'pair','core'}, dimensions={0} | all-to-all | bytes 131072 | tf_op jit(solution)/shard_map/all_to_all | solution.py:359
  78.2 0.0 copy-start
  78.2 5.7 %gradients.1 = (bf16[8,128,128]{2,1,0:T(8,128)(2,1)S(1)}, f32[4,320,128]{2,1,0:T(8,128)S(1)}, bf16[4,320,128]{2,1,0:T(8,128)(2,1)S(1)}) custom-call(s32[67]{0:T(128)S(1)} %pad_add_fusion.place, bf16[8,128,128]{2,1,0:T(8,128)(2,1)S(1)} %get-tuple-element.31.near_ref, bf16[8,160,128]{2,1,0:T(8,128)(2,1)S(1)} %all_to_all.35.far_ref, ...), custom_call_target="tpu_custom_call" | custom-call | tf_op jit(solution)/shard_map/gradients/pallas_call | solution.py:298
  83.9 1.9 %collective-permute-start.1 = (bf16[4,320,128]{2,1,0:T(8,128)(2,1)S(1)}, bf16[4,320,128]{2,1,0:T(8,128)(2,1)S(1)}, u32[]{:S(2)}, u32[]{:S(2)}) collective-permute-start(bf16[4,320,128]{2,1,0:T(8,128)(2,1)S(1)} %get-tuple-element.38), channel_id=1, source_target_pairs={{0,8},{8,0},{1,9},{9,1},{2,10},{10,2},{3,11},{11,3},{4,12},{12,4},... | collective-permute-start | bytes 983048 | tf_op jit(solution)/shard_map/ppermute | solution.py:367
  85.8 1.6 %collective-permute-done.1 = bf16[4,320,128]{2,1,0:T(8,128)(2,1)S(1)} collective-permute-done((bf16[4,320,128]{2,1,0:T(8,128)(2,1)S(1)}, bf16[4,320,128]{2,1,0:T(8,128)(2,1)S(1)}, u32[]{:S(2)}, u32[]{:S(2)}) %collective-permute-start.1) | collective-permute-done | bytes 327712 | tf_op jit(solution)/shard_map/ppermute | solution.py:367
  87.4 0.1 add_convert_fusion
  87.5 13.2 %all_to_all.38.near_ref = bf16[4,320,128]{2,1,0:T(8,128)(2,1)S(1)} all-to-all(bf16[4,320,128]{2,1,0:T(8,128)(2,1)S(1)} %add_convert_fusion), channel_id=1, replica_groups=mesh['far'=8,'pair'=4,'core'=2,'head'=8] {'pair'}, dimensions={0} | all-to-all | bytes 655360 | tf_op jit(solution)/shard_map/all_to_all | solution.py:359
  100.7 0.1 fold.1
  100.8 16.4 %all_to_all.39.far_ref = bf16[8,160,128]{2,1,0:T(8,128)(2,1)S(1)} all-to-all(bf16[8,160,128]{2,1,0:T(8,128)(2,1)S(1)} %get-tuple-element.40), channel_id=1, replica_groups=mesh['far'=8,'pair'=4,'core'=2,'head'=8] {'far'}, dimensions={0} | all-to-all | bytes 655360 | tf_op jit(solution)/shard_map/all_to_all | solution.py:359
  117.2 0.0 copy-done
  117.2 1.0 unproject.1
  118.2 3.4 %all-to-all-start.6 = ((bf16[8,128,128]{2,1,0:T(8,128)(2,1)}), bf16[8,128,128]{2,1,0:T(8,128)(2,1)S(1)}, u32[]{:S(2)}, u32[]{:S(2)}) async-start(bf16[8,128,128]{2,1,0:T(8,128)(2,1)} %get-tuple-element.42), calls=%async_computation.6 | async-start | bytes 524288 | tf_op jit(solution)/shard_map/all_to_all | solution.py:359
  121.6 0.7 copy.14
  122.3 10.4 %all-to-all-done.6 = bf16[8,128,128]{2,1,0:T(8,128)(2,1)S(1)} async-done(((bf16[8,128,128]{2,1,0:T(8,128)(2,1)}), bf16[8,128,128]{2,1,0:T(8,128)(2,1)S(1)}, u32[]{:S(2)}, u32[]{:S(2)}) %all-to-all-start.6) | async-done | bytes 262176 | tf_op jit(solution)/shard_map/all_to_all | solution.py:359
  132.7 0.7 reduce_sum.12
  (3 shorter events, 0.0 us)
Async XLA Ops:
  0.6 62.3 %copy-start.1 = (s32[64]{0:T(128)S(1)}, s32[64]{0:T(128)}, u32[]{:S(2)}) copy-start(s32[64]{0:T(128)} %param.12) | copy-start | bytes 772
  2.1 24.6 %all-to-all-start = ((bf16[8,128,128]{2,1,0:T(8,128)(2,1)}), bf16[8,128,128]{2,1,0:T(8,128)(2,1)S(1)}, u32[]{:S(2)}, u32[]{:S(2)}) async-start(bf16[8,128,128]{2,1,0:T(8,128)(2,1)} %broadcast_in_dim.6), calls=%async_computation | async-start | bytes 524288 | tf_op jit(solution)/shard_map/all_to_all | solution.py:359
  60.4 3.6 %collective-permute-start = (bf16[4,384,128]{2,1,0:T(8,128)(2,1)S(1)}, bf16[4,384,128]{2,1,0:T(8,128)(2,1)S(1)}, u32[]{:S(2)}, u32[]{:S(2)}) collective-permute-start(bf16[4,384,128]{2,1,0:T(8,128)(2,1)S(1)} %all_to_all.36.mine_ref), channel_id=1, source_target_pairs={{0,8},{8,0},{1,9},{9,1},{2,10},{10,2},{3,11},{11,3},{4,12},{12,4},... | collective-permute-start | bytes 1179656 | tf_op jit(solution)/shard_map/ppermute | solution.py:367
  78.2 39.0 %copy-start = (bf16[3,64,1024]{2,1,0:T(8,128)(2,1)S(1)}, bf16[3,64,1024]{2,1,0:T(8,128)(2,1)}, u32[]{:S(2)}) copy-start(bf16[3,64,1024]{2,1,0:T(8,128)(2,1)} %param.9) | copy-start | bytes 1179652
  83.9 3.5 %collective-permute-start.1 = (bf16[4,320,128]{2,1,0:T(8,128)(2,1)S(1)}, bf16[4,320,128]{2,1,0:T(8,128)(2,1)S(1)}, u32[]{:S(2)}, u32[]{:S(2)}) collective-permute-start(bf16[4,320,128]{2,1,0:T(8,128)(2,1)S(1)} %get-tuple-element.38), channel_id=1, source_target_pairs={{0,8},{8,0},{1,9},{9,1},{2,10},{10,2},{3,11},{11,3},{4,12},{12,4},... | collective-permute-start | bytes 983048 | tf_op jit(solution)/shard_map/ppermute | solution.py:367
  118.2 14.5 %all-to-all-start.6 = ((bf16[8,128,128]{2,1,0:T(8,128)(2,1)}), bf16[8,128,128]{2,1,0:T(8,128)(2,1)S(1)}, u32[]{:S(2)}, u32[]{:S(2)}) async-start(bf16[8,128,128]{2,1,0:T(8,128)(2,1)} %get-tuple-element.42), calls=%async_computation.6 | async-start | bytes 524288 | tf_op jit(solution)/shard_map/all_to_all | solution.py:359

commit v9 on v8

--- a/solution.py
+++ b/solution.py
@@ -136,6 +136,9 @@
             at = (v + SPAN) * B
             shifts[u, :, at : at + B] = jnp.where(v > place[0], edges[:, B:], edges[:, :B])
     put_band(place[1], place[0] + 2, 2 * G)
+    for u in range(G):
+        for v, apart in near_tiles(place, u):
+            put_band(u, v, apart)
     queries = near_ref[:, :, :E].reshape(N, E)
     grads = near_ref[:, :, E:].reshape(N, E)
     for at in range(0, N, 2 * B):
@@ -143,8 +146,6 @@
         slope_ref[:, at : at + 2 * B] = nt(grads, values[at : at + 2 * B])
     for u in range(G):
         rows = slice(u * B, (u + 1) * B)
-        for v, apart in near_tiles(place, u):
-            put_band(u, v, apart)
         pieces = []
         for v in range(G):
             at = (v + SPAN) * B
@@ -338,7 +339,7 @@
     total = jnp.sum(far_ref[...].astype(F32), axis=0)
     pairs = total[:B].astype(BF)
     table_ref[...] = jnp.concatenate([total[B:, :E], total[B:, E:]], axis=0)
-    terms = nn(query_ref[...], weights_ref[:E]) + nn(pairs, weights_ref[E:])
+    terms = nn(jnp.concatenate([query_ref[...], pairs], axis=1), weights_ref[...])
     for h in range(G):
         out_ref[h] = terms[:, h * B : (h + 1) * B].astype(BF)
 

time: 134 us -> 133 us (level)
  no operation moved by 1% of the time
where the time goes in v9:
time: 133 us; the launch traced here: 132 us
  blocking collectives  71.1 us (53%)
  waiting for transfers between devices  21.9 us (16%)
  starting transfers between devices  20 us (15%)
  Pallas kernels  12.1 us (9%)
  local copies, waits for them, and re-layouts  5.04 us (4%)
  between operations  1.38 us (1%)
    all_to_all x5, blocking collectives, exchange(): return lax.all_to_all(parts, axis, 0, 0, tiled=True)  71.1 us
    all_to_all x2, waiting for transfers between devices, exchange(): return lax.all_to_all(parts, axis, 0, 0, tiled=True)  19.4 us
    all_to_all x2, starting transfers between devices, exchange(): return lax.all_to_all(parts, axis, 0, 0, tiled=True)  16.2 us
    pallas_call x1, Pallas kernels, gradients(): pl.pallas_call(grads_kernel, in_specs=[SCALARS] + [ARRAY] * 7, out_specs=...  5.66 us
    pallas_call x1, Pallas kernels, statistics(): pl.pallas_call(stats_kernel, in_specs=[SCALARS] + [ARRAY] * 3, out_specs=...  4.9 us
    ppermute x2, starting transfers between devices, other_core(): return lax.ppermute(shard, 'core', [(0, 1), (1, 0)])  3.83 us
    unnamed x8, local copies, waits for them, and re-layouts  3.41 us
  transfers between devices with their start and end apart: 4, of which 4 were waited for; matrix products, arithmetic and copies ran while one was open for 3% of the time, Pallas kernels for 0%

profile of v9, /device:TPU:8, one launch (start us, length us, event | category | flops | bytes accessed | tf_op | source)
XLA Modules:
  0.0 132.5 jit_solution(9143656877552582571)
XLA Ops:
  0.6 0.0 copy-start.1
  0.6 1.5 %broadcast_in_dim.6 = bf16[8,128,128]{2,1,0:T(8,128)(2,1)} broadcast(bf16[128,128]{1,0:T(8,128)(2,1)} %param.8), dimensions={1,2} | broadcast | bytes 294912 | tf_op jit(solution)/shard_map/broadcast_in_dim | solution.py:364
  2.1 12.7 %all-to-all-start = ((bf16[8,128,128]{2,1,0:T(8,128)(2,1)}), bf16[8,128,128]{2,1,0:T(8,128)(2,1)S(1)}, u32[]{:S(2)}, u32[]{:S(2)}) async-start(bf16[8,128,128]{2,1,0:T(8,128)(2,1)} %broadcast_in_dim.6), calls=%async_computation | async-start | bytes 524288 | tf_op jit(solution)/shard_map/all_to_all | solution.py:360
  14.9 0.8 copy.12
  15.7 0.8 copy.13.grad_ref
  16.5 1.1 copy.15
  17.6 0.1 copy.17
  17.7 0.1 pad_maximum_fusion.chunk_ref
  17.8 9.0 %all-to-all-done.frames_ref = bf16[8,128,128]{2,1,0:T(8,128)(2,1)S(1)} async-done(((bf16[8,128,128]{2,1,0:T(8,128)(2,1)}), bf16[8,128,128]{2,1,0:T(8,128)(2,1)S(1)}, u32[]{:S(2)}, u32[]{:S(2)}) %all-to-all-start) | async-done | bytes 262176 | tf_op jit(solution)/shard_map/all_to_all | solution.py:360
  26.8 0.5 project.1
  27.2 17.0 %all_to_all.35.far_ref = bf16[8,160,128]{2,1,0:T(8,128)(2,1)S(1)} all-to-all(bf16[8,160,128]{2,1,0:T(8,128)(2,1)S(1)} %get-tuple-element.30), channel_id=1, replica_groups=mesh['far'=8,'pair'=4,'core'=2,'head'=8] {'far'}, dimensions={0} | all-to-all | bytes 655360 | tf_op jit(solution)/shard_map/all_to_all | solution.py:360
  44.2 0.1 broadcast_dynamic-update-slice_fusion
  44.3 16.1 %all_to_all.36.mine_ref = bf16[4,384,128]{2,1,0:T(8,128)(2,1)S(1)} all-to-all(bf16[4,384,128]{2,1,0:T(8,128)(2,1)S(1)} %broadcast_dynamic-update-slice_fusion), channel_id=1, replica_groups=mesh['far'=8,'pair'=4,'core'=2,'head'=8] {'pair'}, dimensions={0} | all-to-all | bytes 786432 | tf_op jit(solution)/shard_map/all_to_all | solution.py:360
  60.4 1.9 %collective-permute-start = (bf16[4,384,128]{2,1,0:T(8,128)(2,1)S(1)}, bf16[4,384,128]{2,1,0:T(8,128)(2,1)S(1)}, u32[]{:S(2)}, u32[]{:S(2)}) collective-permute-start(bf16[4,384,128]{2,1,0:T(8,128)(2,1)S(1)} %all_to_all.36.mine_ref), channel_id=1, source_target_pairs={{0,8},{8,0},{1,9},{9,1},{2,10},{10,2},{3,11},{11,3},{4,12},{12,4},... | collective-permute-start | bytes 1179656 | tf_op jit(solution)/shard_map/ppermute | solution.py:368
  63.0 0.0 copy-done.1
  63.0 0.1 pad_add_fusion.place
  63.0 0.9 collective-permute-done.theirs_ref
  64.0 4.9 %statistics.1 = (f32[1024,1024]{1,0:T(8,128)S(1)}, f32[1024,1024]{1,0:T(8,128)S(1)}, bf16[8,128,128]{2,1,0:T(8,128)(2,1)S(1)}, f32[16,128]{1,0:T(8,128)S(1)}, f3...) custom-call(s32[67]{0:T(128)S(1)} %pad_add_fusion.place, bf16[4,384,128]{2,1,0:T(8,128)(2,1)S(1)} %all_to_all.36.mine_ref, ...), custom_call_target="tpu_custom_call" | custom-call | tf_op jit(solution)/shard_map/statistics/pallas_call | solution.py:168
  68.9 8.4 %all_to_all.37.parts_ref = f32[8,16,128]{2,1,0:T(8,128)S(1)} all-to-all(f32[8,16,128]{2,1,0:T(8,128)S(1)} %broadcast_in_dim.8), channel_id=1, replica_groups=mesh['far'=8,'pair'=4,'core'=2,'head'=8] {'pair','core'}, dimensions={0} | all-to-all | bytes 131072 | tf_op jit(solution)/shard_map/all_to_all | solution.py:360
  77.4 0.0 copy-start
  77.4 5.7 %gradients.1 = (bf16[8,128,128]{2,1,0:T(8,128)(2,1)S(1)}, f32[4,320,128]{2,1,0:T(8,128)S(1)}, bf16[4,320,128]{2,1,0:T(8,128)(2,1)S(1)}) custom-call(s32[67]{0:T(128)S(1)} %pad_add_fusion.place, bf16[8,128,128]{2,1,0:T(8,128)(2,1)S(1)} %get-tuple-element.31.near_ref, bf16[8,160,128]{2,1,0:T(8,128)(2,1)S(1)} %all_to_all.35.far_ref, ...), custom_call_target="tpu_custom_call" | custom-call | tf_op jit(solution)/shard_map/gradients/pallas_call | solution.py:299
  83.0 1.9 %collective-permute-start.1 = (bf16[4,320,128]{2,1,0:T(8,128)(2,1)S(1)}, bf16[4,320,128]{2,1,0:T(8,128)(2,1)S(1)}, u32[]{:S(2)}, u32[]{:S(2)}) collective-permute-start(bf16[4,320,128]{2,1,0:T(8,128)(2,1)S(1)} %get-tuple-element.38), channel_id=1, source_target_pairs={{0,8},{8,0},{1,9},{9,1},{2,10},{10,2},{3,11},{11,3},{4,12},{12,4},... | collective-permute-start | bytes 983048 | tf_op jit(solution)/shard_map/ppermute | solution.py:368
  84.9 1.6 %collective-permute-done.1 = bf16[4,320,128]{2,1,0:T(8,128)(2,1)S(1)} collective-permute-done((bf16[4,320,128]{2,1,0:T(8,128)(2,1)S(1)}, bf16[4,320,128]{2,1,0:T(8,128)(2,1)S(1)}, u32[]{:S(2)}, u32[]{:S(2)}) %collective-permute-start.1) | collective-permute-done | bytes 327712 | tf_op jit(solution)/shard_map/ppermute | solution.py:368
  86.5 0.1 add_convert_fusion
  86.6 13.2 %all_to_all.38.near_ref = bf16[4,320,128]{2,1,0:T(8,128)(2,1)S(1)} all-to-all(bf16[4,320,128]{2,1,0:T(8,128)(2,1)S(1)} %add_convert_fusion), channel_id=1, replica_groups=mesh['far'=8,'pair'=4,'core'=2,'head'=8] {'pair'}, dimensions={0} | all-to-all | bytes 655360 | tf_op jit(solution)/shard_map/all_to_all | solution.py:360
  99.9 0.1 fold.1
  99.9 16.4 %all_to_all.39.far_ref = bf16[8,160,128]{2,1,0:T(8,128)(2,1)S(1)} all-to-all(bf16[8,160,128]{2,1,0:T(8,128)(2,1)S(1)} %get-tuple-element.40), channel_id=1, replica_groups=mesh['far'=8,'pair'=4,'core'=2,'head'=8] {'far'}, dimensions={0} | all-to-all | bytes 655360 | tf_op jit(solution)/shard_map/all_to_all | solution.py:360
  116.3 0.0 copy-done
  116.3 1.0 unproject.1
  117.3 3.4 %all-to-all-start.6 = ((bf16[8,128,128]{2,1,0:T(8,128)(2,1)}), bf16[8,128,128]{2,1,0:T(8,128)(2,1)S(1)}, u32[]{:S(2)}, u32[]{:S(2)}) async-start(bf16[8,128,128]{2,1,0:T(8,128)(2,1)} %get-tuple-element.42), calls=%async_computation.6 | async-start | bytes 524288 | tf_op jit(solution)/shard_map/all_to_all | solution.py:360
  120.7 0.7 copy.14
  121.4 10.4 %all-to-all-done.6 = bf16[8,128,128]{2,1,0:T(8,128)(2,1)S(1)} async-done(((bf16[8,128,128]{2,1,0:T(8,128)(2,1)}), bf16[8,128,128]{2,1,0:T(8,128)(2,1)S(1)}, u32[]{:S(2)}, u32[]{:S(2)}) %all-to-all-start.6) | async-done | bytes 262176 | tf_op jit(solution)/shard_map/all_to_all | solution.py:360
  131.8 0.7 reduce_sum.12
  (3 shorter events, 0.0 us)
Async XLA Ops:
  0.6 62.3 %copy-start.1 = (s32[64]{0:T(128)S(1)}, s32[64]{0:T(128)}, u32[]{:S(2)}) copy-start(s32[64]{0:T(128)} %param.12) | copy-start | bytes 772
  2.1 24.6 %all-to-all-start = ((bf16[8,128,128]{2,1,0:T(8,128)(2,1)}), bf16[8,128,128]{2,1,0:T(8,128)(2,1)S(1)}, u32[]{:S(2)}, u32[]{:S(2)}) async-start(bf16[8,128,128]{2,1,0:T(8,128)(2,1)} %broadcast_in_dim.6), calls=%async_computation | async-start | bytes 524288 | tf_op jit(solution)/shard_map/all_to_all | solution.py:360
  60.4 3.6 %collective-permute-start = (bf16[4,384,128]{2,1,0:T(8,128)(2,1)S(1)}, bf16[4,384,128]{2,1,0:T(8,128)(2,1)S(1)}, u32[]{:S(2)}, u32[]{:S(2)}) collective-permute-start(bf16[4,384,128]{2,1,0:T(8,128)(2,1)S(1)} %all_to_all.36.mine_ref), channel_id=1, source_target_pairs={{0,8},{8,0},{1,9},{9,1},{2,10},{10,2},{3,11},{11,3},{4,12},{12,4},... | collective-permute-start | bytes 1179656 | tf_op jit(solution)/shard_map/ppermute | solution.py:368
  77.4 39.0 %copy-start = (bf16[3,64,1024]{2,1,0:T(8,128)(2,1)S(1)}, bf16[3,64,1024]{2,1,0:T(8,128)(2,1)}, u32[]{:S(2)}) copy-start(bf16[3,64,1024]{2,1,0:T(8,128)(2,1)} %param.9) | copy-start | bytes 1179652
  83.0 3.5 %collective-permute-start.1 = (bf16[4,320,128]{2,1,0:T(8,128)(2,1)S(1)}, bf16[4,320,128]{2,1,0:T(8,128)(2,1)S(1)}, u32[]{:S(2)}, u32[]{:S(2)}) collective-permute-start(bf16[4,320,128]{2,1,0:T(8,128)(2,1)S(1)} %get-tuple-element.38), channel_id=1, source_target_pairs={{0,8},{8,0},{1,9},{9,1},{2,10},{10,2},{3,11},{11,3},{4,12},{12,4},... | collective-permute-start | bytes 983048 | tf_op jit(solution)/shard_map/ppermute | solution.py:368
  117.3 14.5 %all-to-all-start.6 = ((bf16[8,128,128]{2,1,0:T(8,128)(2,1)}), bf16[8,128,128]{2,1,0:T(8,128)(2,1)S(1)}, u32[]{:S(2)}, u32[]{:S(2)}) async-start(bf16[8,128,128]{2,1,0:T(8,128)(2,1)} %get-tuple-element.42), calls=%async_computation.6 | async-start | bytes 524288 | tf_op jit(solution)/shard_map/all_to_all | solution.py:360
